TPU v7x, 32 devices: a whole 2x2x4 slice. The times are simulated.
32 devices in a mesh: samp: 16 (over z, y, x), blk: 2 (over core).
Axes of the slice: x: 2, y: 2, z: 4, core: 2. Of those that a mesh axis runs over, the one named last changes fastest.
Arguments:
- tokens: bfloat16 [96, 800, 384], P('samp', 'blk')
- view_count: int32 [96], P('samp'), may hold values from 1 to 4, as said below
- norm1_gain: bfloat16 [384], replicated, may hold values from 0.5 to 1.5
- norm1_bias: bfloat16 [384], replicated, may hold values from -0.59765625 to 0.59765625
- w_qkv: bfloat16 [384, 1152], replicated, may hold values from -0.3125 to 0.3125
- qv_bias: bfloat16 [768], replicated, may hold values from -1.1953125 to 1.1953125
- w_out: bfloat16 [384, 384], replicated, may hold values from -3.5 to 3.5
- out_bias: bfloat16 [384], replicated, may hold values from -0.59765625 to 0.59765625
- norm2_gain: bfloat16 [384], replicated, may hold values from 0.5 to 1.5
- norm2_bias: bfloat16 [384], replicated, may hold values from -0.59765625 to 0.59765625
- w_fc1: bfloat16 [384, 1536], replicated, may hold values from -0.3125 to 0.3125
- fc1_bias: bfloat16 [1536], replicated, may hold values from -1.796875 to 1.796875
- w_fc2: bfloat16 [1536, 384], replicated, may hold values from -0.15625 to 0.15625
- fc2_bias: bfloat16 [384], replicated, may hold values from -0.59765625 to 0.59765625
- cot_tokens: bfloat16 [96, 800, 384], P('samp', 'blk'), may hold values from -6 to 6
- cot_cls: bfloat16 [96, 384], P(('samp', 'blk'))
Outputs:
- tokens_out: bfloat16 [96, 800, 384], P('samp', 'blk')
- cls_norm: bfloat16 [96, 384], P(('samp', 'blk'))
- grad_tokens: bfloat16 [96, 800, 384], P('samp', 'blk')
- grad_norm1_gain: float32 [384], replicated
- grad_norm1_bias: float32 [384], replicated
- grad_w_qkv: float32 [384, 1152], replicated
- grad_qv_bias: float32 [768], replicated
- grad_w_out: float32 [384, 384], replicated
- grad_out_bias: float32 [384], replicated
- grad_norm2_gain: float32 [384], replicated
- grad_norm2_bias: float32 [384], replicated
- grad_w_fc1: float32 [384, 1536], replicated
- grad_fc1_bias: float32 [1536], replicated
- grad_w_fc2: float32 [1536, 384], replicated
- grad_fc2_bias: float32 [384], replicated
Inputs may be any that keep to these rules, and one draw needn't show every extreme that they name: `view_count`: each index of samp holds 6 samples in a row, and one of them has 4 views.
All inputs are finite; a program needn't handle non-finite values.
Results may differ from a plain program's by a relative error of at most 0.0096.
Values may be sent and summed in bfloat16 or wider, within the bound.
No kernel may reach another device: no remote copies, remote signals or barrier semaphores. Data moves between devices by JAX's collectives and lax.ppermute only.
A program may use at most 320 MiB of HBM per device.

v0:
```python
import functools
import math

import jax
import jax.numpy as jnp
import numpy as np
from jax import lax
from jax.experimental import pallas as pl
from jax.experimental.pallas import tpu as pltpu
from jax.sharding import PartitionSpec as P

HEAD_DIM = 64
VIEW_ROWS = 196
NORM_EPS = 1e-06
CLS_EPS = 1e-05
MASKED = -1e30
LOG2E = math.log2(math.e)
LN2 = math.log(2.0)
SCALE = HEAD_DIM ** (-0.5)
SUM_LOW = 1e-15
SUM_HIGH = 1e15
BF = jnp.bfloat16
F32 = jnp.float32
VMEM_BYTES = 60 * 2**20


def dot(a, b, ca, cb):
    return lax.dot_general(a, b, (((ca,), (cb,)), ((), ())), preferred_element_type=F32)


def norm_parts(values):
    centre = jnp.mean(values, -1, keepdims=True)
    offset = values - centre
    rstd = lax.rsqrt(jnp.mean(offset * offset, -1, keepdims=True) + NORM_EPS)
    return offset * rstd, rstd


def gelu_cdf(values):
    return 0.5 + 0.5 * lax.erf(values * (0.5**0.5))


def params(semantics):
    return pltpu.CompilerParams(dimension_semantics=semantics, vmem_limit_bytes=VMEM_BYTES)


def whole(shape):
    return pl.BlockSpec(shape, lambda *_: (0,) * len(shape))


def key_counts(rows):
    views = (rows - 1) // VIEW_ROWS
    return [(v, min(rows, -(-(1 + VIEW_ROWS * v) // 16) * 16)) for v in range(1, views + 1)]


GAIN1, SHIFT1, GAIN2, SHIFT2, OUT_BIAS, FC2_BIAS, QV_BIAS, FC1_BIAS = 0, 1, 2, 3, 4, 5, 6, 8


def row_of(pack_ref, index):
    return pack_ref[index : index + 1, :]


def place_halves(target_ref, core, own, far):
    half = own.shape[0]
    target_ref[pl.ds(pl.multiple_of(core * half, 16), half), :] = own
    target_ref[pl.ds(pl.multiple_of((1 - core) * half, 16), half), :] = far


def split_halves(source_ref, core, own_ref, far_ref):
    half = own_ref.shape[1]
    own_ref[0] = source_ref[pl.ds(pl.multiple_of(core * half, 16), half), :]
    far_ref[0] = source_ref[pl.ds(pl.multiple_of((1 - core) * half, 16), half), :]


def project_kernel(
    blk_ref, views_ref, own_ref, far_ref, w_ref, pack_ref, w_out_ref, w1_ref, w2_ref, cot_ref,
    x_ref, hat_ref, rstd_ref, qkv_ref, cls_ref, stat_ref, mix_ref, first_ref, full_ref,
):
    step = pl.program_id(0)
    rows = x_ref.shape[1]
    width = own_ref.shape[2]
    place_halves(full_ref, blk_ref[0], own_ref[0], far_ref[0])
    x_ref[0] = full_ref[...]
    values = full_ref[...].astype(F32)
    hat, rstd = norm_parts(values)
    hat_ref[0] = hat.astype(BF)
    rstd_ref[0] = rstd
    normed = (hat * row_of(pack_ref, GAIN1) + row_of(pack_ref, SHIFT1)).astype(BF)
    columns = pack_ref[0:8, :].T
    for third in range(3):
        part = pl.ds(third * width, width)
        piece = dot(w_ref[part, :], normed, 1, 1)
        if third == 0:
            piece = (piece + columns[:, QV_BIAS : QV_BIAS + 1]) * (SCALE * LOG2E)
        if third == 2:
            piece = piece + columns[:, QV_BIAS + 1 : QV_BIAS + 2]
        qkv_ref[0, part, :] = piece.astype(BF)

    lead = qkv_ref[0, pl.ds(0, width), :128].astype(F32).T[0:1, :]
    head_of = lax.broadcasted_iota(jnp.int32, (8, width), 1) // HEAD_DIM
    pick = head_of == lax.broadcasted_iota(jnp.int32, (8, width), 0)
    queries = jnp.where(pick, lead, 0.0).astype(BF)
    scores = dot(queries, qkv_ref[0, pl.ds(width, width), :], 1, 0)
    limit = 1 + VIEW_ROWS * views_ref[blk_ref[CORE] * pl.num_programs(0) + step]
    place = lax.broadcasted_iota(jnp.int32, (8, rows), 1)
    scores = jnp.where(place < limit, scores, MASKED)
    powers = jnp.exp2(scores - jnp.max(scores, -1, keepdims=True))
    chances = (powers / jnp.sum(powers, -1, keepdims=True)).astype(BF)
    mixed = dot(chances, qkv_ref[0, pl.ds(2 * width, width), :], 1, 1)
    mix_ref[pl.ds(step, 1), :] = jnp.sum(jnp.where(pick, mixed, 0.0), 0, keepdims=True)
    first_ref[pl.ds(step, 1), :] = values[0:1, :]

    @pl.when(step == pl.num_programs(0) - 1)
    def _():
        branch = dot(mix_ref[...].astype(BF), w_out_ref[...], 1, 0) + row_of(pack_ref, OUT_BIAS)
        middle = first_ref[...] + branch
        normed2 = norm_parts(middle)[0] * row_of(pack_ref, GAIN2) + row_of(pack_ref, SHIFT2)
        normed2 = normed2.astype(BF)
        output = middle + row_of(pack_ref, FC2_BIAS)
        for j in range(w1_ref.shape[1] // width):
            cols = slice(j * width, (j + 1) * width)
            pre = dot(normed2, w1_ref[:, cols], 1, 0) + row_of(pack_ref, FC1_BIAS + j)
            act = (pre * gelu_cdf(pre)).astype(BF)
            output = output + dot(act, w2_ref[cols, :], 1, 0)
        cls_ref[...] = output
        count = cot_ref.shape[0]
        cls = output[:count]
        cot = cot_ref[...].astype(F32)
        stat_ref[...] = jnp.zeros_like(stat_ref)
        for k, term in enumerate((cls, cls * cls, cot, cot * cls)):
            stat_ref[k : k + 1, :] = jnp.sum(term, 0, keepdims=True)


def attention_kernel(core_ref, views_ref, q_ref, k_ref, v_ref, pow_ref, sum_ref, att_ref):
    sample = pl.program_id(0)
    pair = pl.program_id(1)
    rows = q_ref.shape[2]
    views = views_ref[core_ref[CORE] * pl.num_programs(0) + sample]
    limit = 1 + VIEW_ROWS * views
    ones = jnp.ones((16, rows), BF)

    def heads():
        for h in range(2):
            yield h, pl.ds(h * HEAD_DIM, HEAD_DIM)

    def store(h, mixed):
        total = mixed[HEAD_DIM : HEAD_DIM + 1]
        sum_ref[0, pl.ds(2 * pair + h, 1), :] = total
        att_ref[0, h * HEAD_DIM : (h + 1) * HEAD_DIM, :] = (mixed[:HEAD_DIM] / total).astype(BF)

    for count, keys in key_counts(rows):

        @pl.when(views == count)
        def _(keys=keys):
            main = keys - 16
            for h, lanes in heads():
                scores = dot(k_ref[0, lanes, :keys], q_ref[0, lanes, :], 0, 0)
                pow_ref[0, h, :main, :] = jnp.exp2(scores[:main]).astype(BF)
                place = main + lax.broadcasted_iota(jnp.int32, (16, rows), 0)
                tail = jnp.where(place < limit, scores[main:], MASKED)
                pow_ref[0, h, main:keys, :] = jnp.exp2(tail).astype(BF)
                left = jnp.concatenate((v_ref[0, lanes, :keys], ones[:, :keys]), 0)
                store(h, dot(left, pow_ref[0, h, :keys, :], 1, 0))

    first = sum_ref[0, pl.ds(2 * pair, 1), :]
    second = sum_ref[0, pl.ds(2 * pair + 1, 1), :]
    least = jnp.min(jnp.minimum(first, second))
    plain = (least > SUM_LOW) & (jnp.max(jnp.maximum(first, second)) < SUM_HIGH)

    @pl.when(jnp.logical_not(plain))
    def _():
        for h, lanes in heads():
            scores = dot(k_ref[0, lanes, :], q_ref[0, lanes, :], 0, 0)
            place = lax.broadcasted_iota(jnp.int32, (rows, rows), 0)
            scores = jnp.where(place < limit, scores, MASKED)
            pow_ref[0, h] = jnp.exp2(scores - jnp.max(scores, 0, keepdims=True)).astype(BF)
            left = jnp.concatenate((v_ref[0, lanes, :], ones), 0)
            store(h, dot(left, pow_ref[0, h], 1, 0))


def mlp_kernel(
    blk_ref, x_ref, att_ref, w_out_ref, w1_ref, w2_ref, pack_ref,
    hat_ref, rstd_ref, act_ref, slope_ref, own_ref, far_ref, out_ref,
):
    half = own_ref.shape[1]
    width = own_ref.shape[2]
    branch = dot(att_ref[0], w_out_ref[...], 0, 0) + row_of(pack_ref, OUT_BIAS)
    middle = x_ref[0].astype(F32) + branch
    hat, rstd = norm_parts(middle)
    hat_ref[0] = hat.astype(BF)
    rstd_ref[0] = rstd
    normed = (hat * row_of(pack_ref, GAIN2) + row_of(pack_ref, SHIFT2)).astype(BF)
    for r in range(2):
        part = slice(r * half, (r + 1) * half)
        for j in range(w1_ref.shape[1] // width):
            cols = slice(j * width, (j + 1) * width)
            pre = dot(normed[part], w1_ref[:, cols], 1, 0) + row_of(pack_ref, FC1_BIAS + j)
            cdf = gelu_cdf(pre)
            bell = jnp.exp(pre * pre * -0.5) * (1.0 / math.sqrt(2.0 * math.pi))
            act_ref[0, part, cols] = (pre * cdf).astype(BF)
            slope_ref[0, part, cols] = (cdf + pre * bell).astype(BF)
        output = middle[part] + dot(act_ref[0, part, :], w2_ref[...], 1, 0)
        out_ref[part, :] = (output + row_of(pack_ref, FC2_BIAS)).astype(BF)
    split_halves(out_ref, blk_ref[0], own_ref, far_ref)


def mlp_grads_kernel(
    core_ref, own_ref, far_ref, cls_ref, cot_ref, *refs, samples, parts, peers
):
    stat_refs = refs[:peers]
    act_ref, slope_ref, hat_ref, w2_ref = refs[peers : peers + 4]
    dpre_ref, dcls_ref, norm_ref, bias_ref, kept_ref, sent_ref = refs[peers + 4 : peers + 10]
    g_ref, acc2_ref, acc1_ref, flat_ref = refs[peers + 10 :]
    step = pl.program_id(0)
    width = own_ref.shape[2]
    hidden = w2_ref.shape[0]

    @pl.when(step == 0)
    def _():
        acc2_ref[...] = jnp.zeros_like(acc2_ref)
        acc1_ref[...] = jnp.zeros_like(acc1_ref)
        bias_ref[...] = jnp.zeros_like(bias_ref)
        stats = stat_refs[0][...]
        for other in stat_refs[1:]:
            stats = stats + other[...]
        local = cot_ref.shape[0]
        cls = cls_ref[...][:local]
        cot = cot_ref[...].astype(F32)
        mean = stats[0:1] / samples
        scale = lax.rsqrt(stats[1:2] / samples - mean * mean + CLS_EPS)
        hat = (cls - mean) * scale
        norm_ref[...] = hat.astype(BF)
        cross = scale * (stats[3:4] - mean * stats[2:3])
        dcls_ref[...] = jnp.zeros_like(dcls_ref)
        dcls_ref[:local, :] = scale * (cot - stats[2:3] / samples - hat * (cross / samples))

    place_halves(g_ref, core_ref[0], own_ref[0].astype(F32), far_ref[0].astype(F32))
    g_ref[0:1, :] = g_ref[0:1, :] + dcls_ref[pl.ds(step, 1), :]
    g_mlp = g_ref[...].astype(BF)
    hat = hat_ref[0]
    blocks = hidden // width
    for j in range(blocks):
        cols = slice(j * width, (j + 1) * width)
        d_act = dot(g_mlp, w2_ref[cols, :], 1, 1)
        d_pre = (d_act * slope_ref[0, :, cols].astype(F32)).astype(BF)
        dpre_ref[0, :, cols] = d_pre
        bias_ref[j : j + 1, :] += jnp.sum(d_pre.astype(F32), 0, keepdims=True)
        acc1_ref[:, cols] += dot(hat, d_pre, 0, 0)
        acc2_ref[cols, :] += dot(act_ref[0, :, cols], g_mlp, 0, 0)
    bias_ref[blocks : blocks + 1, :] += jnp.sum(g_mlp.astype(F32), 0, keepdims=True)

    @pl.when(step == pl.num_programs(0) - 1)
    def _():
        flat_ref[:hidden, :] = acc2_ref[...].astype(BF)
        for j in range(blocks):
            rows = slice(hidden + j * width, hidden + (j + 1) * width)
            flat_ref[rows, :] = acc1_ref[:, j * width : (j + 1) * width].astype(BF)
        clear_rest(flat_ref, 2 * hidden)
        write_halves(core_ref[0], flat_ref, parts, kept_ref, sent_ref)


def mlp_back_kernel(
    blk_ref, own_ref, far_ref, dcls_ref, dpre_ref, hat_ref, rstd_ref, att_ref, sum_ref,
    bias_in_ref, pack_ref, w1_ref, w_out_ref,
    gmid_ref, dmix_ref, inner_ref, out_grad_ref, bias_ref, g_ref,
):
    step = pl.program_id(0)
    width = own_ref.shape[2]
    blocks = w1_ref.shape[1] // width

    @pl.when(step == 0)
    def _():
        out_grad_ref[...] = jnp.zeros_like(out_grad_ref)
        bias_ref[...] = bias_in_ref[...]

    place_halves(g_ref, blk_ref[0], own_ref[0].astype(F32), far_ref[0].astype(F32))
    g_ref[0:1, :] = g_ref[0:1, :] + dcls_ref[pl.ds(step, 1), :]
    d_norm = dot(dpre_ref[0], w1_ref[...], 1, 1)
    u = d_norm * row_of(pack_ref, GAIN2)
    hat = hat_ref[0].astype(F32)
    g_mid = g_ref[...] + rstd_ref[0] * (
        u - jnp.mean(u, -1, keepdims=True) - hat * jnp.mean(u * hat, -1, keepdims=True)
    )
    g_attn = g_mid.astype(BF)
    gmid_ref[0] = g_attn
    out_grad_ref[...] += dot(att_ref[0], g_attn, 1, 0)
    bias_ref[blocks + 1 : blocks + 2, :] += jnp.sum(g_attn.astype(F32), 0, keepdims=True)
    d_mix = dot(w_out_ref[...], g_attn, 1, 1)
    for h in range(width // HEAD_DIM):
        part = slice(h * HEAD_DIM, (h + 1) * HEAD_DIM)
        piece = d_mix[part] / sum_ref[0, h : h + 1, :]
        dmix_ref[0, part, :] = piece.astype(BF)
        inner_ref[0, h : h + 1, :] = jnp.sum(piece * att_ref[0, part, :].astype(F32), 0, keepdims=True)


def attention_back_kernel(
    core_ref, views_ref, q_ref, k_ref, v_ref, pow_ref, dmix_ref, inner_ref, hat_ref,
    dqkv_ref, grad_ref, sums_ref, *, pair
):
    sample = pl.program_id(0)
    rows = hat_ref.shape[1]
    views = views_ref[core_ref[CORE] * pl.num_programs(0) + sample]
    for count, keys in key_counts(rows):

        @pl.when(views == count)
        def _(keys=keys):
            for h in range(2):
                lanes = slice(h * HEAD_DIM, (h + 1) * HEAD_DIM)
                d_mix = dmix_ref[0, lanes, :]
                powers = pow_ref[0, h, :keys, :]
                d_weights = dot(v_ref[0, lanes, :keys], d_mix, 0, 0)
                inner = inner_ref[0, 2 * pair + h : 2 * pair + h + 1, :]
                d_scores = (powers.astype(F32) * (d_weights - inner)).astype(BF)
                d_query = dot(k_ref[0, lanes, :keys], d_scores, 1, 0) * SCALE
                d_key = dot(q_ref[0, lanes, :], d_scores, 1, 1) * LN2
                d_value = dot(d_mix, powers, 1, 1)
                base = h * HEAD_DIM
                dqkv_ref[0, base : base + HEAD_DIM, :] = d_query.astype(BF)
                dqkv_ref[0, 128 + base : 128 + base + HEAD_DIM, :keys] = d_key.astype(BF)
                dqkv_ref[0, 256 + base : 256 + base + HEAD_DIM, :keys] = d_value.astype(BF)
                if keys < rows:
                    blank = jnp.zeros((HEAD_DIM, rows - keys), BF)
                    dqkv_ref[0, 128 + base : 128 + base + HEAD_DIM, keys:] = blank
                    dqkv_ref[0, 256 + base : 256 + base + HEAD_DIM, keys:] = blank

    @pl.when(sample == 0)
    def _():
        grad_ref[...] = jnp.zeros_like(grad_ref)
        sums_ref[...] = jnp.zeros_like(sums_ref)

    d_part = dqkv_ref[0]
    grad_ref[...] += dot(d_part, hat_ref[0], 1, 0)
    sums_ref[...] += dot(jnp.ones((16, rows), BF), d_part, 1, 1)[:8]


def tokens_back_kernel(core_ref, *refs, pairs):
    dqkv_refs = refs[:pairs]
    w_ref, pack_ref, hat_ref, rstd_ref, gmid_ref, own_ref, far_ref, out_ref = refs[pairs:]
    width = own_ref.shape[2]
    d_norm = None
    for pair in range(pairs):
        w = jnp.concatenate(
            [w_ref[t * width + pair * 128 : t * width + (pair + 1) * 128, :] for t in range(3)], 0
        )
        piece = dot(dqkv_refs[pair][0], w, 0, 0)
        d_norm = piece if d_norm is None else d_norm + piece
    w = d_norm * row_of(pack_ref, GAIN1)
    hat = hat_ref[0].astype(F32)
    back = rstd_ref[0] * (
        w - jnp.mean(w, -1, keepdims=True) - hat * jnp.mean(w * hat, -1, keepdims=True)
    )
    out_ref[...] = (gmid_ref[0].astype(F32) + back).astype(BF)
    split_halves(out_ref, core_ref[0], own_ref, far_ref)


def clear_rest(ref, used):
    if ref.shape[0] > used:
        ref[used:, :] = jnp.zeros((ref.shape[0] - used, ref.shape[1]), ref.dtype)


def write_halves(core, flat_ref, parts, kept_ref, sent_ref):
    start = at = 0
    for size in parts:
        half = size // 2
        mine = pl.multiple_of(start + core * half, 16)
        other = pl.multiple_of(start + (1 - core) * half, 16)
        kept_ref[at : at + half, :] = flat_ref[pl.ds(mine, half), :]
        sent_ref[at : at + half, :] = flat_ref[pl.ds(other, half), :]
        start += size
        at += half


def pack_kernel(core_ref, *refs, pairs, parts):
    grad_refs = refs[:pairs]
    sums_refs = refs[pairs : 2 * pairs]
    out_grad_ref, bias_ref, kept_ref, sent_ref, flat_ref = refs[2 * pairs :]
    width = out_grad_ref.shape[0]
    for pair in range(pairs):
        flat_ref[pair * width : (pair + 1) * width, :] = grad_refs[pair][...].astype(BF)
    at = pairs * width
    flat_ref[at : at + width, :] = out_grad_ref[...].astype(BF)
    at += width
    clear_rest(flat_ref, at)
    vectors = [bias_ref[0:8, :]]
    rows = lax.broadcasted_iota(jnp.int32, (8, width), 0)
    extra = jnp.zeros((8, width), F32)
    for pair in range(pairs):
        extra = jnp.where(rows == pair, sums_refs[pair][0:1, :], extra)
    vectors.append(extra)
    flat_ref[at : at + 16, :] = jnp.concatenate(vectors, 0).astype(BF)
    write_halves(core_ref[0], flat_ref, parts, kept_ref, sent_ref)


def swap_cores(value):
    return lax.ppermute(value, "blk", [(0, 1), (1, 0)])


def stages(count, first=4):
    out = []
    stride = 1
    while stride < count:
        left = count // stride
        radix = first if not out and left % first == 0 else 4 if left % 4 == 0 else 2
        out.append((stride, radix))
        stride *= radix
    return out


def shifted(value, stage, steps, axis="samp"):
    stride, radix = stage
    count = lax.axis_size(axis)
    pairs = []
    for source in range(count):
        digit = (source // stride) % radix
        pairs.append((source, source + ((digit + steps) % radix - digit) * stride))
    return lax.ppermute(value, axis, pairs)


def small_call(kernel, args, outs, scratch=(), ties=(), name=None):
    def body(*refs):
        kernel(*refs[: len(args)], *refs[len(args) + len(ties) :])

    vmem = pl.BlockSpec(memory_space=pltpu.VMEM)
    size = lambda a: math.prod(a.shape) * jnp.dtype(a.dtype).itemsize
    total = sum(size(a) for a in (*args[1:], *outs)) + sum(
        math.prod(a.shape) * jnp.dtype(a.dtype).itemsize for a in scratch
    )
    return pl.pallas_call(
        body,
        in_specs=[
            pl.BlockSpec(memory_space=pltpu.SMEM),
            *[vmem] * (len(args) - 1),
            *[pl.BlockSpec(memory_space=pl.ANY)] * len(ties),
        ],
        out_specs=[vmem] * len(outs),
        out_shape=outs,
        scratch_shapes=list(scratch),
        compiler_params=pltpu.CompilerParams(vmem_limit_bytes=2 * total + 4 * 2**20),
        name=name,
    )(*args, *ties)


def spread_kernel(info_ref, *refs, groups):
    inputs = sum(count for count, *_ in groups)
    outputs = sum(radix for _, _, radix, _ in groups)
    at, out_at = 0, inputs
    for g, (count, rows, radix, slot) in enumerate(groups):
        part = slice(rows[0], rows[1])
        total = refs[at][part, :].astype(F32)
        for k in range(1, count):
            total = total + refs[at + k][part, :].astype(F32)
        if radix == 1:
            refs[out_at][...] = total.astype(BF)
        else:
            total_ref = refs[inputs + outputs + g]
            total_ref[...] = total.astype(BF)
            size = total_ref.shape[0] // radix
            for k in range(radix):
                start = lax.rem(info_ref[slot] + k, radix) * size
                refs[out_at + k][...] = total_ref[pl.ds(pl.multiple_of(start, 16), size), :]
        at += count
        out_at += radix


def collect_kernel(info_ref, *refs, groups):
    at, out_at = 0, sum(groups)
    for count in groups:
        size = refs[at].shape[0]
        for k in range(count):
            refs[out_at][k * size : (k + 1) * size, :] = refs[at + k][...]
        at += count
        out_at += 1


CORE = 0


class Layout:
    def __init__(self, count, chains):
        self.base = stages(count)
        self.count = count
        self.columns = {"core": 0}
        table = np.zeros((2 * count, 1 + len(self.base)), np.int32)
        for device in range(2 * count):
            samp = device // 2
            table[device, 0] = device % 2
            for i, (stride, radix) in enumerate(self.base):
                table[device, 1 + i] = (samp // stride) % radix
        tables = [table]
        self.place_at = []
        width = table.shape[1]
        for parts in chains:
            rows = np.stack([self.places(device, parts) for device in range(2 * count)])
            self.place_at.append(width)
            width += rows.shape[1]
            tables.append(rows)
        self.table = np.concatenate(tables, 1).astype(np.int32)

    def orders(self, parts):
        n = len(self.base)
        return [[(i + k) % n for k in range(n)] for i in range(len(parts))]

    def places(self, device, parts):
        core, samp = device % 2, device // 2
        out = []
        start = 0
        for size, order in zip(parts, self.orders(parts)):
            half = size // 2
            offsets = np.array([start + core * half, start + (1 - core) * half])
            unit = half
            for index in order:
                stride, radix = self.base[index]
                unit //= radix
                digit = ((samp // stride) % radix - np.arange(radix)) % radix
                offsets = (offsets[:, None] + (digit * unit)[None, :]).reshape(-1)
            out.append(offsets)
            start += size
        return np.concatenate(out)


class Chain:
    def __init__(self, layout, index, parts, info):
        self.layout = layout
        self.place = layout.place_at[index]
        self.parts = parts
        self.info = info
        self.orders = layout.orders(parts)
        self.rounds = len(layout.base)

    def start(self, kept, sent):
        self.pending = [[kept, swap_cores(sent)]]
        return kept

    def scatter(self, level, ties=()):
        groups, args = [], [self.info]
        at = 0
        last = level == self.rounds
        for part, order in enumerate(self.orders):
            arrays = self.pending[0] if level == 0 else self.pending[part]
            size = self.parts[part] // 2 if level == 0 else arrays[0].shape[0]
            rows = (at, at + size)
            if level == 0:
                at += size
            radix = 1 if last else self.layout.base[order[level]][1]
            slot = 0 if last else 1 + order[level]
            groups.append((len(arrays), rows, radix, slot))
            args += arrays
        width = args[1].shape[1]
        outs = []
        for _, rows, radix, _ in groups:
            outs += [jax.ShapeDtypeStruct(((rows[1] - rows[0]) // radix, width), BF)] * radix
        scratch = [pltpu.VMEM((rows[1] - rows[0], width), BF) for _, rows, _, _ in groups]
        result = small_call(
            functools.partial(spread_kernel, groups=tuple(groups)), args, outs, scratch, ties, "spread"
        )
        pieces = []
        at = 0
        for _, _, radix, _ in groups:
            pieces.append(list(result[at : at + radix]))
            at += radix
        if last:
            self.values = [group[0] for group in pieces]
            return self.gather(level - 1)
        self.pending = [
            [group[0]]
            + [shifted(group[k], self.layout.base[order[level]], k) for k in range(1, len(group))]
            for group, order in zip(pieces, self.orders)
        ]
        return pieces[0][0]

    def gather(self, level):
        self.pending = []
        for value, order in zip(self.values, self.orders):
            stage = self.layout.base[order[level]]
            self.pending.append([value] + [shifted(value, stage, k) for k in range(1, stage[1])])
        return self.values[0]

    def collect(self, level, ties=()):
        groups = tuple(len(group) for group in self.pending)
        args = [self.info] + [piece for group in self.pending for piece in group]
        outs = [
            jax.ShapeDtypeStruct((len(group) * group[0].shape[0], group[0].shape[1]), BF)
            for group in self.pending
        ]
        self.values = small_call(
            functools.partial(collect_kernel, groups=groups), args, outs, (), ties, "collect"
        )
        if level > 0:
            return self.gather(level - 1)
        self.pending = [[value, swap_cores(value)] for value in self.values]
        return self.values[0]

    def arrived(self):
        return [side for group in self.pending for side in group]

    def units(self):
        return [size // 2 // self.layout.count for size in self.parts]


def restore(info_ref, flat_ref, refs, units, chunks, at):
    for part, unit in enumerate(units):
        for side in range(2):
            ref = refs[2 * part + side]

            def body(i, carry, ref=ref, unit=unit, at=at):
                start = pl.multiple_of(info_ref[at + i], 16)
                source = pl.multiple_of(i * unit, 16)
                flat_ref[pl.ds(start, unit), :] = ref[pl.ds(source, unit), :]
                return carry

            lax.fori_loop(0, chunks, body, 0)
            at += chunks


def finish_mlp_kernel(info_ref, *refs, units, chunks, at):
    ins = 2 * len(units)
    g_refs = refs[:ins]
    fc2_ref, turned_ref, flat_ref = refs[ins:]
    restore(info_ref, flat_ref, g_refs, units, chunks, at)
    hidden, width = fc2_ref.shape
    fc2_ref[...] = flat_ref[:hidden, :].astype(F32)
    for j in range(hidden // width):
        rows = slice(hidden + j * width, hidden + (j + 1) * width)
        turned_ref[:, j * width : (j + 1) * width] = flat_ref[rows, :].astype(F32)


def finish_kernel(info_ref, *refs, units, chunks, at, pairs):
    ins = 2 * len(units)
    g_refs = refs[:ins]
    pack_ref, w_qkv_ref, w1_ref, turned_ref = refs[ins : ins + 4]
    w_qkv_grad_ref, w_out_grad_ref, fc1_grad_ref, vector_ref, flat_ref = refs[ins + 4 :]
    restore(info_ref, flat_ref, g_refs, units, chunks, at)
    width = w_out_grad_ref.shape[0]
    hidden = fc1_grad_ref.shape[1]
    blocks = hidden // width
    at = pairs * width
    w_out_grad_ref[...] = flat_ref[at : at + width, :].astype(F32)
    vectors = flat_ref[at + width : at + width + 16, :].astype(F32)
    columns = pack_ref[0:8, :].T
    gain = jnp.zeros((width, 1), F32)
    shift = jnp.zeros((width, 1), F32)
    for pair in range(pairs):
        hats = flat_ref[pair * width : (pair + 1) * width, :].astype(F32).T
        sums = vectors[8 + pair : 9 + pair]
        result = hats * columns[:, GAIN1 : GAIN1 + 1] + columns[:, SHIFT1 : SHIFT1 + 1] * sums
        for t in range(3):
            cols = slice(t * width + pair * 128, t * width + (pair + 1) * 128)
            own = slice(t * 128, (t + 1) * 128)
            w_qkv_grad_ref[:, cols] = result[:, own]
            w = w_qkv_ref[:, cols].astype(F32)
            gain = gain + jnp.sum(w * hats[:, own], -1, keepdims=True)
            shift = shift + jnp.sum(w * sums[:, own], -1, keepdims=True)
    gain2 = jnp.zeros((width, 1), F32)
    shift2 = jnp.zeros((width, 1), F32)
    for j in range(blocks):
        cols = slice(j * width, (j + 1) * width)
        hats = turned_ref[:, cols]
        sums = vectors[j : j + 1]
        fc1_grad_ref[:, cols] = hats * columns[:, GAIN2 : GAIN2 + 1] + columns[:, SHIFT2 : SHIFT2 + 1] * sums
        w = w1_ref[:, cols].astype(F32)
        gain2 = gain2 + jnp.sum(w * hats, -1, keepdims=True)
        shift2 = shift2 + jnp.sum(w * sums, -1, keepdims=True)
    vector_ref[0:16, :] = vectors
    lane = lax.broadcasted_iota(jnp.int32, (width, 128), 1)
    wide = jnp.where(lane == 0, gain, jnp.where(lane == 1, shift, jnp.where(lane == 2, gain2, shift2)))
    vector_ref[16:24, :] = wide.T[0:8]


def pad_rows(count, unit):
    return -(-count // unit) * unit


def per_device(
    tokens, view_count, norm1_gain, norm1_bias, w_qkv, qv_bias, w_out, out_bias,
    norm2_gain, norm2_bias, w_fc1, fc1_bias, w_fc2, fc2_bias, cot_tokens, cot_cls,
):
    core = lax.axis_index("blk")
    cores = lax.axis_size("blk")
    count = lax.axis_size("samp")
    samples, half, width = tokens.shape
    local = samples // cores
    rows = half * cores
    hidden = w_fc1.shape[1]
    blocks = hidden // width
    heads = width // HEAD_DIM
    pairs = heads // 2
    sds = jax.ShapeDtypeStruct

    unit = 32 * count

    def split_rows(used):
        total = pad_rows(used, unit)
        second = pad_rows(total // 3, unit)
        return [max(total - second, unit), second]

    parts1 = split_rows(2 * hidden)
    parts2 = split_rows(pairs * 384 + width + 16)
    layout = Layout(count, (parts1, parts2))
    device = lax.axis_index("samp") * cores + core
    info = lax.dynamic_index_in_dim(jnp.asarray(layout.table), device, 0, keepdims=False)

    theirs = (1 - core) * local
    far_tokens = swap_cores(lax.dynamic_slice_in_dim(tokens, theirs, local, 0))
    far_cot = swap_cores(lax.dynamic_slice_in_dim(cot_tokens, theirs, local, 0))

    w_turned = w_qkv.T
    pack = jnp.concatenate(
        (
            norm1_gain, norm1_bias, norm2_gain, norm2_bias, out_bias, fc2_bias, qv_bias, fc1_bias,
            jnp.zeros(((8 - blocks) * width,), BF),
        )
    ).astype(F32).reshape(16, width)

    vmem = pl.BlockSpec(memory_space=pltpu.VMEM)
    half_spec = lambda f: pl.BlockSpec((1, half, width), f)
    own_map = lambda s, b, *_: (b[CORE] * local + s, 0, 0)
    by_sample = lambda s, *_: (s, 0, 0)
    rows_spec = pl.BlockSpec((1, rows, width), by_sample)
    turned_spec = pl.BlockSpec((1, width, rows), by_sample)
    rstd_spec = pl.BlockSpec((1, rows, 1), by_sample)
    hidden_spec = pl.BlockSpec((1, rows, hidden), by_sample)
    eight_spec = pl.BlockSpec((1, 8, rows), by_sample)

    def big_call(kernel, prefetch, args, in_specs, outs, out_specs, scratch=(), ties=(), grid=(local,), name=None):
        n = len(prefetch) + len(args)

        def body(*refs):
            kernel(*refs[:n], *refs[n + len(ties) :])

        return pl.pallas_call(
            body,
            grid_spec=pltpu.PrefetchScalarGridSpec(
                num_scalar_prefetch=len(prefetch),
                grid=grid,
                in_specs=[*in_specs, *[pl.BlockSpec(memory_space=pl.ANY)] * len(ties)],
                out_specs=out_specs,
                scratch_shapes=list(scratch),
            ),
            out_shape=outs,
            compiler_params=params(("arbitrary",) * len(grid)),
            name=name,
        )(*prefetch, *args, *ties)

    x_full, hat1, rstd1, qkv, cls_rows, stats = big_call(
        project_kernel,
        (info, view_count),
        (tokens, far_tokens, w_turned, pack, w_out, w_fc1, w_fc2, cot_cls),
        [half_spec(own_map), half_spec(by_sample), *[vmem] * 6],
        [
            sds((local, rows, width), BF),
            sds((local, rows, width), BF),
            sds((local, rows, 1), F32),
            sds((local, 3 * width, rows), BF),
            sds((8, width), F32),
            sds((8, width), F32),
        ],
        [
            rows_spec, rows_spec, rstd_spec,
            pl.BlockSpec((1, 3 * width, rows), by_sample), vmem, vmem,
        ],
        [pltpu.VMEM((8, width), F32), pltpu.VMEM((8, width), F32), pltpu.VMEM((rows, width), BF)],
        name="project",
    )

    both = ("samp", "blk")
    first, *later = stages(count * cores, 8)
    stat_parts = [stats] + [shifted(stats, first, k, both) for k in range(1, first[1])]

    qkv_specs = lambda p: [
        pl.BlockSpec((1, 128, rows), lambda s, *a, t=t: (s, t * pairs + p(*a), 0)) for t in range(3)
    ]
    powers, totals, mixed = big_call(
        attention_kernel,
        (info, view_count),
        (qkv, qkv, qkv),
        qkv_specs(lambda p, *_: p),
        [
            sds((local, heads, rows, rows), BF),
            sds((local, 8, rows), F32),
            sds((local, width, rows), BF),
        ],
        [
            pl.BlockSpec((1, 2, rows, rows), lambda s, p, *_: (s, p, 0, 0)),
            pl.BlockSpec((1, 8, rows), lambda s, p, *_: (s, 0, 0)),
            pl.BlockSpec((1, 128, rows), lambda s, p, *_: (s, p, 0)),
        ],
        grid=(local, pairs),
        name="attention",
    )

    def add_kernel(info_ref, *refs):
        total = refs[0][...]
        for ref in refs[1:-1]:
            total = total + ref[...]
        refs[-1][...] = total

    tie = totals
    for stage in later:
        stats = small_call(
            add_kernel, [info, *stat_parts], [sds((8, width), F32)], (), (tie,), "add"
        )[0]
        stat_parts = [stats] + [shifted(stats, stage, k, both) for k in range(1, stage[1])]
        tie = stats

    hat2, rstd2, act, slope, out_own, out_far = big_call(
        mlp_kernel,
        (info,),
        (x_full, mixed, w_out, w_fc1, w_fc2, pack),
        [rows_spec, turned_spec, vmem, vmem, vmem, vmem],
        [
            sds((local, rows, width), BF),
            sds((local, rows, 1), F32),
            sds((local, rows, hidden), BF),
            sds((local, rows, hidden), BF),
            sds((samples, half, width), BF),
            sds((local, half, width), BF),
        ],
        [rows_spec, rstd_spec, hidden_spec, hidden_spec, half_spec(own_map), half_spec(by_sample)],
        [pltpu.VMEM((rows, width), BF)],
        (tie,),
        name="mlp",
    )
    out_came = swap_cores(out_far)

    d_pre, d_cls, cls_norm, biases, kept1, sent1 = big_call(
        functools.partial(
            mlp_grads_kernel, samples=local * cores * count, parts=parts1, peers=len(stat_parts)
        ),
        (info,),
        (cot_tokens, far_cot, cls_rows, cot_cls, *stat_parts, act, slope, hat2, w_fc2),
        [
            half_spec(own_map), half_spec(by_sample), vmem, vmem, *[vmem] * len(stat_parts),
            hidden_spec, hidden_spec, rows_spec, vmem,
        ],
        [
            sds((local, rows, hidden), BF),
            sds((8, width), F32),
            sds((local, width), BF),
            sds((8, width), F32),
            sds((sum(parts1) // 2, width), BF),
            sds((sum(parts1) // 2, width), BF),
        ],
        [hidden_spec, vmem, vmem, vmem, vmem, vmem],
        [
            pltpu.VMEM((rows, width), F32),
            pltpu.VMEM((hidden, width), F32),
            pltpu.VMEM((width, hidden), F32),
            pltpu.VMEM((sum(parts1), width), BF),
        ],
        name="mlp_grads",
    )
    chain1 = Chain(layout, 0, parts1, info)
    tie = chain1.start(kept1, sent1)

    g_mid, d_mix, inner, out_grad, biases = big_call(
        mlp_back_kernel,
        (info,),
        (cot_tokens, far_cot, d_cls, d_pre, hat2, rstd2, mixed, totals, biases, pack, w_fc1, w_out),
        [
            half_spec(own_map), half_spec(by_sample), vmem, hidden_spec, rows_spec, rstd_spec,
            turned_spec, eight_spec, vmem, vmem, vmem, vmem,
        ],
        [
            sds((local, rows, width), BF),
            sds((local, width, rows), BF),
            sds((local, 8, rows), F32),
            sds((width, width), F32),
            sds((8, width), F32),
        ],
        [rows_spec, turned_spec, eight_spec, vmem, vmem],
        [pltpu.VMEM((rows, width), F32)],
        name="mlp_back",
    )

    steps = [functools.partial(chain1.scatter, level) for level in range(chain1.rounds + 1)]
    steps += [functools.partial(chain1.collect, level) for level in reversed(range(chain1.rounds))]
    done = inner
    d_parts, grads, sums = [], [], []
    for pair in range(pairs):
        tie = steps.pop(0)(ties=(done,))
        d_part, grad, total = big_call(
            functools.partial(attention_back_kernel, pair=pair),
            (info, view_count),
            (qkv, qkv, qkv, powers, d_mix, inner, hat1),
            [
                *qkv_specs(lambda *_, p=pair: p),
                pl.BlockSpec((1, 2, rows, rows), lambda s, *_, p=pair: (s, p, 0, 0)),
                pl.BlockSpec((1, 128, rows), lambda s, *_, p=pair: (s, p, 0)),
                eight_spec,
                rows_spec,
            ],
            [
                sds((local, 384, rows), BF),
                sds((384, width), F32),
                sds((8, 384), F32),
            ],
            [pl.BlockSpec((1, 384, rows), by_sample), vmem, vmem],
            (),
            (tie,),
            name="attention_back",
        )
        d_parts.append(d_part)
        grads.append(grad)
        sums.append(total)
        done = total

    tie = steps.pop(0)(ties=(done,))
    chain2 = Chain(layout, 1, parts2, info)
    kept2, sent2 = small_call(
        functools.partial(pack_kernel, pairs=pairs, parts=parts2),
        (info, *grads, *sums, out_grad, biases),
        [sds((sum(parts2) // 2, width), BF)] * 2,
        [pltpu.VMEM((sum(parts2), width), BF)],
        (tie,),
        name="pack",
    )
    tie2 = chain2.start(kept2, sent2)
    steps2 = [functools.partial(chain2.scatter, level) for level in range(chain2.rounds + 1)]
    steps2 += [functools.partial(chain2.collect, level) for level in reversed(range(chain2.rounds))]

    grad_own, grad_far = big_call(
        functools.partial(tokens_back_kernel, pairs=pairs),
        (info,),
        (*d_parts, w_turned, pack, hat1, rstd1, g_mid),
        [
            *[pl.BlockSpec((1, 384, rows), by_sample)] * pairs,
            vmem, vmem, rows_spec, rstd_spec, rows_spec,
        ],
        [sds((samples, half, width), BF), sds((local, half, width), BF)],
        [half_spec(own_map), half_spec(by_sample)],
        [pltpu.VMEM((rows, width), BF)],
        (tie, tie2),
        name="tokens_back",
    )
    grad_came = swap_cores(grad_far)
    done = grad_far
    while steps or steps2:
        ties = (done,)
        if steps2:
            steps2.pop(0)(ties=ties)
        if steps:
            steps.pop(0)(ties=ties)
        done = info

    def finish(kernel, chain, args, outs, **options):
        return small_call(
            functools.partial(
                kernel, units=chain.units(), chunks=count, at=chain.place, **options
            ),
            (info, *chain.arrived(), *args),
            [sds(shape, F32) for shape in outs],
            [pltpu.VMEM((sum(chain.parts), width), BF)],
            name="finish",
        )

    grad_w_fc2, turned = finish(finish_mlp_kernel, chain1, (), ((hidden, width), (width, hidden)))
    grad_w_qkv, grad_w_out, grad_w_fc1, vectors = finish(
        finish_kernel, chain2, (pack, w_qkv, w_fc1, turned),
        ((width, 3 * width), (width, width), (width, hidden), (24, width)), pairs=pairs,
    )
    column_sums = vectors[8 : 8 + pairs].reshape(pairs, 3, 128)
    grad_qv_bias = jnp.concatenate((column_sums[:, 0].reshape(-1), column_sums[:, 2].reshape(-1)))
    tokens_out = lax.dynamic_update_slice_in_dim(out_own, out_came, theirs, 0)
    grad_tokens = lax.dynamic_update_slice_in_dim(grad_own, grad_came, theirs, 0)
    return (
        tokens_out, cls_norm, grad_tokens, vectors[16], vectors[17], grad_w_qkv, grad_qv_bias,
        grad_w_out, vectors[blocks + 1], vectors[18], vectors[19], grad_w_fc1,
        vectors[:blocks].reshape(hidden), grad_w_fc2, vectors[blocks],
    )


def solution(mesh):
    split = P("samp", "blk", None)
    classes = P(("samp", "blk"), None)
    return jax.shard_map(
        per_device,
        mesh=mesh,
        in_specs=(split, P("samp"), *([P()] * 12), split, classes),
        out_specs=(split, classes, split, *([P()] * 12)),
        check_vma=False,
    )
```

profile of v0, /device:TPU:0, one launch (start us, length us, event | category | flops | bytes accessed | tf_op | source)
XLA Modules:
  0.0 292.6 jit_solution(15114145372413067202)
XLA Ops:
  11.0 13.7 %project.1 = (bf16[3,800,384]{2,1,0:T(8,128)(2,1)}, bf16[3,800,384]{2,1,0:T(8,128)(2,1)}, f32[3,800,1]{2,1,0:T(8,128)}, bf16[3,1152,800]{2,1,0:T(8,128)(2,1)}, f32[8,384]{1,0:T(8,128)}, /*index=5*/f32[8,384]{1,0:T(8,128)}) custom-call(s32[131]{0:T(256)} %bitcast.4, s32[6]{0:T(128)} %refs_1_.13, bf16[6,400,384]{2,1,0:T(8,128)(2,1)} %refs_2_.1, ...), custom_call_target="tpu_custom_call" | custom-call | tf_op jit(solution)/shard_map/project/pallas_call | solution.py:729
  24.7 3.6 %collective-permute-start.7 = (f32[8,384]{1,0:T(8,128)}, f32[8,384]{1,0:T(8,128)S(1)}, u32[]{:S(2)}, u32[]{:S(2)}) collective-permute-start(f32[8,384]{1,0:T(8,128)} %get-tuple-element.107.refs_1_), channel_id=1, source_target_pairs={{0,7},{1,0},{2,1},{3,2},{4,3},{5,4},{6,5},{7,6},{8,15},{9,8},{10,9... | collective-permute-start | bytes 36872 | tf_op jit(solution)/shard_map/ppermute | solution.py:415
  33.7 17.6 %attention.1 = (bf16[3,6,800,800]{3,2,1,0:T(8,128)(2,1)}, f32[3,8,800]{2,1,0:T(8,128)}, bf16[3,384,800]{2,1,0:T(8,128)(2,1)}) custom-call(s32[131]{0:T(256)} %bitcast.5, s32[6]{0:T(128)} %refs_1_.13, bf16[3,1152,800]{2,1,0:T(8,128)(2,1)} %get-tuple-element.105.refs_2_.refs_3_.refs_4_, bf16[3,1152,800]{2,1,0:T(8,128)(2,1)} %get-tuple-element.105.refs_2_.refs_3_.refs_4_, ...), custom_call_target="tpu_custom_call" | custom-call | tf_op jit(solution)/shard_map/attention/pallas_call | solution.py:729
  52.8 4.4 %collective-permute-start.12 = (f32[8,384]{1,0:T(8,128)S(1)}, f32[8,384]{1,0:T(8,128)S(1)}, u32[]{:S(2)}, u32[]{:S(2)}) collective-permute-start(f32[8,384]{1,0:T(8,128)S(1)} %add.25.refs_7_.refs_5_), channel_id=1, source_target_pairs={{0,24},{1,25},{2,26},{3,27},{4,28},{5,29},{6,30},{7,31},{8,0},{9,1... | collective-permute-start | bytes 36872 | tf_op jit(solution)/shard_map/ppermute | solution.py:415
  59.1 19.5 %mlp.1 = (bf16[3,800,384]{2,1,0:T(8,128)(2,1)}, f32[3,800,1]{2,1,0:T(8,128)}, bf16[3,800,1536]{2,1,0:T(8,128)(2,1)}, bf16[3,800,1536]{2,1,0:T(8,128)(2,1)}, bf16...) custom-call(s32[131]{0:T(256)} %bitcast.6, bf16[3,800,384]{2,1,0:T(8,128)(2,1)} %get-tuple-element.104.refs_1_, ...), custom_call_target="tpu_custom_call" | custom-call | tf_op jit(solution)/shard_map/mlp/pallas_call | solution.py:729
  79.6 23.3 %mlp_grads.1 = (bf16[3,800,1536]{2,1,0:T(8,128)(2,1)}, f32[8,384]{1,0:T(8,128)}, bf16[3,384]{1,0:T(4,128)(2,1)}, f32[8,384]{1,0:T(8,128)}, bf16[1536,384]{1,0:T(8,128)(2,1)}, /*index=5*/bf16[1536,384]{1,0:T(8,128)(2,1)}) custom-call(s32[131]{0:T(256)} %bitcast.7, bf16[6,400,384]{2,1,0:T(8,128)(2,1)} %refs_1_.10, bf16[3,400,384]{2,1,0:T(8,128)(2,1)} %copy-done.34, ...), custom_call_target="tpu_custom_call" | custom-call | tf_op jit(solution)/shard_map/mlp_grads/pallas_call | solution.py:729
  103.0 13.4 %mlp_back.1 = (bf16[3,800,384]{2,1,0:T(8,128)(2,1)}, bf16[3,384,800]{2,1,0:T(8,128)(2,1)}, f32[3,8,800]{2,1,0:T(8,128)}, f32[384,384]{1,0:T(8,128)}, f32[8,384]{1,0:T(8,128)}) custom-call(s32[131]{0:T(256)} %bitcast.8, bf16[6,400,384]{2,1,0:T(8,128)(2,1)} %refs_1_.10, bf16[3,400,384]{2,1,0:T(8,128)(2,1)} %copy-done.34, f32[8,384]{1,0:T(8,128)} %get-tuple-element.117.refs_3_, ...), custom_call_target="tpu_custom_call" | custom-call | tf_op jit(solution)/shard_map/mlp_back/pallas_call | solution.py:729
  128.3 11.6 %attention_back.3 = (bf16[3,384,800]{2,1,0:T(8,128)(2,1)}, f32[384,384]{1,0:T(8,128)}, f32[8,384]{1,0:T(8,128)}) custom-call(s32[131]{0:T(256)} %bitcast.9, s32[6]{0:T(128)} %refs_1_.13, bf16[3,1152,800]{2,1,0:T(8,128)(2,1)} %get-tuple-element.105.refs_2_.refs_3_.refs_4_, bf16[3,1152,800]{2,1,0:T(8,128)(2,1)} %get-tuple-element.105.refs_2_.refs_3_.refs_4_, ...), custom_call_target="tpu_custom_call" | custom-call | tf_op jit(solution)/shard_map/attention_back/pallas_call | solution.py:729
  146.0 2.9 collective-permute-start.22
  149.1 2.9 collective-permute-start.25
  152.0 11.9 %attention_back.4 = (bf16[3,384,800]{2,1,0:T(8,128)(2,1)}, f32[384,384]{1,0:T(8,128)}, f32[8,384]{1,0:T(8,128)}) custom-call(s32[131]{0:T(256)} %bitcast.10, s32[6]{0:T(128)} %refs_1_.13, bf16[3,1152,800]{2,1,0:T(8,128)(2,1)} %get-tuple-element.105.refs_2_.refs_3_.refs_4_, bf16[3,1152,800]{2,1,0:T(8,128)(2,1)} %get-tuple-element.105.refs_2_.refs_3_.refs_4_, ...), custom_call_target="tpu_custom_call" | custom-call | tf_op jit(solution)/shard_map/attention_back/pallas_call | solution.py:729
  172.8 11.6 %attention_back.5 = (bf16[3,384,800]{2,1,0:T(8,128)(2,1)}, f32[384,384]{1,0:T(8,128)}, f32[8,384]{1,0:T(8,128)}) custom-call(s32[131]{0:T(256)} %bitcast.11, s32[6]{0:T(128)} %refs_1_.13, bf16[3,1152,800]{2,1,0:T(8,128)(2,1)} %get-tuple-element.105.refs_2_.refs_3_.refs_4_, bf16[3,1152,800]{2,1,0:T(8,128)(2,1)} %get-tuple-element.105.refs_2_.refs_3_.refs_4_, ...), custom_call_target="tpu_custom_call" | custom-call | tf_op jit(solution)/shard_map/attention_back/pallas_call | solution.py:729
  191.6 4.9 %collective-permute-start.65 = (bf16[128,384]{1,0:T(8,128)(2,1)S(1)}, bf16[128,384]{1,0:T(8,128)(2,1)S(1)}, u32[]{:S(2)}, u32[]{:S(2)}) collective-permute-start(bf16[128,384]{1,0:T(8,128)(2,1)S(1)} %get-tuple-element.184.refs_5_), channel_id=1, source_target_pairs={{0,24},{2,26},{4,28},{6,30},{8,0},{10,2},{12,4},{14,6},{16,8},{18,... | collective-permute-start | bytes 294920 | tf_op jit(solution)/shard_map/ppermute | solution.py:415
  199.1 10.2 %tokens_back.1 = (bf16[6,400,384]{2,1,0:T(8,128)(2,1)}, bf16[3,400,384]{2,1,0:T(8,128)(2,1)}) custom-call(s32[131]{0:T(256)} %bitcast.12, bf16[3,384,800]{2,1,0:T(8,128)(2,1)} %get-tuple-element.127.refs_1_, bf16[3,384,800]{2,1,0:T(8,128)(2,1)} %get-tuple-element.137.refs_2_, bf16[3,384,800]{2,1,0:T(8,128)(2,1)} %get-tuple-element.147.refs_3_, ...), custom_call_target="tpu_custom_call" | custom-call | tf_op jit(solution)/shard_map/tokens_back/pallas_call | solution.py:729
  210.4 2.9 collective-permute-start.36
  225.7 2.9 %collective-permute-done.62.refs_4_ = bf16[256,384]{1,0:T(8,128)(2,1)S(1)} collective-permute-done((bf16[256,384]{1,0:T(8,128)(2,1)S(1)}, bf16[256,384]{1,0:T(8,128)(2,1)S(1)}, u32[]{:S(2)}, u32[]{:S(2)}) %collective-permute-start.62) | collective-permute-done | bytes 196640 | tf_op jit(solution)/shard_map/ppermute | solution.py:415
  228.7 3.7 %collective-permute-done.61.refs_3_ = bf16[256,384]{1,0:T(8,128)(2,1)S(1)} collective-permute-done((bf16[256,384]{1,0:T(8,128)(2,1)S(1)}, bf16[256,384]{1,0:T(8,128)(2,1)S(1)}, u32[]{:S(2)}, u32[]{:S(2)}) %collective-permute-start.61) | collective-permute-done | bytes 196640 | tf_op jit(solution)/shard_map/ppermute | solution.py:415
  232.6 3.6 %collective-permute-start.42 = (bf16[32,384]{1,0:T(8,128)(2,1)S(1)}, bf16[32,384]{1,0:T(8,128)(2,1)S(1)}, u32[]{:S(2)}, u32[]{:S(2)}) collective-permute-start(bf16[32,384]{1,0:T(8,128)(2,1)S(1)} %get-tuple-element.173), channel_id=1, source_target_pairs={{0,24},{2,26},{4,28},{6,30},{8,0},{10,2},{12,4},{14,6},{16,8},{18,... | collective-permute-start | bytes 73736 | tf_op jit(solution)/shard_map/ppermute | solution.py:415
  243.1 4.0 %collective-permute-start.48 = (bf16[32,384]{1,0:T(8,128)(2,1)S(1)}, bf16[32,384]{1,0:T(8,128)(2,1)S(1)}, u32[]{:S(2)}, u32[]{:S(2)}) collective-permute-start(bf16[32,384]{1,0:T(8,128)(2,1)S(1)} %get-tuple-element.178.refs_1_), channel_id=1, source_target_pairs={{0,24},{2,26},{4,28},{6,30},{8,0},{10,2},{12,4},{14,6},{16,8},{18,... | collective-permute-start | bytes 73736 | tf_op jit(solution)/shard_map/ppermute | solution.py:415
  248.9 3.0 %collective-permute-done.47.refs_3_ = bf16[32,384]{1,0:T(8,128)(2,1)S(1)} collective-permute-done((bf16[32,384]{1,0:T(8,128)(2,1)S(1)}, bf16[32,384]{1,0:T(8,128)(2,1)S(1)}, u32[]{:S(2)}, u32[]{:S(2)}) %collective-permute-start.47) | collective-permute-done | bytes 24608 | tf_op jit(solution)/shard_map/ppermute | solution.py:415
  268.8 2.7 collective-permute-done.52.refs_2_
  273.7 3.3 %collective-permute-done.56.refs_7_ = bf16[128,384]{1,0:T(8,128)(2,1)S(1)} collective-permute-done((bf16[128,384]{1,0:T(8,128)(2,1)S(1)}, bf16[128,384]{1,0:T(8,128)(2,1)S(1)}, u32[]{:S(2)}, u32[]{:S(2)}) %collective-permute-start.56) | collective-permute-done | bytes 98336 | tf_op jit(solution)/shard_map/ppermute | solution.py:415
  282.2 2.8 finish.2
  285.0 5.5 %finish.3 = (f32[384,1152]{1,0:T(8,128)}, f32[384,384]{1,0:T(8,128)}, f32[384,1536]{1,0:T(8,128)}, f32[24,384]{1,0:T(8,128)S(1)}) custom-call(s32[131]{0:T(256)S(1)} %bitcast.30, bf16[512,384]{1,0:T(8,128)(2,1)S(1)} %get-tuple-element.182.refs_1_, bf16[512,384]{1,0:T(8,128)(2,1)S(1)} %collective-permute-done.58.refs_2_, ...), custom_call_target="tpu_custom_call" | custom-call | tf_op jit(solution)/shard_map/finish/pallas_call | solution.py:427
  (260 shorter events, 104.9 us)
Async XLA Ops:
  5.7 72.9 %collective-permute-start.9 = (bf16[3,400,384]{2,1,0:T(8,128)(2,1)}, bf16[3,400,384]{2,1,0:T(8,128)(2,1)S(1)}, u32[]{:S(2)}, u32[]{:S(2)}) collective-permute-start(bf16[3,400,384]{2,1,0:T(8,128)(2,1)} %constant_dynamic-slice_fusion), channel_id=1, source_target_pairs={{0,1},{1,0},{2,3},{3,2},{4,5},{5,4},{6,7},{7,6},{8,9},{9,8},{10,11... | collective-permute-start | bytes 2764808 | tf_op jit(solution)/shard_map/ppermute | solution.py:394
  29.0 22.4 %collective-permute-start.4 = (f32[8,384]{1,0:T(8,128)}, f32[8,384]{1,0:T(8,128)S(1)}, u32[]{:S(2)}, u32[]{:S(2)}) collective-permute-start(f32[8,384]{1,0:T(8,128)} %get-tuple-element.107.refs_1_), channel_id=1, source_target_pairs={{0,4},{1,5},{2,6},{3,7},{4,0},{5,1},{6,2},{7,3},{8,12},{9,13},{10,... | collective-permute-start | bytes 36872 | tf_op jit(solution)/shard_map/ppermute | solution.py:415
  30.5 20.8 %collective-permute-start.3 = (f32[8,384]{1,0:T(8,128)}, f32[8,384]{1,0:T(8,128)S(1)}, u32[]{:S(2)}, u32[]{:S(2)}) collective-permute-start(f32[8,384]{1,0:T(8,128)} %get-tuple-element.107.refs_1_), channel_id=1, source_target_pairs={{0,3},{1,4},{2,5},{3,6},{4,7},{5,0},{6,1},{7,2},{8,11},{9,12},{10,... | collective-permute-start | bytes 36872 | tf_op jit(solution)/shard_map/ppermute | solution.py:415
  32.3 19.1 %collective-permute-start.2 = (f32[8,384]{1,0:T(8,128)}, f32[8,384]{1,0:T(8,128)S(1)}, u32[]{:S(2)}, u32[]{:S(2)}) collective-permute-start(f32[8,384]{1,0:T(8,128)} %get-tuple-element.107.refs_1_), channel_id=1, source_target_pairs={{0,2},{1,3},{2,4},{3,5},{4,6},{5,7},{6,0},{7,1},{8,10},{9,11},{10,... | collective-permute-start | bytes 36872 | tf_op jit(solution)/shard_map/ppermute | solution.py:415
  33.2 18.2 %collective-permute-start.1 = (f32[8,384]{1,0:T(8,128)}, f32[8,384]{1,0:T(8,128)S(1)}, u32[]{:S(2)}, u32[]{:S(2)}) collective-permute-start(f32[8,384]{1,0:T(8,128)} %get-tuple-element.107.refs_1_), channel_id=1, source_target_pairs={{0,1},{1,2},{2,3},{3,4},{4,5},{5,6},{6,7},{7,0},{8,9},{9,10},{10,1... | collective-permute-start | bytes 36872 | tf_op jit(solution)/shard_map/ppermute | solution.py:415
  52.8 25.8 %collective-permute-start.12 = (f32[8,384]{1,0:T(8,128)S(1)}, f32[8,384]{1,0:T(8,128)S(1)}, u32[]{:S(2)}, u32[]{:S(2)}) collective-permute-start(f32[8,384]{1,0:T(8,128)S(1)} %add.25.refs_7_.refs_5_), channel_id=1, source_target_pairs={{0,24},{1,25},{2,26},{3,27},{4,28},{5,29},{6,30},{7,31},{8,0},{9,1... | collective-permute-start | bytes 36872 | tf_op jit(solution)/shard_map/ppermute | solution.py:415
  57.2 21.4 %collective-permute-start.11 = (f32[8,384]{1,0:T(8,128)S(1)}, f32[8,384]{1,0:T(8,128)S(1)}, u32[]{:S(2)}, u32[]{:S(2)}) collective-permute-start(f32[8,384]{1,0:T(8,128)S(1)} %add.25.refs_7_.refs_5_), channel_id=1, source_target_pairs={{0,16},{1,17},{2,18},{3,19},{4,20},{5,21},{6,22},{7,23},{8,24},{9,... | collective-permute-start | bytes 36872 | tf_op jit(solution)/shard_map/ppermute | solution.py:415
  57.2 21.5 %collective-permute-start.10 = (f32[8,384]{1,0:T(8,128)S(1)}, f32[8,384]{1,0:T(8,128)S(1)}, u32[]{:S(2)}, u32[]{:S(2)}) collective-permute-start(f32[8,384]{1,0:T(8,128)S(1)} %add.25.refs_7_.refs_5_), channel_id=1, source_target_pairs={{0,8},{1,9},{2,10},{3,11},{4,12},{5,13},{6,14},{7,15},{8,16},{9,17... | collective-permute-start | bytes 36872 | tf_op jit(solution)/shard_map/ppermute | solution.py:415
  121.5 18.4 %collective-permute-start.14 = (bf16[256,384]{1,0:T(8,128)(2,1)S(1)}, bf16[256,384]{1,0:T(8,128)(2,1)S(1)}, u32[]{:S(2)}, u32[]{:S(2)}) collective-permute-start(bf16[256,384]{1,0:T(8,128)(2,1)S(1)} %get-tuple-element.128), channel_id=1, source_target_pairs={{0,2},{2,4},{4,6},{6,0},{8,10},{10,12},{12,14},{14,8},{16,18},{18,... | collective-permute-start | bytes 589832 | tf_op jit(solution)/shard_map/ppermute | solution.py:415
  122.2 17.7 %collective-permute-start.15 = (bf16[256,384]{1,0:T(8,128)(2,1)S(1)}, bf16[256,384]{1,0:T(8,128)(2,1)S(1)}, u32[]{:S(2)}, u32[]{:S(2)}) collective-permute-start(bf16[256,384]{1,0:T(8,128)(2,1)S(1)} %get-tuple-element.129), channel_id=1, source_target_pairs={{0,4},{2,6},{4,0},{6,2},{8,12},{10,14},{12,8},{14,10},{16,20},{18,... | collective-permute-start | bytes 589832 | tf_op jit(solution)/shard_map/ppermute | solution.py:415
  123.8 16.1 %collective-permute-start.16 = (bf16[256,384]{1,0:T(8,128)(2,1)S(1)}, bf16[256,384]{1,0:T(8,128)(2,1)S(1)}, u32[]{:S(2)}, u32[]{:S(2)}) collective-permute-start(bf16[256,384]{1,0:T(8,128)(2,1)S(1)} %get-tuple-element.130), channel_id=1, source_target_pairs={{0,6},{2,0},{4,2},{6,4},{8,14},{10,8},{12,10},{14,12},{16,22},{18,... | collective-permute-start | bytes 589832 | tf_op jit(solution)/shard_map/ppermute | solution.py:415
  143.9 20.1 %collective-permute-start.20 = (bf16[64,384]{1,0:T(8,128)(2,1)S(1)}, bf16[64,384]{1,0:T(8,128)(2,1)S(1)}, u32[]{:S(2)}, u32[]{:S(2)}) collective-permute-start(bf16[64,384]{1,0:T(8,128)(2,1)S(1)} %get-tuple-element.138), channel_id=1, source_target_pairs={{0,8},{2,10},{4,12},{6,14},{8,16},{10,18},{12,20},{14,22},{16,24},... | collective-permute-start | bytes 147464 | tf_op jit(solution)/shard_map/ppermute | solution.py:415
  143.9 20.1 %collective-permute-start.21 = (bf16[64,384]{1,0:T(8,128)(2,1)S(1)}, bf16[64,384]{1,0:T(8,128)(2,1)S(1)}, u32[]{:S(2)}, u32[]{:S(2)}) collective-permute-start(bf16[64,384]{1,0:T(8,128)(2,1)S(1)} %get-tuple-element.139), channel_id=1, source_target_pairs={{0,16},{2,18},{4,20},{6,22},{8,24},{10,26},{12,28},{14,30},{16,0},... | collective-permute-start | bytes 147464 | tf_op jit(solution)/shard_map/ppermute | solution.py:415
  146.0 18.0 %collective-permute-start.22 = (bf16[64,384]{1,0:T(8,128)(2,1)S(1)}, bf16[64,384]{1,0:T(8,128)(2,1)S(1)}, u32[]{:S(2)}, u32[]{:S(2)}) collective-permute-start(bf16[64,384]{1,0:T(8,128)(2,1)S(1)} %get-tuple-element.140), channel_id=1, source_target_pairs={{0,24},{2,26},{4,28},{6,30},{8,0},{10,2},{12,4},{14,6},{16,8},{18,... | collective-permute-start | bytes 147464 | tf_op jit(solution)/shard_map/ppermute | solution.py:415
  148.9 15.0 %collective-permute-start.24 = (bf16[32,384]{1,0:T(8,128)(2,1)S(1)}, bf16[32,384]{1,0:T(8,128)(2,1)S(1)}, u32[]{:S(2)}, u32[]{:S(2)}) collective-permute-start(bf16[32,384]{1,0:T(8,128)(2,1)S(1)} %get-tuple-element.143), channel_id=1, source_target_pairs={{0,4},{2,6},{4,0},{6,2},{8,12},{10,14},{12,8},{14,10},{16,20},{18,... | collective-permute-start | bytes 73736 | tf_op jit(solution)/shard_map/ppermute | solution.py:415
  165.5 19.0 %collective-permute-start.28 = (bf16[64,384]{1,0:T(8,128)(2,1)S(1)}, bf16[64,384]{1,0:T(8,128)(2,1)S(1)}, u32[]{:S(2)}, u32[]{:S(2)}) collective-permute-start(bf16[64,384]{1,0:T(8,128)(2,1)S(1)} %get-tuple-element.146.refs_9_.refs_1_), channel_id=1, source_target_pairs={{0,24},{2,26},{4,28},{6,30},{8,0},{10,2},{12,4},{14,6},{16,8},{18,... | collective-permute-start | bytes 147464 | tf_op jit(solution)/shard_map/ppermute | solution.py:415
  168.1 16.4 %collective-permute-start.27 = (bf16[64,384]{1,0:T(8,128)(2,1)S(1)}, bf16[64,384]{1,0:T(8,128)(2,1)S(1)}, u32[]{:S(2)}, u32[]{:S(2)}) collective-permute-start(bf16[64,384]{1,0:T(8,128)(2,1)S(1)} %get-tuple-element.146.refs_9_.refs_1_), channel_id=1, source_target_pairs={{0,16},{2,18},{4,20},{6,22},{8,24},{10,26},{12,28},{14,30},{16,0},... | collective-permute-start | bytes 147464 | tf_op jit(solution)/shard_map/ppermute | solution.py:415
  168.9 15.6 %collective-permute-start.26 = (bf16[64,384]{1,0:T(8,128)(2,1)S(1)}, bf16[64,384]{1,0:T(8,128)(2,1)S(1)}, u32[]{:S(2)}, u32[]{:S(2)}) collective-permute-start(bf16[64,384]{1,0:T(8,128)(2,1)S(1)} %get-tuple-element.146.refs_9_.refs_1_), channel_id=1, source_target_pairs={{0,8},{2,10},{4,12},{6,14},{8,16},{10,18},{12,20},{14,22},{16,24},... | collective-permute-start | bytes 147464 | tf_op jit(solution)/shard_map/ppermute | solution.py:415
  191.1 18.1 %collective-permute-start.33 = (bf16[1024,384]{1,0:T(8,128)(2,1)}, bf16[1024,384]{1,0:T(8,128)(2,1)S(1)}, u32[]{:S(2)}, u32[]{:S(2)}) collective-permute-start(bf16[1024,384]{1,0:T(8,128)(2,1)} %get-tuple-element.161), channel_id=1, source_target_pairs={{0,1},{1,0},{2,3},{3,2},{4,5},{5,4},{6,7},{7,6},{8,9},{9,8},{10,11... | collective-permute-start | bytes 2359304 | tf_op jit(solution)/shard_map/ppermute | solution.py:394
  191.1 88.9 %collective-permute-start.8 = (bf16[3,400,384]{2,1,0:T(8,128)(2,1)}, bf16[3,400,384]{2,1,0:T(8,128)(2,1)}, u32[]{:S(2)}, u32[]{:S(2)}) collective-permute-start(bf16[3,400,384]{2,1,0:T(8,128)(2,1)} %get-tuple-element.110), channel_id=1, source_target_pairs={{0,1},{1,0},{2,3},{3,2},{4,5},{5,4},{6,7},{7,6},{8,9},{9,8},{10,11... | collective-permute-start | bytes 2764808 | tf_op jit(solution)/shard_map/ppermute | solution.py:394
  191.6 18.7 %collective-permute-start.65 = (bf16[128,384]{1,0:T(8,128)(2,1)S(1)}, bf16[128,384]{1,0:T(8,128)(2,1)S(1)}, u32[]{:S(2)}, u32[]{:S(2)}) collective-permute-start(bf16[128,384]{1,0:T(8,128)(2,1)S(1)} %get-tuple-element.184.refs_5_), channel_id=1, source_target_pairs={{0,24},{2,26},{4,28},{6,30},{8,0},{10,2},{12,4},{14,6},{16,8},{18,... | collective-permute-start | bytes 294920 | tf_op jit(solution)/shard_map/ppermute | solution.py:415
  197.1 16.2 %collective-permute-start.63 = (bf16[128,384]{1,0:T(8,128)(2,1)S(1)}, bf16[128,384]{1,0:T(8,128)(2,1)S(1)}, u32[]{:S(2)}, u32[]{:S(2)}) collective-permute-start(bf16[128,384]{1,0:T(8,128)(2,1)S(1)} %get-tuple-element.184.refs_5_), channel_id=1, source_target_pairs={{0,8},{2,10},{4,12},{6,14},{8,16},{10,18},{12,20},{14,22},{16,24},... | collective-permute-start | bytes 294920 | tf_op jit(solution)/shard_map/ppermute | solution.py:415
  219.6 62.3 %collective-permute-start.32 = (bf16[3,400,384]{2,1,0:T(8,128)(2,1)}, bf16[3,400,384]{2,1,0:T(8,128)(2,1)S(1)}, u32[]{:S(2)}, u32[]{:S(2)}) collective-permute-start(bf16[3,400,384]{2,1,0:T(8,128)(2,1)} %get-tuple-element.160.refs_5_.refs_9_), channel_id=1, source_target_pairs={{0,1},{1,0},{2,3},{3,2},{4,5},{5,4},{6,7},{7,6},{8,9},{9,8},{10,11... | collective-permute-start | bytes 2764808 | tf_op jit(solution)/shard_map/ppermute | solution.py:394
  241.5 40.7 %collective-permute-start.66 = (bf16[1024,384]{1,0:T(8,128)(2,1)S(1)}, bf16[1024,384]{1,0:T(8,128)(2,1)S(1)}, u32[]{:S(2)}, u32[]{:S(2)}) collective-permute-start(bf16[1024,384]{1,0:T(8,128)(2,1)S(1)} %get-tuple-element.185.refs_1_), channel_id=1, source_target_pairs={{0,1},{1,0},{2,3},{3,2},{4,5},{5,4},{6,7},{7,6},{8,9},{9,8},{10,11... | collective-permute-start | bytes 2359304 | tf_op jit(solution)/shard_map/ppermute | solution.py:394
  (94 other events, 782.0 us)
where the time goes:
time: 297 us; the launch traced here: 293 us
  Pallas kernels  151 us (51%)
  starting transfers between devices  81.4 us (27%)
  waiting for transfers between devices  35.4 us (12%)
  local copies, waits for them, and re-layouts  22.2 us (7%)
    pallas_call x9, Pallas kernels, big_call(): pl.pallas_call(body, grid_spec=pltpu.PrefetchScalarGridSpec(num_scalar_pr...  133 us
    ppermute x58, starting transfers between devices, shifted(): return lax.ppermute(value, axis, pairs)  79.7 us
    ppermute x58, waiting for transfers between devices, shifted(): return lax.ppermute(value, axis, pairs)  35.4 us
    pallas_call x14, Pallas kernels, small_call(): pl.pallas_call(body, in_specs=[pl.BlockSpec(memory_space=pltpu.SMEM), *[v...  18.3 us
    unnamed x109, local copies, waits for them, and re-layouts  12.8 us
  transfers between devices with their start and end apart: 68, of which 18 were waited for; matrix products, arithmetic and copies ran while one was open for 3% of the time, Pallas kernels for 40%

commit v1 on v0

--- a/solution.py
+++ b/solution.py
@@ -22,6 +22,8 @@
 BF = jnp.bfloat16
 F32 = jnp.float32
 VMEM_BYTES = 60 * 2**20
+CORE = 0
+BACK_SETS = (1, 1, 1)
 
 
 def dot(a, b, ca, cb):
@@ -73,17 +75,15 @@
 
 def project_kernel(
     blk_ref, views_ref, own_ref, far_ref, w_ref, pack_ref, w_out_ref, w1_ref, w2_ref, cot_ref,
-    x_ref, hat_ref, rstd_ref, qkv_ref, cls_ref, stat_ref, mix_ref, first_ref, full_ref,
+    hat_ref, qkv_ref, cls_ref, stat_ref, mix_ref, first_ref, full_ref,
 ):
     step = pl.program_id(0)
-    rows = x_ref.shape[1]
+    rows = hat_ref.shape[1]
     width = own_ref.shape[2]
     place_halves(full_ref, blk_ref[0], own_ref[0], far_ref[0])
-    x_ref[0] = full_ref[...]
     values = full_ref[...].astype(F32)
-    hat, rstd = norm_parts(values)
+    hat, _ = norm_parts(values)
     hat_ref[0] = hat.astype(BF)
-    rstd_ref[0] = rstd
     normed = (hat * row_of(pack_ref, GAIN1) + row_of(pack_ref, SHIFT1)).astype(BF)
     columns = pack_ref[0:8, :].T
     for third in range(3):
@@ -130,7 +130,14 @@
             stat_ref[k : k + 1, :] = jnp.sum(term, 0, keepdims=True)
 
 
-def attention_kernel(core_ref, views_ref, q_ref, k_ref, v_ref, pow_ref, sum_ref, att_ref):
+def masked_tail(scores, main, limit):
+    place = main + lax.broadcasted_iota(jnp.int32, scores.shape, 0)
+    return jnp.where(place < limit, scores, MASKED)
+
+
+def attention_kernel(
+    core_ref, views_ref, q_ref, k_ref, v_ref, sum_ref, top_ref, plain_ref, att_ref, pow_ref
+):
     sample = pl.program_id(0)
     pair = pl.program_id(1)
     rows = q_ref.shape[2]
@@ -154,71 +161,52 @@
             main = keys - 16
             for h, lanes in heads():
                 scores = dot(k_ref[0, lanes, :keys], q_ref[0, lanes, :], 0, 0)
-                pow_ref[0, h, :main, :] = jnp.exp2(scores[:main]).astype(BF)
-                place = main + lax.broadcasted_iota(jnp.int32, (16, rows), 0)
-                tail = jnp.where(place < limit, scores[main:], MASKED)
-                pow_ref[0, h, main:keys, :] = jnp.exp2(tail).astype(BF)
+                pow_ref[h, :main, :] = jnp.exp2(scores[:main]).astype(BF)
+                tail = masked_tail(scores[main:], main, limit)
+                pow_ref[h, main:keys, :] = jnp.exp2(tail).astype(BF)
                 left = jnp.concatenate((v_ref[0, lanes, :keys], ones[:, :keys]), 0)
-                store(h, dot(left, pow_ref[0, h, :keys, :], 1, 0))
+                store(h, dot(left, pow_ref[h, :keys, :], 1, 0))
 
     first = sum_ref[0, pl.ds(2 * pair, 1), :]
     second = sum_ref[0, pl.ds(2 * pair + 1, 1), :]
     least = jnp.min(jnp.minimum(first, second))
     plain = (least > SUM_LOW) & (jnp.max(jnp.maximum(first, second)) < SUM_HIGH)
+    plain_ref[sample, pair] = plain.astype(jnp.int32)
 
     @pl.when(jnp.logical_not(plain))
     def _():
         for h, lanes in heads():
             scores = dot(k_ref[0, lanes, :], q_ref[0, lanes, :], 0, 0)
-            place = lax.broadcasted_iota(jnp.int32, (rows, rows), 0)
-            scores = jnp.where(place < limit, scores, MASKED)
-            pow_ref[0, h] = jnp.exp2(scores - jnp.max(scores, 0, keepdims=True)).astype(BF)
+            scores = masked_tail(scores, 0, limit)
+            top = jnp.max(scores, 0, keepdims=True)
+            top_ref[0, pl.ds(2 * pair + h, 1), :] = top
+            pow_ref[h] = jnp.exp2(scores - top).astype(BF)
             left = jnp.concatenate((v_ref[0, lanes, :], ones), 0)
-            store(h, dot(left, pow_ref[0, h], 1, 0))
-
-
-def mlp_kernel(
-    blk_ref, x_ref, att_ref, w_out_ref, w1_ref, w2_ref, pack_ref,
-    hat_ref, rstd_ref, act_ref, slope_ref, own_ref, far_ref, out_ref,
-):
-    half = own_ref.shape[1]
-    width = own_ref.shape[2]
-    branch = dot(att_ref[0], w_out_ref[...], 0, 0) + row_of(pack_ref, OUT_BIAS)
-    middle = x_ref[0].astype(F32) + branch
-    hat, rstd = norm_parts(middle)
-    hat_ref[0] = hat.astype(BF)
-    rstd_ref[0] = rstd
-    normed = (hat * row_of(pack_ref, GAIN2) + row_of(pack_ref, SHIFT2)).astype(BF)
-    for r in range(2):
-        part = slice(r * half, (r + 1) * half)
-        for j in range(w1_ref.shape[1] // width):
-            cols = slice(j * width, (j + 1) * width)
-            pre = dot(normed[part], w1_ref[:, cols], 1, 0) + row_of(pack_ref, FC1_BIAS + j)
-            cdf = gelu_cdf(pre)
-            bell = jnp.exp(pre * pre * -0.5) * (1.0 / math.sqrt(2.0 * math.pi))
-            act_ref[0, part, cols] = (pre * cdf).astype(BF)
-            slope_ref[0, part, cols] = (cdf + pre * bell).astype(BF)
-        output = middle[part] + dot(act_ref[0, part, :], w2_ref[...], 1, 0)
-        out_ref[part, :] = (output + row_of(pack_ref, FC2_BIAS)).astype(BF)
-    split_halves(out_ref, blk_ref[0], own_ref, far_ref)
-
-
-def mlp_grads_kernel(
-    core_ref, own_ref, far_ref, cls_ref, cot_ref, *refs, samples, parts, peers
+            store(h, dot(left, pow_ref[h], 1, 0))
+
+
+def layer_kernel(
+    core_ref, x_own_ref, x_far_ref, own_ref, far_ref, att_ref, sum_ref, cls_ref, cot_ref, *refs,
+    samples, parts, peers
 ):
     stat_refs = refs[:peers]
-    act_ref, slope_ref, hat_ref, w2_ref = refs[peers : peers + 4]
-    dpre_ref, dcls_ref, norm_ref, bias_ref, kept_ref, sent_ref = refs[peers + 4 : peers + 10]
-    g_ref, acc2_ref, acc1_ref, flat_ref = refs[peers + 10 :]
+    w_out_ref, w1_ref, w2_ref, pack_ref = refs[peers : peers + 4]
+    (
+        out_own_ref, out_far_ref, gmid_ref, dmix_ref, inner_ref, out_grad_ref, norm_ref, bias_ref,
+        kept_ref, sent_ref,
+    ) = refs[peers + 4 : peers + 14]
+    full_ref, g_ref, act_ref, dpre_ref, dcls_ref, acc2_ref, acc1_ref, flat_ref = refs[peers + 14 :]
     step = pl.program_id(0)
     width = own_ref.shape[2]
     hidden = w2_ref.shape[0]
+    blocks = hidden // width
 
     @pl.when(step == 0)
     def _():
         acc2_ref[...] = jnp.zeros_like(acc2_ref)
         acc1_ref[...] = jnp.zeros_like(acc1_ref)
         bias_ref[...] = jnp.zeros_like(bias_ref)
+        out_grad_ref[...] = jnp.zeros_like(out_grad_ref)
         stats = stat_refs[0][...]
         for other in stat_refs[1:]:
             stats = stats + other[...]
@@ -233,51 +221,38 @@
         dcls_ref[...] = jnp.zeros_like(dcls_ref)
         dcls_ref[:local, :] = scale * (cot - stats[2:3] / samples - hat * (cross / samples))
 
-    place_halves(g_ref, core_ref[0], own_ref[0].astype(F32), far_ref[0].astype(F32))
+    place_halves(full_ref, core_ref[CORE], x_own_ref[0], x_far_ref[0])
+    place_halves(g_ref, core_ref[CORE], own_ref[0].astype(F32), far_ref[0].astype(F32))
     g_ref[0:1, :] = g_ref[0:1, :] + dcls_ref[pl.ds(step, 1), :]
     g_mlp = g_ref[...].astype(BF)
-    hat = hat_ref[0]
-    blocks = hidden // width
+    bias_ref[blocks : blocks + 1, :] += jnp.sum(g_mlp.astype(F32), 0, keepdims=True)
+
+    branch = dot(att_ref[0], w_out_ref[...], 0, 0) + row_of(pack_ref, OUT_BIAS)
+    middle = full_ref[...].astype(F32) + branch
+    hat, rstd = norm_parts(middle)
+    normed = (hat * row_of(pack_ref, GAIN2) + row_of(pack_ref, SHIFT2)).astype(BF)
+    hat_low = hat.astype(BF)
     for j in range(blocks):
         cols = slice(j * width, (j + 1) * width)
+        pre = dot(normed, w1_ref[:, cols], 1, 0) + row_of(pack_ref, FC1_BIAS + j)
         d_act = dot(g_mlp, w2_ref[cols, :], 1, 1)
-        d_pre = (d_act * slope_ref[0, :, cols].astype(F32)).astype(BF)
-        dpre_ref[0, :, cols] = d_pre
-        bias_ref[j : j + 1, :] += jnp.sum(d_pre.astype(F32), 0, keepdims=True)
-        acc1_ref[:, cols] += dot(hat, d_pre, 0, 0)
-        acc2_ref[cols, :] += dot(act_ref[0, :, cols], g_mlp, 0, 0)
-    bias_ref[blocks : blocks + 1, :] += jnp.sum(g_mlp.astype(F32), 0, keepdims=True)
-
-    @pl.when(step == pl.num_programs(0) - 1)
-    def _():
-        flat_ref[:hidden, :] = acc2_ref[...].astype(BF)
-        for j in range(blocks):
-            rows = slice(hidden + j * width, hidden + (j + 1) * width)
-            flat_ref[rows, :] = acc1_ref[:, j * width : (j + 1) * width].astype(BF)
-        clear_rest(flat_ref, 2 * hidden)
-        write_halves(core_ref[0], flat_ref, parts, kept_ref, sent_ref)
-
-
-def mlp_back_kernel(
-    blk_ref, own_ref, far_ref, dcls_ref, dpre_ref, hat_ref, rstd_ref, att_ref, sum_ref,
-    bias_in_ref, pack_ref, w1_ref, w_out_ref,
-    gmid_ref, dmix_ref, inner_ref, out_grad_ref, bias_ref, g_ref,
-):
-    step = pl.program_id(0)
-    width = own_ref.shape[2]
-    blocks = w1_ref.shape[1] // width
-
-    @pl.when(step == 0)
-    def _():
-        out_grad_ref[...] = jnp.zeros_like(out_grad_ref)
-        bias_ref[...] = bias_in_ref[...]
-
-    place_halves(g_ref, blk_ref[0], own_ref[0].astype(F32), far_ref[0].astype(F32))
-    g_ref[0:1, :] = g_ref[0:1, :] + dcls_ref[pl.ds(step, 1), :]
-    d_norm = dot(dpre_ref[0], w1_ref[...], 1, 1)
+        cdf = gelu_cdf(pre)
+        bell = jnp.exp(pre * pre * -0.5) * (1.0 / math.sqrt(2.0 * math.pi))
+        act = (pre * cdf).astype(BF)
+        act_ref[:, cols] = act
+        d_pre = d_act * (cdf + pre * bell)
+        bias_ref[j : j + 1, :] += jnp.sum(d_pre, 0, keepdims=True)
+        d_pre = d_pre.astype(BF)
+        dpre_ref[:, cols] = d_pre
+        acc1_ref[:, cols] += dot(hat_low, d_pre, 0, 0)
+        acc2_ref[cols, :] += dot(act, g_mlp, 0, 0)
+    output = middle + dot(act_ref[...], w2_ref[...], 1, 0) + row_of(pack_ref, FC2_BIAS)
+    full_ref[...] = output.astype(BF)
+    split_halves(full_ref, core_ref[CORE], out_own_ref, out_far_ref)
+
+    d_norm = dot(dpre_ref[...], w1_ref[...], 1, 1)
     u = d_norm * row_of(pack_ref, GAIN2)
-    hat = hat_ref[0].astype(F32)
-    g_mid = g_ref[...] + rstd_ref[0] * (
+    g_mid = g_ref[...] + rstd * (
         u - jnp.mean(u, -1, keepdims=True) - hat * jnp.mean(u * hat, -1, keepdims=True)
     )
     g_attn = g_mid.astype(BF)
@@ -291,65 +266,98 @@
         dmix_ref[0, part, :] = piece.astype(BF)
         inner_ref[0, h : h + 1, :] = jnp.sum(piece * att_ref[0, part, :].astype(F32), 0, keepdims=True)
 
+    @pl.when(step == pl.num_programs(0) - 1)
+    def _():
+        flat_ref[:hidden, :] = acc2_ref[...].astype(BF)
+        for j in range(blocks):
+            rows = slice(hidden + j * width, hidden + (j + 1) * width)
+            flat_ref[rows, :] = acc1_ref[:, j * width : (j + 1) * width].astype(BF)
+        clear_rest(flat_ref, 2 * hidden)
+        write_halves(core_ref[CORE], flat_ref, parts, kept_ref, sent_ref)
+
 
 def attention_back_kernel(
-    core_ref, views_ref, q_ref, k_ref, v_ref, pow_ref, dmix_ref, inner_ref, hat_ref,
-    dqkv_ref, grad_ref, sums_ref, *, pair
+    core_ref, views_ref, plain_ref, q_ref, k_ref, v_ref, top_ref, dmix_ref, inner_ref, hat_ref,
+    dqkv_ref, grad_ref, sums_ref, pow_ref, *, first
 ):
-    sample = pl.program_id(0)
+    sample = pl.program_id(1)
+    pair = first + pl.program_id(0)
     rows = hat_ref.shape[1]
-    views = views_ref[core_ref[CORE] * pl.num_programs(0) + sample]
+    views = views_ref[core_ref[CORE] * pl.num_programs(1) + sample]
+    limit = 1 + VIEW_ROWS * views
+    plain = plain_ref[sample, pair] == 1
+
+    def back(h, keys):
+        lanes = slice(h * HEAD_DIM, (h + 1) * HEAD_DIM)
+        d_mix = dmix_ref[0, lanes, :]
+        powers = pow_ref[h, :keys, :]
+        d_weights = dot(v_ref[0, lanes, :keys], d_mix, 0, 0)
+        inner = inner_ref[0, pl.ds(2 * pair + h, 1), :]
+        d_scores = (powers.astype(F32) * (d_weights - inner)).astype(BF)
+        d_query = dot(k_ref[0, lanes, :keys], d_scores, 1, 0) * SCALE
+        d_key = dot(q_ref[0, lanes, :], d_scores, 1, 1) * LN2
+        d_value = dot(d_mix, powers, 1, 1)
+        base = h * HEAD_DIM
+        dqkv_ref[0, 0, base : base + HEAD_DIM, :] = d_query.astype(BF)
+        dqkv_ref[0, 0, 128 + base : 128 + base + HEAD_DIM, :keys] = d_key.astype(BF)
+        dqkv_ref[0, 0, 256 + base : 256 + base + HEAD_DIM, :keys] = d_value.astype(BF)
+        if keys < rows:
+            blank = jnp.zeros((HEAD_DIM, rows - keys), BF)
+            dqkv_ref[0, 0, 128 + base : 128 + base + HEAD_DIM, keys:] = blank
+            dqkv_ref[0, 0, 256 + base : 256 + base + HEAD_DIM, keys:] = blank
+
     for count, keys in key_counts(rows):
 
-        @pl.when(views == count)
+        @pl.when((views == count) & plain)
         def _(keys=keys):
+            main = keys - 16
             for h in range(2):
                 lanes = slice(h * HEAD_DIM, (h + 1) * HEAD_DIM)
-                d_mix = dmix_ref[0, lanes, :]
-                powers = pow_ref[0, h, :keys, :]
-                d_weights = dot(v_ref[0, lanes, :keys], d_mix, 0, 0)
-                inner = inner_ref[0, 2 * pair + h : 2 * pair + h + 1, :]
-                d_scores = (powers.astype(F32) * (d_weights - inner)).astype(BF)
-                d_query = dot(k_ref[0, lanes, :keys], d_scores, 1, 0) * SCALE
-                d_key = dot(q_ref[0, lanes, :], d_scores, 1, 1) * LN2
-                d_value = dot(d_mix, powers, 1, 1)
-                base = h * HEAD_DIM
-                dqkv_ref[0, base : base + HEAD_DIM, :] = d_query.astype(BF)
-                dqkv_ref[0, 128 + base : 128 + base + HEAD_DIM, :keys] = d_key.astype(BF)
-                dqkv_ref[0, 256 + base : 256 + base + HEAD_DIM, :keys] = d_value.astype(BF)
-                if keys < rows:
-                    blank = jnp.zeros((HEAD_DIM, rows - keys), BF)
-                    dqkv_ref[0, 128 + base : 128 + base + HEAD_DIM, keys:] = blank
-                    dqkv_ref[0, 256 + base : 256 + base + HEAD_DIM, keys:] = blank
+                scores = dot(k_ref[0, lanes, :keys], q_ref[0, lanes, :], 0, 0)
+                pow_ref[h, :main, :] = jnp.exp2(scores[:main]).astype(BF)
+                tail = masked_tail(scores[main:], main, limit)
+                pow_ref[h, main:keys, :] = jnp.exp2(tail).astype(BF)
+                back(h, keys)
+
+    @pl.when(jnp.logical_not(plain))
+    def _():
+        for h in range(2):
+            lanes = slice(h * HEAD_DIM, (h + 1) * HEAD_DIM)
+            scores = masked_tail(dot(k_ref[0, lanes, :], q_ref[0, lanes, :], 0, 0), 0, limit)
+            top = top_ref[0, pl.ds(2 * pair + h, 1), :]
+            pow_ref[h] = jnp.exp2(scores - top).astype(BF)
+            back(h, rows)
 
     @pl.when(sample == 0)
     def _():
         grad_ref[...] = jnp.zeros_like(grad_ref)
         sums_ref[...] = jnp.zeros_like(sums_ref)
 
-    d_part = dqkv_ref[0]
-    grad_ref[...] += dot(d_part, hat_ref[0], 1, 0)
-    sums_ref[...] += dot(jnp.ones((16, rows), BF), d_part, 1, 1)[:8]
-
-
-def tokens_back_kernel(core_ref, *refs, pairs):
-    dqkv_refs = refs[:pairs]
-    w_ref, pack_ref, hat_ref, rstd_ref, gmid_ref, own_ref, far_ref, out_ref = refs[pairs:]
+    d_part = dqkv_ref[0, 0]
+    grad_ref[0] += dot(d_part, hat_ref[0], 1, 0)
+    sums_ref[0] += dot(jnp.ones((16, rows), BF), d_part, 1, 1)[:8]
+
+
+def tokens_back_kernel(core_ref, *refs, pairs, sets):
+    dqkv_refs = refs[:sets]
+    w_ref, pack_ref, x_own_ref, x_far_ref, gmid_ref, own_ref, far_ref, out_ref = refs[sets:]
     width = own_ref.shape[2]
+    place_halves(out_ref, core_ref[CORE], x_own_ref[0], x_far_ref[0])
+    hat, rstd = norm_parts(out_ref[...].astype(F32))
     d_norm = None
-    for pair in range(pairs):
-        w = jnp.concatenate(
-            [w_ref[t * width + pair * 128 : t * width + (pair + 1) * 128, :] for t in range(3)], 0
-        )
-        piece = dot(dqkv_refs[pair][0], w, 0, 0)
-        d_norm = piece if d_norm is None else d_norm + piece
+    pair = 0
+    for ref in dqkv_refs:
+        for k in range(ref.shape[0]):
+            w = jnp.concatenate(
+                [w_ref[t * width + pair * 128 : t * width + (pair + 1) * 128, :] for t in range(3)], 0
+            )
+            piece = dot(ref[k, 0], w, 0, 0)
+            d_norm = piece if d_norm is None else d_norm + piece
+            pair += 1
     w = d_norm * row_of(pack_ref, GAIN1)
-    hat = hat_ref[0].astype(F32)
-    back = rstd_ref[0] * (
-        w - jnp.mean(w, -1, keepdims=True) - hat * jnp.mean(w * hat, -1, keepdims=True)
-    )
+    back = rstd * (w - jnp.mean(w, -1, keepdims=True) - hat * jnp.mean(w * hat, -1, keepdims=True))
     out_ref[...] = (gmid_ref[0].astype(F32) + back).astype(BF)
-    split_halves(out_ref, core_ref[0], own_ref, far_ref)
+    split_halves(out_ref, core_ref[CORE], own_ref, far_ref)
 
 
 def clear_rest(ref, used):
@@ -369,25 +377,25 @@
         at += half
 
 
-def pack_kernel(core_ref, *refs, pairs, parts):
-    grad_refs = refs[:pairs]
-    sums_refs = refs[pairs : 2 * pairs]
-    out_grad_ref, bias_ref, kept_ref, sent_ref, flat_ref = refs[2 * pairs :]
+def pack_kernel(core_ref, *refs, sets, parts):
+    grad_refs = refs[:sets]
+    sums_refs = refs[sets : 2 * sets]
+    out_grad_ref, bias_ref, kept_ref, sent_ref, flat_ref = refs[2 * sets :]
     width = out_grad_ref.shape[0]
-    for pair in range(pairs):
-        flat_ref[pair * width : (pair + 1) * width, :] = grad_refs[pair][...].astype(BF)
-    at = pairs * width
+    rows = lax.broadcasted_iota(jnp.int32, (8, width), 0)
+    extra = jnp.zeros((8, width), F32)
+    pair = 0
+    for grad_ref, sums_ref in zip(grad_refs, sums_refs):
+        for k in range(grad_ref.shape[0]):
+            flat_ref[pair * width : (pair + 1) * width, :] = grad_ref[k].astype(BF)
+            extra = jnp.where(rows == pair, sums_ref[k][0:1, :], extra)
+            pair += 1
+    at = pair * width
     flat_ref[at : at + width, :] = out_grad_ref[...].astype(BF)
     at += width
     clear_rest(flat_ref, at)
-    vectors = [bias_ref[0:8, :]]
-    rows = lax.broadcasted_iota(jnp.int32, (8, width), 0)
-    extra = jnp.zeros((8, width), F32)
-    for pair in range(pairs):
-        extra = jnp.where(rows == pair, sums_refs[pair][0:1, :], extra)
-    vectors.append(extra)
-    flat_ref[at : at + 16, :] = jnp.concatenate(vectors, 0).astype(BF)
-    write_halves(core_ref[0], flat_ref, parts, kept_ref, sent_ref)
+    flat_ref[at : at + 16, :] = jnp.concatenate((bias_ref[0:8, :], extra), 0).astype(BF)
+    write_halves(core_ref[CORE], flat_ref, parts, kept_ref, sent_ref)
 
 
 def swap_cores(value):
@@ -469,9 +477,6 @@
             refs[out_at][k * size : (k + 1) * size, :] = refs[at + k][...]
         at += count
         out_at += 1
-
-
-CORE = 0
 
 
 class Layout:
@@ -686,14 +691,8 @@
     sds = jax.ShapeDtypeStruct
 
     unit = 32 * count
-
-    def split_rows(used):
-        total = pad_rows(used, unit)
-        second = pad_rows(total // 3, unit)
-        return [max(total - second, unit), second]
-
-    parts1 = split_rows(2 * hidden)
-    parts2 = split_rows(pairs * 384 + width + 16)
+    parts1 = [pad_rows(2 * hidden, unit)]
+    parts2 = [pad_rows(pairs * 384 + width + 16, unit)]
     layout = Layout(count, (parts1, parts2))
     device = lax.axis_index("samp") * cores + core
     info = lax.dynamic_index_in_dim(jnp.asarray(layout.table), device, 0, keepdims=False)
@@ -740,51 +739,20 @@
             name=name,
         )(*prefetch, *args, *ties)
 
-    x_full, hat1, rstd1, qkv, cls_rows, stats = big_call(
+    hat1, qkv, cls_rows, stats = big_call(
         project_kernel,
         (info, view_count),
         (tokens, far_tokens, w_turned, pack, w_out, w_fc1, w_fc2, cot_cls),
         [half_spec(own_map), half_spec(by_sample), *[vmem] * 6],
         [
             sds((local, rows, width), BF),
-            sds((local, rows, width), BF),
-            sds((local, rows, 1), F32),
             sds((local, 3 * width, rows), BF),
             sds((8, width), F32),
             sds((8, width), F32),
         ],
-        [
-            rows_spec, rows_spec, rstd_spec,
-            pl.BlockSpec((1, 3 * width, rows), by_sample), vmem, vmem,
-        ],
+        [rows_spec, pl.BlockSpec((1, 3 * width, rows), by_sample), vmem, vmem],
         [pltpu.VMEM((8, width), F32), pltpu.VMEM((8, width), F32), pltpu.VMEM((rows, width), BF)],
         name="project",
-    )
-
-    both = ("samp", "blk")
-    first, *later = stages(count * cores, 8)
-    stat_parts = [stats] + [shifted(stats, first, k, both) for k in range(1, first[1])]
-
-    qkv_specs = lambda p: [
-        pl.BlockSpec((1, 128, rows), lambda s, *a, t=t: (s, t * pairs + p(*a), 0)) for t in range(3)
-    ]
-    powers, totals, mixed = big_call(
-        attention_kernel,
-        (info, view_count),
-        (qkv, qkv, qkv),
-        qkv_specs(lambda p, *_: p),
-        [
-            sds((local, heads, rows, rows), BF),
-            sds((local, 8, rows), F32),
-            sds((local, width, rows), BF),
-        ],
-        [
-            pl.BlockSpec((1, 2, rows, rows), lambda s, p, *_: (s, p, 0, 0)),
-            pl.BlockSpec((1, 8, rows), lambda s, p, *_: (s, 0, 0)),
-            pl.BlockSpec((1, 128, rows), lambda s, p, *_: (s, p, 0)),
-        ],
-        grid=(local, pairs),
-        name="attention",
     )
 
     def add_kernel(info_ref, *refs):
@@ -793,120 +761,135 @@
             total = total + ref[...]
         refs[-1][...] = total
 
+    first, *later = stages(count)
+    stat_parts = [stats] + [shifted(stats, first, k) for k in range(1, first[1])]
+
+    qkv_specs = lambda f: [
+        pl.BlockSpec((1, 128, rows), lambda *a, t=t: (f(*a)[0], t * pairs + f(*a)[1], 0))
+        for t in range(3)
+    ]
+    totals, tops, plain, mixed = big_call(
+        attention_kernel,
+        (info, view_count),
+        (qkv, qkv, qkv),
+        qkv_specs(lambda s, p, *_: (s, p)),
+        [
+            sds((local, 8, rows), F32),
+            sds((local, 8, rows), F32),
+            sds((local, pairs), jnp.int32),
+            sds((local, width, rows), BF),
+        ],
+        [
+            pl.BlockSpec((1, 8, rows), lambda s, p, *_: (s, 0, 0)),
+            pl.BlockSpec((1, 8, rows), lambda s, p, *_: (s, 0, 0)),
+            pl.BlockSpec(memory_space=pltpu.SMEM),
+            pl.BlockSpec((1, 128, rows), lambda s, p, *_: (s, p, 0)),
+        ],
+        [pltpu.VMEM((2, rows, rows), BF)],
+        grid=(local, pairs),
+        name="attention",
+    )
+
     tie = totals
-    for stage in later:
+    for send in [functools.partial(lambda v, stage: [shifted(v, stage, k) for k in range(1, stage[1])], stage=stage) for stage in later] + [lambda v: [swap_cores(v)]]:
         stats = small_call(
             add_kernel, [info, *stat_parts], [sds((8, width), F32)], (), (tie,), "add"
         )[0]
-        stat_parts = [stats] + [shifted(stats, stage, k, both) for k in range(1, stage[1])]
+        stat_parts = [stats] + send(stats)
         tie = stats
 
-    hat2, rstd2, act, slope, out_own, out_far = big_call(
-        mlp_kernel,
+    tokens_out_own, out_far, g_mid, d_mix, inner, out_grad, cls_norm, biases, kept1, sent1 = big_call(
+        functools.partial(
+            layer_kernel, samples=local * cores * count, parts=parts1, peers=len(stat_parts)
+        ),
         (info,),
-        (x_full, mixed, w_out, w_fc1, w_fc2, pack),
-        [rows_spec, turned_spec, vmem, vmem, vmem, vmem],
+        (
+            tokens, far_tokens, cot_tokens, far_cot, mixed, totals, cls_rows, cot_cls, *stat_parts,
+            w_out, w_fc1, w_fc2, pack,
+        ),
         [
-            sds((local, rows, width), BF),
-            sds((local, rows, 1), F32),
-            sds((local, rows, hidden), BF),
-            sds((local, rows, hidden), BF),
+            half_spec(own_map), half_spec(by_sample), half_spec(own_map), half_spec(by_sample),
+            turned_spec, eight_spec, vmem, vmem, *[vmem] * len(stat_parts), vmem, vmem, vmem, vmem,
+        ],
+        [
             sds((samples, half, width), BF),
             sds((local, half, width), BF),
-        ],
-        [rows_spec, rstd_spec, hidden_spec, hidden_spec, half_spec(own_map), half_spec(by_sample)],
-        [pltpu.VMEM((rows, width), BF)],
-        (tie,),
-        name="mlp",
-    )
-    out_came = swap_cores(out_far)
-
-    d_pre, d_cls, cls_norm, biases, kept1, sent1 = big_call(
-        functools.partial(
-            mlp_grads_kernel, samples=local * cores * count, parts=parts1, peers=len(stat_parts)
-        ),
-        (info,),
-        (cot_tokens, far_cot, cls_rows, cot_cls, *stat_parts, act, slope, hat2, w_fc2),
-        [
-            half_spec(own_map), half_spec(by_sample), vmem, vmem, *[vmem] * len(stat_parts),
-            hidden_spec, hidden_spec, rows_spec, vmem,
-        ],
-        [
-            sds((local, rows, hidden), BF),
-            sds((8, width), F32),
+            sds((local, rows, width), BF),
+            sds((local, width, rows), BF),
+            sds((local, 8, rows), F32),
+            sds((width, width), F32),
             sds((local, width), BF),
             sds((8, width), F32),
             sds((sum(parts1) // 2, width), BF),
             sds((sum(parts1) // 2, width), BF),
         ],
-        [hidden_spec, vmem, vmem, vmem, vmem, vmem],
         [
+            half_spec(own_map), half_spec(by_sample), rows_spec, turned_spec, eight_spec,
+            vmem, vmem, vmem, vmem, vmem,
+        ],
+        [
+            pltpu.VMEM((rows, width), BF),
             pltpu.VMEM((rows, width), F32),
+            pltpu.VMEM((rows, hidden), BF),
+            pltpu.VMEM((rows, hidden), BF),
+            pltpu.VMEM((8, width), F32),
             pltpu.VMEM((hidden, width), F32),
             pltpu.VMEM((width, hidden), F32),
             pltpu.VMEM((sum(parts1), width), BF),
         ],
-        name="mlp_grads",
+        name="layer",
     )
+    out_own = tokens_out_own
+    out_came = swap_cores(out_far)
     chain1 = Chain(layout, 0, parts1, info)
-    tie = chain1.start(kept1, sent1)
-
-    g_mid, d_mix, inner, out_grad, biases = big_call(
-        mlp_back_kernel,
-        (info,),
-        (cot_tokens, far_cot, d_cls, d_pre, hat2, rstd2, mixed, totals, biases, pack, w_fc1, w_out),
-        [
-            half_spec(own_map), half_spec(by_sample), vmem, hidden_spec, rows_spec, rstd_spec,
-            turned_spec, eight_spec, vmem, vmem, vmem, vmem,
-        ],
-        [
-            sds((local, rows, width), BF),
-            sds((local, width, rows), BF),
-            sds((local, 8, rows), F32),
-            sds((width, width), F32),
-            sds((8, width), F32),
-        ],
-        [rows_spec, turned_spec, eight_spec, vmem, vmem],
-        [pltpu.VMEM((rows, width), F32)],
-        name="mlp_back",
-    )
+    chain1.start(kept1, sent1)
+
+    def attention_back(first, number, ties):
+        place = lambda p, s, *_: (s, first + p)
+        return big_call(
+            functools.partial(attention_back_kernel, first=first),
+            (info, view_count, plain),
+            (qkv, qkv, qkv, tops, d_mix, inner, hat1),
+            [
+                *qkv_specs(place),
+                pl.BlockSpec((1, 8, rows), lambda p, s, *_: (s, 0, 0)),
+                pl.BlockSpec((1, 128, rows), lambda p, s, *_: (s, first + p, 0)),
+                pl.BlockSpec((1, 8, rows), lambda p, s, *_: (s, 0, 0)),
+                pl.BlockSpec((1, rows, width), lambda p, s, *_: (s, 0, 0)),
+            ],
+            [
+                sds((number, local, 384, rows), BF),
+                sds((number, 384, width), F32),
+                sds((number, 8, 384), F32),
+            ],
+            [
+                pl.BlockSpec((1, 1, 384, rows), lambda p, s, *_: (p, s, 0, 0)),
+                pl.BlockSpec((1, 384, width), lambda p, s, *_: (p, 0, 0)),
+                pl.BlockSpec((1, 8, 384), lambda p, s, *_: (p, 0, 0)),
+            ],
+            [pltpu.VMEM((2, rows, rows), BF)],
+            ties,
+            grid=(number, local),
+            name="attention_back",
+        )
 
     steps = [functools.partial(chain1.scatter, level) for level in range(chain1.rounds + 1)]
     steps += [functools.partial(chain1.collect, level) for level in reversed(range(chain1.rounds))]
-    done = inner
+    done, tie = inner, inner
     d_parts, grads, sums = [], [], []
-    for pair in range(pairs):
-        tie = steps.pop(0)(ties=(done,))
-        d_part, grad, total = big_call(
-            functools.partial(attention_back_kernel, pair=pair),
-            (info, view_count),
-            (qkv, qkv, qkv, powers, d_mix, inner, hat1),
-            [
-                *qkv_specs(lambda *_, p=pair: p),
-                pl.BlockSpec((1, 2, rows, rows), lambda s, *_, p=pair: (s, p, 0, 0)),
-                pl.BlockSpec((1, 128, rows), lambda s, *_, p=pair: (s, p, 0)),
-                eight_spec,
-                rows_spec,
-            ],
-            [
-                sds((local, 384, rows), BF),
-                sds((384, width), F32),
-                sds((8, 384), F32),
-            ],
-            [pl.BlockSpec((1, 384, rows), by_sample), vmem, vmem],
-            (),
-            (tie,),
-            name="attention_back",
-        )
+    at = 0
+    for number in BACK_SETS:
+        d_part, grad, total = attention_back(at, number, (tie,))
+        at += number
         d_parts.append(d_part)
         grads.append(grad)
         sums.append(total)
         done = total
-
-    tie = steps.pop(0)(ties=(done,))
+        tie = steps.pop(0)(ties=(done,))
+
     chain2 = Chain(layout, 1, parts2, info)
     kept2, sent2 = small_call(
-        functools.partial(pack_kernel, pairs=pairs, parts=parts2),
+        functools.partial(pack_kernel, sets=len(grads), parts=parts2),
         (info, *grads, *sums, out_grad, biases),
         [sds((sum(parts2) // 2, width), BF)] * 2,
         [pltpu.VMEM((sum(parts2), width), BF)],
@@ -918,12 +901,14 @@
     steps2 += [functools.partial(chain2.collect, level) for level in reversed(range(chain2.rounds))]
 
     grad_own, grad_far = big_call(
-        functools.partial(tokens_back_kernel, pairs=pairs),
+        functools.partial(tokens_back_kernel, pairs=pairs, sets=len(d_parts)),
         (info,),
-        (*d_parts, w_turned, pack, hat1, rstd1, g_mid),
+        (*d_parts, w_turned, pack, tokens, far_tokens, g_mid),
         [
-            *[pl.BlockSpec((1, 384, rows), by_sample)] * pairs,
-            vmem, vmem, rows_spec, rstd_spec, rows_spec,
+            *[
+                pl.BlockSpec((d.shape[0], 1, 384, rows), lambda s, *_: (0, s, 0, 0)) for d in d_parts
+            ],
+            vmem, vmem, half_spec(own_map), half_spec(by_sample), rows_spec,
         ],
         [sds((samples, half, width), BF), sds((local, half, width), BF)],
         [half_spec(own_map), half_spec(by_sample)],
@@ -935,10 +920,10 @@
     done = grad_far
     while steps or steps2:
         ties = (done,)
+        if steps:
+            steps.pop(0)(ties=ties)
         if steps2:
             steps2.pop(0)(ties=ties)
-        if steps:
-            steps.pop(0)(ties=ties)
         done = info
 
     def finish(kernel, chain, args, outs, **options):

time: 297 us -> 259 us (0.87)
  starting transfers between devices: 81.4 us -> 52.7 us
  waiting for transfers between devices: 35.4 us -> 25.9 us
  Pallas kernels: 151 us -> 155 us
    ppermute x58 -> x30, starting transfers between devices: 79.7 us -> 51.1 us  [shifted(): return lax.ppermute(value, axis, pairs)]
    ppermute x58 -> x30, waiting for transfers between devices: 35.4 us -> 24.7 us  [shifted(): return lax.ppermute(value, axis, pairs)]
    pallas_call x9 -> x7, Pallas kernels: 133 us -> 137 us  [big_call(): pl.pallas_call(body, grid_spec=pltpu.PrefetchScalarGridSpec(num_scalar_pr...]
    pallas_call x14 -> x15, Pallas kernels: 18.3 us -> 17.7 us  [small_call(): pl.pallas_call(body, in_specs=[pl.BlockSpec(memory_space=pltpu.SMEM), *[v...]
    unnamed x109 -> x99, local copies, waits for them, and re-layouts: 12.8 us -> 12.2 us
  transfers between devices with their start and end apart: 68 -> 39, of which waited for: 18 -> 12; matrix products, arithmetic and copies ran while one was open for 3% -> 3% of each run, Pallas kernels for 40% -> 40%
where the time goes in v1:
time: 259 us; the launch traced here: 255 us
  Pallas kernels  155 us (60%)
  starting transfers between devices  52.7 us (20%)
  waiting for transfers between devices  25.9 us (10%)
  local copies, waits for them, and re-layouts  19.5 us (8%)
    pallas_call x7, Pallas kernels, big_call(): pl.pallas_call(body, grid_spec=pltpu.PrefetchScalarGridSpec(num_scalar_pr...  137 us
    ppermute x30, starting transfers between devices, shifted(): return lax.ppermute(value, axis, pairs)  51.1 us
    ppermute x30, waiting for transfers between devices, shifted(): return lax.ppermute(value, axis, pairs)  24.7 us
    pallas_call x15, Pallas kernels, small_call(): pl.pallas_call(body, in_specs=[pl.BlockSpec(memory_space=pltpu.SMEM), *[v...  17.7 us
    unnamed x99, local copies, waits for them, and re-layouts  12.2 us
  transfers between devices with their start and end apart: 39, of which 12 were waited for; matrix products, arithmetic and copies ran while one was open for 3% of the time, Pallas kernels for 40%

profile of v1, /device:TPU:0, one launch (start us, length us, event | category | flops | bytes accessed | tf_op | source)
XLA Modules:
  0.0 255.1 jit_solution(907686034568596533)
XLA Ops:
  0.7 2.3 constant_dynamic-slice_fusion.1
  11.0 13.3 %project.1 = (bf16[3,800,384]{2,1,0:T(8,128)(2,1)}, bf16[3,1152,800]{2,1,0:T(8,128)(2,1)}, f32[8,384]{1,0:T(8,128)}, f32[8,384]{1,0:T(8,128)}) custom-call(s32[67]{0:T(128)} %fusion.refs_0_.refs_5_, s32[6]{0:T(128)} %refs_1_.11, bf16[6,400,384]{2,1,0:T(8,128)(2,1)} %refs_6_.3, bf16[3,400,384]{2,1,0:T(8,128)(2,1)} %copy-done.30, bf16[1152,384]{1,0:T(8,128)(2,1)} %bitcast.5, ...), custom_call_target="tpu_custom_call" | custom-call | tf_op jit(solution)/shard_map/project/pallas_call | solution.py:728
  24.3 3.9 %collective-permute-start.4 = (f32[8,384]{1,0:T(8,128)}, f32[8,384]{1,0:T(8,128)S(1)}, u32[]{:S(2)}, u32[]{:S(2)}) collective-permute-start(f32[8,384]{1,0:T(8,128)} %get-tuple-element.72.refs_1_), channel_id=1, source_target_pairs={{0,6},{2,0},{4,2},{6,4},{8,14},{10,8},{12,10},{14,12},{16,22},{18,... | collective-permute-start | bytes 36872 | tf_op jit(solution)/shard_map/ppermute | solution.py:423
  29.2 15.8 %attention.1 = (f32[3,8,800]{2,1,0:T(8,128)}, f32[3,8,800]{2,1,0:T(8,128)}, s32[3,3]{1,0:T(4,128)}, bf16[3,384,800]{2,1,0:T(8,128)(2,1)}) custom-call(s32[67]{0:T(128)} %fusion.refs_0_.refs_5_, s32[6]{0:T(128)} %refs_1_.11, bf16[3,1152,800]{2,1,0:T(8,128)(2,1)} %get-tuple-element.68.refs_2_.refs_3_.refs_4_.refs_5_, ...), custom_call_target="tpu_custom_call" | custom-call | tf_op jit(solution)/shard_map/attention/pallas_call | solution.py:728
  52.3 2.3 collective-permute-done.5.refs_2_
  57.0 42.7 %layer.1 = (bf16[6,400,384]{2,1,0:T(8,128)(2,1)}, bf16[3,400,384]{2,1,0:T(8,128)(2,1)}, bf16[3,800,384]{2,1,0:T(8,128)(2,1)}, bf16[3,384,800]{2,1,0:T(8,128)(2,1...) custom-call(s32[67]{0:T(128)} %fusion.refs_0_.refs_5_, ...), custom_call_target="tpu_custom_call" | custom-call | tf_op jit(solution)/shard_map/layer/pallas_call | solution.py:728
  99.9 24.3 %attention_back.3 = (bf16[1,3,384,800]{3,2,1,0:T(8,128)(2,1)}, f32[1,384,384]{2,1,0:T(8,128)}, f32[1,8,384]{2,1,0:T(8,128)}) custom-call(s32[67]{0:T(128)} %fusion.refs_0_.refs_5_, s32[6]{0:T(128)} %refs_1_.11, s32[3,3]{1,0:T(4,128)} %get-tuple-element.76.refs_2_, bf16[3,1152,800]{2,1,0:T(8,128)(2,1)} %get-tuple-element.68.refs_2_.refs_3_.refs_4_.refs_5_, ...), custom_call_target="tpu_custom_call" | custom-call | tf_op jit(solution)/shard_map/attention_back/pallas_call | solution.py:728
  128.0 3.9 %collective-permute-start.12 = (bf16[384,384]{1,0:T(8,128)(2,1)}, bf16[384,384]{1,0:T(8,128)(2,1)S(1)}, u32[]{:S(2)}, u32[]{:S(2)}) collective-permute-start(bf16[384,384]{1,0:T(8,128)(2,1)} %get-tuple-element.88), channel_id=1, source_target_pairs={{0,4},{2,6},{4,0},{6,2},{8,12},{10,14},{12,8},{14,10},{16,20},{18,... | collective-permute-start | bytes 884744 | tf_op jit(solution)/shard_map/ppermute | solution.py:423
  131.9 15.6 %attention_back.4 = (bf16[1,3,384,800]{3,2,1,0:T(8,128)(2,1)}, f32[1,384,384]{2,1,0:T(8,128)}, f32[1,8,384]{2,1,0:T(8,128)}) custom-call(s32[67]{0:T(128)} %fusion.refs_0_.refs_5_, s32[6]{0:T(128)} %refs_1_.11, s32[3,3]{1,0:T(4,128)} %get-tuple-element.76.refs_2_, bf16[3,1152,800]{2,1,0:T(8,128)(2,1)} %get-tuple-element.68.refs_2_.refs_3_.refs_4_.refs_5_, ...), custom_call_target="tpu_custom_call" | custom-call | tf_op jit(solution)/shard_map/attention_back/pallas_call | solution.py:728
  150.7 3.1 %collective-permute-start.16 = (bf16[96,384]{1,0:T(8,128)(2,1)S(1)}, bf16[96,384]{1,0:T(8,128)(2,1)S(1)}, u32[]{:S(2)}, u32[]{:S(2)}) collective-permute-start(bf16[96,384]{1,0:T(8,128)(2,1)S(1)} %get-tuple-element.96), channel_id=1, source_target_pairs={{0,24},{2,26},{4,28},{6,30},{8,0},{10,2},{12,4},{14,6},{16,8},{18,... | collective-permute-start | bytes 221192 | tf_op jit(solution)/shard_map/ppermute | solution.py:423
  153.8 15.4 %attention_back.5 = (bf16[1,3,384,800]{3,2,1,0:T(8,128)(2,1)}, f32[1,384,384]{2,1,0:T(8,128)}, f32[1,8,384]{2,1,0:T(8,128)}) custom-call(s32[67]{0:T(128)} %fusion.refs_0_.refs_5_, s32[6]{0:T(128)} %refs_1_.11, s32[3,3]{1,0:T(4,128)} %get-tuple-element.76.refs_2_, bf16[3,1152,800]{2,1,0:T(8,128)(2,1)} %get-tuple-element.68.refs_2_.refs_3_.refs_4_.refs_5_, ...), custom_call_target="tpu_custom_call" | custom-call | tf_op jit(solution)/shard_map/attention_back/pallas_call | solution.py:728
  173.5 10.1 %tokens_back.1 = (bf16[6,400,384]{2,1,0:T(8,128)(2,1)}, bf16[3,400,384]{2,1,0:T(8,128)(2,1)}) custom-call(s32[67]{0:T(128)} %fusion.refs_0_.refs_5_, bf16[1,3,384,800]{3,2,1,0:T(8,128)(2,1)} %get-tuple-element.81.refs_1_, bf16[1,3,384,800]{3,2,1,0:T(8,128)(2,1)} %get-tuple-element.86.refs_2_, bf16[1,3,384,800]{3,2,1,0:T(8,128)(2,1)} %get-tuple-element.92.refs_3_, ...), custom_call_target="tpu_custom_call" | custom-call | tf_op jit(solution)/shard_map/tokens_back/pallas_call | solution.py:728
  184.7 2.7 %collective-permute-start.34 = (bf16[96,384]{1,0:T(8,128)(2,1)S(1)}, bf16[96,384]{1,0:T(8,128)(2,1)S(1)}, u32[]{:S(2)}, u32[]{:S(2)}) collective-permute-start(bf16[96,384]{1,0:T(8,128)(2,1)S(1)} %copy-done.8), channel_id=1, source_target_pairs={{0,24},{2,26},{4,28},{6,30},{8,0},{10,2},{12,4},{14,6},{16,8},{18,... | collective-permute-start | bytes 221192 | tf_op jit(solution)/shard_map/ppermute | solution.py:423
  190.6 2.9 %collective-permute-start.21 = (bf16[256,384]{1,0:T(8,128)(2,1)S(1)}, bf16[256,384]{1,0:T(8,128)(2,1)S(1)}, u32[]{:S(2)}, u32[]{:S(2)}) collective-permute-start(bf16[256,384]{1,0:T(8,128)(2,1)S(1)} %get-tuple-element.110), channel_id=1, source_target_pairs={{0,6},{2,0},{4,2},{6,4},{8,14},{10,8},{12,10},{14,12},{16,22},{18,... | collective-permute-start | bytes 589832 | tf_op jit(solution)/shard_map/ppermute | solution.py:423
  193.4 2.3 collective-permute-done.33.refs_3_
  196.3 2.6 %collective-permute-start.37 = (bf16[384,384]{1,0:T(8,128)(2,1)S(1)}, bf16[384,384]{1,0:T(8,128)(2,1)S(1)}, u32[]{:S(2)}, u32[]{:S(2)}) collective-permute-start(bf16[384,384]{1,0:T(8,128)(2,1)S(1)} %collect.6.refs_1_), channel_id=1, source_target_pairs={{0,6},{2,0},{4,2},{6,4},{8,14},{10,8},{12,10},{14,12},{16,22},{18,... | collective-permute-start | bytes 884744 | tf_op jit(solution)/shard_map/ppermute | solution.py:423
  202.0 4.4 %collective-permute-done.22.refs_2_ = bf16[64,384]{1,0:T(8,128)(2,1)S(1)} collective-permute-done((bf16[64,384]{1,0:T(8,128)(2,1)S(1)}, bf16[64,384]{1,0:T(8,128)(2,1)S(1)}, u32[]{:S(2)}, u32[]{:S(2)}) %collective-permute-start.22) | collective-permute-done | bytes 49184 | tf_op jit(solution)/shard_map/ppermute | solution.py:423
  207.4 3.5 %collective-permute-done.24.refs_4_ = bf16[64,384]{1,0:T(8,128)(2,1)S(1)} collective-permute-done((bf16[64,384]{1,0:T(8,128)(2,1)S(1)}, bf16[64,384]{1,0:T(8,128)(2,1)S(1)}, u32[]{:S(2)}, u32[]{:S(2)}) %collective-permute-start.24) | collective-permute-done | bytes 49184 | tf_op jit(solution)/shard_map/ppermute | solution.py:423
  215.6 3.4 %collective-permute-done.26.refs_3_ = bf16[64,384]{1,0:T(8,128)(2,1)S(1)} collective-permute-done((bf16[64,384]{1,0:T(8,128)(2,1)S(1)}, bf16[64,384]{1,0:T(8,128)(2,1)S(1)}, u32[]{:S(2)}, u32[]{:S(2)}) %collective-permute-start.26) | collective-permute-done | bytes 49184 | tf_op jit(solution)/shard_map/ppermute | solution.py:423
  219.5 11.2 %collective-permute-start.30 = (bf16[256,384]{1,0:T(8,128)(2,1)S(1)}, bf16[256,384]{1,0:T(8,128)(2,1)S(1)}, u32[]{:S(2)}, u32[]{:S(2)}) collective-permute-start(bf16[256,384]{1,0:T(8,128)(2,1)S(1)} %collect.4.refs_1_), channel_id=1, source_target_pairs={{0,6},{2,0},{4,2},{6,4},{8,14},{10,8},{12,10},{14,12},{16,22},{18,... | collective-permute-start | bytes 589832 | tf_op jit(solution)/shard_map/ppermute | solution.py:423
  234.9 4.7 %collective-permute-start.28 = (bf16[256,384]{1,0:T(8,128)(2,1)S(1)}, bf16[256,384]{1,0:T(8,128)(2,1)S(1)}, u32[]{:S(2)}, u32[]{:S(2)}) collective-permute-start(bf16[256,384]{1,0:T(8,128)(2,1)S(1)} %collect.4.refs_1_), channel_id=1, source_target_pairs={{0,2},{2,4},{4,6},{6,0},{8,10},{10,12},{12,14},{14,8},{16,18},{18,... | collective-permute-start | bytes 589832 | tf_op jit(solution)/shard_map/ppermute | solution.py:423
  239.6 2.6 %collective-permute-done.29.refs_3_ = bf16[256,384]{1,0:T(8,128)(2,1)S(1)} collective-permute-done((bf16[256,384]{1,0:T(8,128)(2,1)S(1)}, bf16[256,384]{1,0:T(8,128)(2,1)S(1)}, u32[]{:S(2)}, u32[]{:S(2)}) %collective-permute-start.29) | collective-permute-done | bytes 196640 | tf_op jit(solution)/shard_map/ppermute | solution.py:423
  245.2 2.5 finish.2
  247.8 5.3 %finish.3 = (f32[384,1152]{1,0:T(8,128)}, f32[384,384]{1,0:T(8,128)}, f32[384,1536]{1,0:T(8,128)}, f32[24,384]{1,0:T(8,128)S(1)}) custom-call(s32[67]{0:T(128)S(1)} %copy-done.18, bf16[1024,384]{1,0:T(8,128)(2,1)S(1)} %collect.5.refs_1_, bf16[1024,384]{1,0:T(8,128)(2,1)S(1)} %collective-permute-done.31.refs_2_, f32[16,384]{1,0:T(8,128)S(1)} %copy-done.9, ...), custom_call_target="tpu_custom_call" | custom-call | tf_op jit(solution)/shard_map/finish/pallas_call | solution.py:435
  (191 shorter events, 52.8 us)
Async XLA Ops:
  4.8 50.5 %collective-permute-start.1 = (bf16[3,400,384]{2,1,0:T(8,128)(2,1)S(1)}, bf16[3,400,384]{2,1,0:T(8,128)(2,1)}, u32[]{:S(2)}, u32[]{:S(2)}) collective-permute-start(bf16[3,400,384]{2,1,0:T(8,128)(2,1)S(1)} %constant_dynamic-slice_fusion), channel_id=1, source_target_pairs={{0,1},{1,0},{2,3},{3,2},{4,5},{5,4},{6,7},{7,6},{8,9},{9,8},{10,11... | collective-permute-start | bytes 2764808 | tf_op jit(solution)/shard_map/ppermute | solution.py:402
  24.3 20.7 %collective-permute-start.4 = (f32[8,384]{1,0:T(8,128)}, f32[8,384]{1,0:T(8,128)S(1)}, u32[]{:S(2)}, u32[]{:S(2)}) collective-permute-start(f32[8,384]{1,0:T(8,128)} %get-tuple-element.72.refs_1_), channel_id=1, source_target_pairs={{0,6},{2,0},{4,2},{6,4},{8,14},{10,8},{12,10},{14,12},{16,22},{18,... | collective-permute-start | bytes 36872 | tf_op jit(solution)/shard_map/ppermute | solution.py:423
  28.1 16.9 %collective-permute-start.3 = (f32[8,384]{1,0:T(8,128)}, f32[8,384]{1,0:T(8,128)S(1)}, u32[]{:S(2)}, u32[]{:S(2)}) collective-permute-start(f32[8,384]{1,0:T(8,128)} %get-tuple-element.72.refs_1_), channel_id=1, source_target_pairs={{0,4},{2,6},{4,0},{6,2},{8,12},{10,14},{12,8},{14,10},{16,20},{18,... | collective-permute-start | bytes 36872 | tf_op jit(solution)/shard_map/ppermute | solution.py:423
  28.6 16.4 %collective-permute-start.2 = (f32[8,384]{1,0:T(8,128)}, f32[8,384]{1,0:T(8,128)S(1)}, u32[]{:S(2)}, u32[]{:S(2)}) collective-permute-start(f32[8,384]{1,0:T(8,128)} %get-tuple-element.72.refs_1_), channel_id=1, source_target_pairs={{0,2},{2,4},{4,6},{6,0},{8,10},{10,12},{12,14},{14,8},{16,18},{18,... | collective-permute-start | bytes 36872 | tf_op jit(solution)/shard_map/ppermute | solution.py:423
  99.7 24.5 %collective-permute-start.10 = (bf16[1536,384]{1,0:T(8,128)(2,1)}, bf16[1536,384]{1,0:T(8,128)(2,1)S(1)}, u32[]{:S(2)}, u32[]{:S(2)}) collective-permute-start(bf16[1536,384]{1,0:T(8,128)(2,1)} %get-tuple-element.83), channel_id=1, source_target_pairs={{0,1},{1,0},{2,3},{3,2},{4,5},{5,4},{6,7},{7,6},{8,9},{9,8},{10,11... | collective-permute-start | bytes 3538952 | tf_op jit(solution)/shard_map/ppermute | solution.py:402
  127.7 19.8 %collective-permute-start.11 = (bf16[384,384]{1,0:T(8,128)(2,1)}, bf16[384,384]{1,0:T(8,128)(2,1)S(1)}, u32[]{:S(2)}, u32[]{:S(2)}) collective-permute-start(bf16[384,384]{1,0:T(8,128)(2,1)} %get-tuple-element.87), channel_id=1, source_target_pairs={{0,2},{2,4},{4,6},{6,0},{8,10},{10,12},{12,14},{14,8},{16,18},{18,... | collective-permute-start | bytes 884744 | tf_op jit(solution)/shard_map/ppermute | solution.py:423
  128.0 19.5 %collective-permute-start.12 = (bf16[384,384]{1,0:T(8,128)(2,1)}, bf16[384,384]{1,0:T(8,128)(2,1)S(1)}, u32[]{:S(2)}, u32[]{:S(2)}) collective-permute-start(bf16[384,384]{1,0:T(8,128)(2,1)} %get-tuple-element.88), channel_id=1, source_target_pairs={{0,4},{2,6},{4,0},{6,2},{8,12},{10,14},{12,8},{14,10},{16,20},{18,... | collective-permute-start | bytes 884744 | tf_op jit(solution)/shard_map/ppermute | solution.py:423
  131.9 15.7 %collective-permute-start.13 = (bf16[384,384]{1,0:T(8,128)(2,1)S(1)}, bf16[384,384]{1,0:T(8,128)(2,1)S(1)}, u32[]{:S(2)}, u32[]{:S(2)}) collective-permute-start(bf16[384,384]{1,0:T(8,128)(2,1)S(1)} %get-tuple-element.89), channel_id=1, source_target_pairs={{0,6},{2,0},{4,2},{6,4},{8,14},{10,8},{12,10},{14,12},{16,22},{18,... | collective-permute-start | bytes 884744 | tf_op jit(solution)/shard_map/ppermute | solution.py:423
  149.7 19.6 %collective-permute-start.14 = (bf16[96,384]{1,0:T(8,128)(2,1)S(1)}, bf16[96,384]{1,0:T(8,128)(2,1)S(1)}, u32[]{:S(2)}, u32[]{:S(2)}) collective-permute-start(bf16[96,384]{1,0:T(8,128)(2,1)S(1)} %get-tuple-element.94), channel_id=1, source_target_pairs={{0,8},{2,10},{4,12},{6,14},{8,16},{10,18},{12,20},{14,22},{16,24},... | collective-permute-start | bytes 221192 | tf_op jit(solution)/shard_map/ppermute | solution.py:423
  149.7 19.6 %collective-permute-start.15 = (bf16[96,384]{1,0:T(8,128)(2,1)S(1)}, bf16[96,384]{1,0:T(8,128)(2,1)S(1)}, u32[]{:S(2)}, u32[]{:S(2)}) collective-permute-start(bf16[96,384]{1,0:T(8,128)(2,1)S(1)} %get-tuple-element.95), channel_id=1, source_target_pairs={{0,16},{2,18},{4,20},{6,22},{8,24},{10,26},{12,28},{14,30},{16,0},... | collective-permute-start | bytes 221192 | tf_op jit(solution)/shard_map/ppermute | solution.py:423
  150.7 18.6 %collective-permute-start.16 = (bf16[96,384]{1,0:T(8,128)(2,1)S(1)}, bf16[96,384]{1,0:T(8,128)(2,1)S(1)}, u32[]{:S(2)}, u32[]{:S(2)}) collective-permute-start(bf16[96,384]{1,0:T(8,128)(2,1)S(1)} %get-tuple-element.96), channel_id=1, source_target_pairs={{0,24},{2,26},{4,28},{6,30},{8,0},{10,2},{12,4},{14,6},{16,8},{18,... | collective-permute-start | bytes 221192 | tf_op jit(solution)/shard_map/ppermute | solution.py:423
  173.5 10.1 %collective-permute-start.18 = (bf16[1024,384]{1,0:T(8,128)(2,1)S(1)}, bf16[1024,384]{1,0:T(8,128)(2,1)S(1)}, u32[]{:S(2)}, u32[]{:S(2)}) collective-permute-start(bf16[1024,384]{1,0:T(8,128)(2,1)S(1)} %get-tuple-element.106), channel_id=1, source_target_pairs={{0,1},{1,0},{2,3},{3,2},{4,5},{5,4},{6,7},{7,6},{8,9},{9,8},{10,11... | collective-permute-start | bytes 2359304 | tf_op jit(solution)/shard_map/ppermute | solution.py:402
  184.6 14.3 %collective-permute-start.19 = (bf16[256,384]{1,0:T(8,128)(2,1)S(1)}, bf16[256,384]{1,0:T(8,128)(2,1)S(1)}, u32[]{:S(2)}, u32[]{:S(2)}) collective-permute-start(bf16[256,384]{1,0:T(8,128)(2,1)S(1)} %get-tuple-element.108), channel_id=1, source_target_pairs={{0,2},{2,4},{4,6},{6,0},{8,10},{10,12},{12,14},{14,8},{16,18},{18,... | collective-permute-start | bytes 589832 | tf_op jit(solution)/shard_map/ppermute | solution.py:423
  187.4 8.3 %collective-permute-start.33 = (bf16[96,384]{1,0:T(8,128)(2,1)S(1)}, bf16[96,384]{1,0:T(8,128)(2,1)S(1)}, u32[]{:S(2)}, u32[]{:S(2)}) collective-permute-start(bf16[96,384]{1,0:T(8,128)(2,1)S(1)} %copy-done.8), channel_id=1, source_target_pairs={{0,16},{2,18},{4,20},{6,22},{8,24},{10,26},{12,28},{14,30},{16,0},... | collective-permute-start | bytes 221192 | tf_op jit(solution)/shard_map/ppermute | solution.py:423
  190.6 9.0 %collective-permute-start.20 = (bf16[256,384]{1,0:T(8,128)(2,1)S(1)}, bf16[256,384]{1,0:T(8,128)(2,1)S(1)}, u32[]{:S(2)}, u32[]{:S(2)}) collective-permute-start(bf16[256,384]{1,0:T(8,128)(2,1)S(1)} %get-tuple-element.109), channel_id=1, source_target_pairs={{0,4},{2,6},{4,0},{6,2},{8,12},{10,14},{12,8},{14,10},{16,20},{18,... | collective-permute-start | bytes 589832 | tf_op jit(solution)/shard_map/ppermute | solution.py:423
  190.6 9.0 %collective-permute-start.21 = (bf16[256,384]{1,0:T(8,128)(2,1)S(1)}, bf16[256,384]{1,0:T(8,128)(2,1)S(1)}, u32[]{:S(2)}, u32[]{:S(2)}) collective-permute-start(bf16[256,384]{1,0:T(8,128)(2,1)S(1)} %get-tuple-element.110), channel_id=1, source_target_pairs={{0,6},{2,0},{4,2},{6,4},{8,14},{10,8},{12,10},{14,12},{16,22},{18,... | collective-permute-start | bytes 589832 | tf_op jit(solution)/shard_map/ppermute | solution.py:423
  196.3 16.6 %collective-permute-start.37 = (bf16[384,384]{1,0:T(8,128)(2,1)S(1)}, bf16[384,384]{1,0:T(8,128)(2,1)S(1)}, u32[]{:S(2)}, u32[]{:S(2)}) collective-permute-start(bf16[384,384]{1,0:T(8,128)(2,1)S(1)} %collect.6.refs_1_), channel_id=1, source_target_pairs={{0,6},{2,0},{4,2},{6,4},{8,14},{10,8},{12,10},{14,12},{16,22},{18,... | collective-permute-start | bytes 884744 | tf_op jit(solution)/shard_map/ppermute | solution.py:423
  198.9 14.6 %collective-permute-start.36 = (bf16[384,384]{1,0:T(8,128)(2,1)S(1)}, bf16[384,384]{1,0:T(8,128)(2,1)S(1)}, u32[]{:S(2)}, u32[]{:S(2)}) collective-permute-start(bf16[384,384]{1,0:T(8,128)(2,1)S(1)} %collect.6.refs_1_), channel_id=1, source_target_pairs={{0,4},{2,6},{4,0},{6,2},{8,12},{10,14},{12,8},{14,10},{16,20},{18,... | collective-permute-start | bytes 884744 | tf_op jit(solution)/shard_map/ppermute | solution.py:423
  198.9 14.7 %collective-permute-start.35 = (bf16[384,384]{1,0:T(8,128)(2,1)S(1)}, bf16[384,384]{1,0:T(8,128)(2,1)S(1)}, u32[]{:S(2)}, u32[]{:S(2)}) collective-permute-start(bf16[384,384]{1,0:T(8,128)(2,1)S(1)} %collect.6.refs_1_), channel_id=1, source_target_pairs={{0,2},{2,4},{4,6},{6,0},{8,10},{10,12},{12,14},{14,8},{16,18},{18,... | collective-permute-start | bytes 884744 | tf_op jit(solution)/shard_map/ppermute | solution.py:423
  213.6 29.9 %collective-permute-start.9 = (bf16[3,400,384]{2,1,0:T(8,128)(2,1)S(1)}, bf16[3,400,384]{2,1,0:T(8,128)(2,1)S(1)}, u32[]{:S(2)}, u32[]{:S(2)}) collective-permute-start(bf16[3,400,384]{2,1,0:T(8,128)(2,1)S(1)} %copy-done.44), channel_id=1, source_target_pairs={{0,1},{1,0},{2,3},{3,2},{4,5},{5,4},{6,7},{7,6},{8,9},{9,8},{10,11... | collective-permute-start | bytes 2764808 | tf_op jit(solution)/shard_map/ppermute | solution.py:402
  219.5 15.3 %collective-permute-start.30 = (bf16[256,384]{1,0:T(8,128)(2,1)S(1)}, bf16[256,384]{1,0:T(8,128)(2,1)S(1)}, u32[]{:S(2)}, u32[]{:S(2)}) collective-permute-start(bf16[256,384]{1,0:T(8,128)(2,1)S(1)} %collect.4.refs_1_), channel_id=1, source_target_pairs={{0,6},{2,0},{4,2},{6,4},{8,14},{10,8},{12,10},{14,12},{16,22},{18,... | collective-permute-start | bytes 589832 | tf_op jit(solution)/shard_map/ppermute | solution.py:423
  230.7 14.5 %collective-permute-start.38 = (bf16[1536,384]{1,0:T(8,128)(2,1)S(1)}, bf16[1536,384]{1,0:T(8,128)(2,1)S(1)}, u32[]{:S(2)}, u32[]{:S(2)}) collective-permute-start(bf16[1536,384]{1,0:T(8,128)(2,1)S(1)} %collect.7.refs_1_), channel_id=1, source_target_pairs={{0,1},{1,0},{2,3},{3,2},{4,5},{5,4},{6,7},{7,6},{8,9},{9,8},{10,11... | collective-permute-start | bytes 3538952 | tf_op jit(solution)/shard_map/ppermute | solution.py:402
  230.7 13.0 %collective-permute-start.17 = (bf16[3,400,384]{2,1,0:T(8,128)(2,1)}, bf16[3,400,384]{2,1,0:T(8,128)(2,1)S(1)}, u32[]{:S(2)}, u32[]{:S(2)}) collective-permute-start(bf16[3,400,384]{2,1,0:T(8,128)(2,1)} %get-tuple-element.105.refs_3_.refs_5_), channel_id=1, source_target_pairs={{0,1},{1,0},{2,3},{3,2},{4,5},{5,4},{6,7},{7,6},{8,9},{9,8},{10,11... | collective-permute-start | bytes 2764808 | tf_op jit(solution)/shard_map/ppermute | solution.py:402
  231.2 11.0 %collective-permute-start.29 = (bf16[256,384]{1,0:T(8,128)(2,1)S(1)}, bf16[256,384]{1,0:T(8,128)(2,1)S(1)}, u32[]{:S(2)}, u32[]{:S(2)}) collective-permute-start(bf16[256,384]{1,0:T(8,128)(2,1)S(1)} %collect.4.refs_1_), channel_id=1, source_target_pairs={{0,4},{2,6},{4,0},{6,2},{8,12},{10,14},{12,8},{14,10},{16,20},{18,... | collective-permute-start | bytes 589832 | tf_op jit(solution)/shard_map/ppermute | solution.py:423
  (60 other events, 506.5 us)

commit v2 on v1

v2 whole, which is shorter than its diff:
```python
import functools
import math

import jax
import jax.numpy as jnp
import numpy as np
from jax import lax
from jax.experimental import pallas as pl
from jax.experimental.pallas import tpu as pltpu
from jax.sharding import PartitionSpec as P

HEAD_DIM = 64
VIEW_ROWS = 196
NORM_EPS = 1e-06
CLS_EPS = 1e-05
MASKED = -1e30
LOG2E = math.log2(math.e)
LN2 = math.log(2.0)
SCALE = HEAD_DIM ** (-0.5)
SUM_LOW = 1e-15
SUM_HIGH = 1e15
BF = jnp.bfloat16
F32 = jnp.float32
VMEM_BYTES = 60 * 2**20
CORE = 0
EXTRA = 16


def dot(a, b, ca, cb):
    return lax.dot_general(a, b, (((ca,), (cb,)), ((), ())), preferred_element_type=F32)


def norm_parts(values):
    centre = jnp.mean(values, -1, keepdims=True)
    offset = values - centre
    rstd = lax.rsqrt(jnp.mean(offset * offset, -1, keepdims=True) + NORM_EPS)
    return offset * rstd, rstd


def gelu_cdf(values):
    return 0.5 + 0.5 * lax.erf(values * (0.5**0.5))


def params(semantics):
    return pltpu.CompilerParams(dimension_semantics=semantics, vmem_limit_bytes=VMEM_BYTES)


def whole(shape):
    return pl.BlockSpec(shape, lambda *_: (0,) * len(shape))


def key_counts(rows):
    views = (rows - 1) // VIEW_ROWS
    return [(v, min(rows, -(-(1 + VIEW_ROWS * v) // 16) * 16)) for v in range(1, views + 1)]


GAIN1, SHIFT1, GAIN2, SHIFT2, OUT_BIAS, FC2_BIAS, QV_BIAS, FC1_BIAS = 0, 1, 2, 3, 4, 5, 6, 8


def row_of(pack_ref, index):
    return pack_ref[index : index + 1, :]


def place_halves(target_ref, core, own, far):
    half = own.shape[0]
    target_ref[pl.ds(pl.multiple_of(core * half, 16), half), :] = own
    target_ref[pl.ds(pl.multiple_of((1 - core) * half, 16), half), :] = far


def split_halves(source_ref, core, own_ref, far_ref):
    half = own_ref.shape[1]
    own_ref[0] = source_ref[pl.ds(pl.multiple_of(core * half, 16), half), :]
    far_ref[0] = source_ref[pl.ds(pl.multiple_of((1 - core) * half, 16), half), :]


def project_kernel(
    blk_ref, views_ref, own_ref, far_ref, w_ref, pack_ref, w_out_ref, w1_ref, w2_ref, cot_ref,
    hat_ref, qkv_ref, cls_ref, stat_ref, mix_ref, first_ref, full_ref,
):
    step = pl.program_id(0)
    rows = hat_ref.shape[1]
    width = own_ref.shape[2]
    place_halves(full_ref, blk_ref[0], own_ref[0], far_ref[0])
    values = full_ref[...].astype(F32)
    hat, _ = norm_parts(values)
    hat_ref[0] = hat.astype(BF)
    normed = (hat * row_of(pack_ref, GAIN1) + row_of(pack_ref, SHIFT1)).astype(BF)
    columns = pack_ref[0:8, :].T
    for third in range(3):
        part = pl.ds(third * width, width)
        piece = dot(w_ref[part, :], normed, 1, 1)
        if third == 0:
            piece = (piece + columns[:, QV_BIAS : QV_BIAS + 1]) * (SCALE * LOG2E)
        if third == 2:
            piece = piece + columns[:, QV_BIAS + 1 : QV_BIAS + 2]
        qkv_ref[0, part, :] = piece.astype(BF)

    lead = qkv_ref[0, pl.ds(0, width), :128].astype(F32).T[0:1, :]
    head_of = lax.broadcasted_iota(jnp.int32, (8, width), 1) // HEAD_DIM
    pick = head_of == lax.broadcasted_iota(jnp.int32, (8, width), 0)
    queries = jnp.where(pick, lead, 0.0).astype(BF)
    scores = dot(queries, qkv_ref[0, pl.ds(width, width), :], 1, 0)
    limit = 1 + VIEW_ROWS * views_ref[blk_ref[CORE] * pl.num_programs(0) + step]
    place = lax.broadcasted_iota(jnp.int32, (8, rows), 1)
    scores = jnp.where(place < limit, scores, MASKED)
    powers = jnp.exp2(scores - jnp.max(scores, -1, keepdims=True))
    chances = (powers / jnp.sum(powers, -1, keepdims=True)).astype(BF)
    mixed = dot(chances, qkv_ref[0, pl.ds(2 * width, width), :], 1, 1)
    mix_ref[pl.ds(step, 1), :] = jnp.sum(jnp.where(pick, mixed, 0.0), 0, keepdims=True)
    first_ref[pl.ds(step, 1), :] = values[0:1, :]

    @pl.when(step == pl.num_programs(0) - 1)
    def _():
        branch = dot(mix_ref[...].astype(BF), w_out_ref[...], 1, 0) + row_of(pack_ref, OUT_BIAS)
        middle = first_ref[...] + branch
        normed2 = norm_parts(middle)[0] * row_of(pack_ref, GAIN2) + row_of(pack_ref, SHIFT2)
        normed2 = normed2.astype(BF)
        output = middle + row_of(pack_ref, FC2_BIAS)
        for j in range(w1_ref.shape[1] // width):
            cols = slice(j * width, (j + 1) * width)
            pre = dot(normed2, w1_ref[:, cols], 1, 0) + row_of(pack_ref, FC1_BIAS + j)
            act = (pre * gelu_cdf(pre)).astype(BF)
            output = output + dot(act, w2_ref[cols, :], 1, 0)
        cls_ref[...] = output
        count = cot_ref.shape[0]
        cls = output[:count]
        cot = cot_ref[...].astype(F32)
        stat_ref[...] = jnp.zeros_like(stat_ref)
        for k, term in enumerate((cls, cls * cls, cot, cot * cls)):
            stat_ref[k : k + 1, :] = jnp.sum(term, 0, keepdims=True)


def masked_tail(scores, main, limit):
    place = main + lax.broadcasted_iota(jnp.int32, scores.shape, 0)
    return jnp.where(place < limit, scores, MASKED)


def attention_kernel(
    core_ref, views_ref, qkv_ref, sum_ref, top_ref, plain_ref, att_ref, pow_ref
):
    sample = pl.program_id(0)
    rows = qkv_ref.shape[2]
    width = att_ref.shape[1]
    heads = width // HEAD_DIM
    views = views_ref[core_ref[CORE] * pl.num_programs(0) + sample]
    limit = 1 + VIEW_ROWS * views
    ones = jnp.ones((16, rows), BF)

    def store(h, mixed):
        total = mixed[HEAD_DIM : HEAD_DIM + 1]
        sum_ref[0, h : h + 1, :] = total
        att_ref[0, h * HEAD_DIM : (h + 1) * HEAD_DIM, :] = (mixed[:HEAD_DIM] * (1.0 / total)).astype(BF)

    sum_ref[0, heads:8, :] = jnp.ones((8 - heads, rows), F32)
    for count, keys in key_counts(rows):

        @pl.when(views == count)
        def _(keys=keys):
            main = keys - 16
            for h in range(heads):
                query, key, value = head_parts(qkv_ref, h, width, keys)
                slot = h % pow_ref.shape[0]
                scores = dot(key, query, 0, 0)
                pow_ref[slot, :main, :] = jnp.exp2(scores[:main]).astype(BF)
                tail = masked_tail(scores[main:], main, limit)
                pow_ref[slot, main:keys, :] = jnp.exp2(tail).astype(BF)
                left = jnp.concatenate((value, ones[:, :keys]), 0)
                store(h, dot(left, pow_ref[slot, :keys, :], 1, 0))

    totals = sum_ref[0]
    plain = (jnp.min(totals) > SUM_LOW) & (jnp.max(totals) < SUM_HIGH)
    plain_ref[sample] = plain.astype(jnp.int32)

    @pl.when(jnp.logical_not(plain))
    def _():
        for h in range(heads):
            query, key, value = head_parts(qkv_ref, h, width, rows)
            slot = h % pow_ref.shape[0]
            scores = masked_tail(dot(key, query, 0, 0), 0, limit)
            top = jnp.max(scores, 0, keepdims=True)
            top_ref[0, h : h + 1, :] = top
            pow_ref[slot] = jnp.exp2(scores - top).astype(BF)
            left = jnp.concatenate((value, ones), 0)
            store(h, dot(left, pow_ref[slot], 1, 0))


def head_parts(qkv_ref, h, width, keys):
    part = lambda t: slice(t * width + h * HEAD_DIM, t * width + (h + 1) * HEAD_DIM)
    return qkv_ref[0, part(0), :], qkv_ref[0, part(1), :keys], qkv_ref[0, part(2), :keys]


def layer_kernel(
    core_ref, x_own_ref, x_far_ref, own_ref, far_ref, att_ref, sum_ref, cls_ref, cot_ref, *refs,
    samples, parts, peers
):
    stat_refs = refs[:peers]
    w_out_ref, w1_ref, w2_ref, pack_ref = refs[peers : peers + 4]
    (
        out_own_ref, out_far_ref, gmid_ref, dmix_ref, inner_ref, out_grad_ref, norm_ref, bias_ref,
        kept_ref, sent_ref,
    ) = refs[peers + 4 : peers + 14]
    full_ref, g_ref, act_ref, dpre_ref, dcls_ref, acc2_ref, acc1_ref, flat_ref = refs[peers + 14 :]
    step = pl.program_id(0)
    width = own_ref.shape[2]
    hidden = w2_ref.shape[0]
    blocks = hidden // width

    @pl.when(step == 0)
    def _():
        acc2_ref[...] = jnp.zeros_like(acc2_ref)
        acc1_ref[...] = jnp.zeros_like(acc1_ref)
        bias_ref[...] = jnp.zeros_like(bias_ref)
        out_grad_ref[...] = jnp.zeros_like(out_grad_ref)
        stats = stat_refs[0][...]
        for other in stat_refs[1:]:
            stats = stats + other[...]
        local = cot_ref.shape[0]
        cls = cls_ref[...][:local]
        cot = cot_ref[...].astype(F32)
        mean = stats[0:1] / samples
        scale = lax.rsqrt(stats[1:2] / samples - mean * mean + CLS_EPS)
        hat = (cls - mean) * scale
        norm_ref[...] = hat.astype(BF)
        cross = scale * (stats[3:4] - mean * stats[2:3])
        dcls_ref[...] = jnp.zeros_like(dcls_ref)
        dcls_ref[:local, :] = scale * (cot - stats[2:3] / samples - hat * (cross / samples))

    place_halves(full_ref, core_ref[CORE], x_own_ref[0], x_far_ref[0])
    place_halves(g_ref, core_ref[CORE], own_ref[0].astype(F32), far_ref[0].astype(F32))
    g_ref[0:1, :] = g_ref[0:1, :] + dcls_ref[pl.ds(step, 1), :]
    g_mlp = g_ref[...].astype(BF)
    bias_ref[blocks : blocks + 1, :] += jnp.sum(g_mlp.astype(F32), 0, keepdims=True)

    branch = dot(att_ref[0], w_out_ref[...], 0, 0) + row_of(pack_ref, OUT_BIAS)
    middle = full_ref[...].astype(F32) + branch
    hat, rstd = norm_parts(middle)
    normed = (hat * row_of(pack_ref, GAIN2) + row_of(pack_ref, SHIFT2)).astype(BF)
    hat_low = hat.astype(BF)
    for j in range(blocks):
        cols = slice(j * width, (j + 1) * width)
        pre = dot(normed, w1_ref[:, cols], 1, 0) + row_of(pack_ref, FC1_BIAS + j)
        d_act = dot(g_mlp, w2_ref[cols, :], 1, 1)
        cdf = gelu_cdf(pre)
        bell = jnp.exp2(pre * pre * (-0.5 * LOG2E) - 0.5 * math.log2(2.0 * math.pi))
        act_ref[:, cols] = (pre * cdf).astype(BF)
        d_pre = d_act * (cdf + pre * bell)
        bias_ref[j : j + 1, :] += jnp.sum(d_pre, 0, keepdims=True)
        dpre_ref[:, cols] = d_pre.astype(BF)
    acc1_ref[...] += dot(hat_low, dpre_ref[...], 0, 0)
    acc2_ref[...] += dot(act_ref[...], g_mlp, 0, 0)
    output = middle + dot(act_ref[...], w2_ref[...], 1, 0) + row_of(pack_ref, FC2_BIAS)
    full_ref[...] = output.astype(BF)
    split_halves(full_ref, core_ref[CORE], out_own_ref, out_far_ref)

    d_norm = dot(dpre_ref[...], w1_ref[...], 1, 1)
    u = d_norm * row_of(pack_ref, GAIN2)
    g_mid = g_ref[...] + rstd * (
        u - jnp.mean(u, -1, keepdims=True) - hat * jnp.mean(u * hat, -1, keepdims=True)
    )
    g_attn = g_mid.astype(BF)
    gmid_ref[0] = g_attn
    out_grad_ref[...] += dot(att_ref[0], g_attn, 1, 0)
    bias_ref[blocks + 1 : blocks + 2, :] += jnp.sum(g_attn.astype(F32), 0, keepdims=True)
    d_mix = dot(w_out_ref[...], g_attn, 1, 1)
    for h in range(width // HEAD_DIM):
        part = slice(h * HEAD_DIM, (h + 1) * HEAD_DIM)
        piece = d_mix[part] * (1.0 / sum_ref[0, h : h + 1, :])
        dmix_ref[0, part, :] = piece.astype(BF)
        inner_ref[0, h : h + 1, :] = jnp.sum(piece * att_ref[0, part, :].astype(F32), 0, keepdims=True)

    @pl.when(step == pl.num_programs(0) - 1)
    def _():
        flat_ref[:hidden, :] = acc2_ref[...].astype(BF)
        for j in range(blocks):
            rows = slice(hidden + j * width, hidden + (j + 1) * width)
            flat_ref[rows, :] = acc1_ref[:, j * width : (j + 1) * width].astype(BF)
        clear_rest(flat_ref, 2 * hidden)
        write_halves(core_ref[CORE], flat_ref, parts, kept_ref, sent_ref)


def attention_back_kernel(
    core_ref, views_ref, plain_ref, qkv_ref, top_ref, dmix_ref, inner_ref, hat_ref,
    dqkv_ref, grad_ref, sums_ref, pow_ref, *, sample, samples
):
    rows, width = hat_ref.shape[1:]
    heads = width // HEAD_DIM
    views = views_ref[core_ref[CORE] * samples + sample]
    limit = 1 + VIEW_ROWS * views
    plain = plain_ref[sample] == 1

    def back(h, parts, slot, keys):
        query, key, value = parts
        place = lambda t: slice(t * width + h * HEAD_DIM, t * width + (h + 1) * HEAD_DIM)
        d_mix = dmix_ref[0, place(0), :]
        powers = pow_ref[slot, :keys, :]
        d_weights = dot(value, d_mix, 0, 0)
        inner = inner_ref[0, h : h + 1, :]
        d_scores = (powers.astype(F32) * (d_weights - inner)).astype(BF)
        d_query = dot(key, d_scores, 1, 0) * SCALE
        d_key = dot(query, d_scores, 1, 1) * LN2
        d_value = dot(d_mix, powers, 1, 1)
        dqkv_ref[0, place(0), :] = d_query.astype(BF)
        dqkv_ref[0, place(1), :keys] = d_key.astype(BF)
        dqkv_ref[0, place(2), :keys] = d_value.astype(BF)
        if keys < rows:
            blank = jnp.zeros((HEAD_DIM, rows - keys), BF)
            dqkv_ref[0, place(1), keys:] = blank
            dqkv_ref[0, place(2), keys:] = blank

    for count, keys in key_counts(rows):

        @pl.when((views == count) & plain)
        def _(keys=keys):
            main = keys - 16
            for h in range(heads):
                slot = h % pow_ref.shape[0]
                parts = head_parts(qkv_ref, h, width, keys)
                scores = dot(parts[1], parts[0], 0, 0)
                pow_ref[slot, :main, :] = jnp.exp2(scores[:main]).astype(BF)
                tail = masked_tail(scores[main:], main, limit)
                pow_ref[slot, main:keys, :] = jnp.exp2(tail).astype(BF)
                back(h, parts, slot, keys)

    @pl.when(jnp.logical_not(plain))
    def _():
        for h in range(heads):
            slot = h % pow_ref.shape[0]
            parts = head_parts(qkv_ref, h, width, rows)
            scores = masked_tail(dot(parts[1], parts[0], 0, 0), 0, limit)
            pow_ref[slot] = jnp.exp2(scores - top_ref[0, h : h + 1, :]).astype(BF)
            back(h, parts, slot, rows)

    right = jnp.concatenate((hat_ref[0], jnp.ones((rows, 128), BF)), 1)
    result = dot(dqkv_ref[0], right, 1, 0)
    grad_ref[...] = result[:, :width].astype(BF)
    sums_ref[...] = result[:, width:].T[:8]


def tokens_back_kernel(core_ref, *refs, sets):
    dqkv_refs = refs[:sets]
    w_ref, pack_ref, x_own_ref, x_far_ref, gmid_ref, own_ref, far_ref, out_ref, d_ref, sems = refs[sets:]
    step = pl.program_id(0)

    def fetch(k):
        return pltpu.make_async_copy(dqkv_refs[k].at[0], d_ref.at[k], sems.at[k])

    @pl.when(step == 0)
    def _():
        for k in range(sets):
            fetch(k).start()

    for k in range(sets):

        @pl.when(step == k)
        def _(k=k):
            fetch(k).wait()

    d_norm = dot(d_ref[step], w_ref[...], 0, 0)
    place_halves(out_ref, core_ref[CORE], x_own_ref[0], x_far_ref[0])
    hat, rstd = norm_parts(out_ref[...].astype(F32))
    w = d_norm * row_of(pack_ref, GAIN1)
    back = rstd * (w - jnp.mean(w, -1, keepdims=True) - hat * jnp.mean(w * hat, -1, keepdims=True))
    out_ref[...] = (gmid_ref[0].astype(F32) + back).astype(BF)
    split_halves(out_ref, core_ref[CORE], own_ref, far_ref)


def clear_rest(ref, used):
    if ref.shape[0] > used:
        ref[used:, :] = jnp.zeros((ref.shape[0] - used, ref.shape[1]), ref.dtype)


def write_halves(core, flat_ref, parts, kept_ref, sent_ref):
    start = at = 0
    for size in parts:
        half = size // 2
        mine = pl.multiple_of(start + core * half, 16)
        other = pl.multiple_of(start + (1 - core) * half, 16)
        kept_ref[at : at + half, :] = flat_ref[pl.ds(mine, half), :]
        sent_ref[at : at + half, :] = flat_ref[pl.ds(other, half), :]
        start += size
        at += half


def pack_kernel(core_ref, *refs, sets, parts):
    grad_refs = refs[:sets]
    sums_refs = refs[sets : 2 * sets]
    out_grad_ref, bias_ref, kept_ref, sent_ref, flat_ref = refs[2 * sets :]
    width = out_grad_ref.shape[0]
    used = grad_refs[0].shape[0]
    total, sums = grad_refs[0][...].astype(F32), sums_refs[0][...]
    for grad_ref, sums_ref in zip(grad_refs[1:], sums_refs[1:]):
        total = total + grad_ref[...].astype(F32)
        sums = sums + sums_ref[...]
    flat_ref[:used, :] = total.astype(BF)
    flat_ref[used : used + width, :] = out_grad_ref[...].astype(BF)
    clear_rest(flat_ref, used + width)
    write_halves(core_ref[CORE], flat_ref, parts, kept_ref, sent_ref)
    rows = lax.broadcasted_iota(jnp.int32, (8, width), 0)
    extra = jnp.zeros((8, width), F32)
    for t in range(used // width):
        extra = jnp.where(rows == t, sums[0:1, t * width : (t + 1) * width], extra)
    vectors = jnp.concatenate((bias_ref[0:8, :], extra), 0).astype(BF)
    at = sum(parts) // 2
    kept_ref[at : at + EXTRA, :] = vectors
    sent_ref[at : at + EXTRA, :] = vectors


def swap_cores(value):
    return lax.ppermute(value, "blk", [(0, 1), (1, 0)])


def stages(count, first=4):
    out = []
    stride = 1
    while stride < count:
        left = count // stride
        radix = first if not out and left % first == 0 else 4 if left % 4 == 0 else 2
        out.append((stride, radix))
        stride *= radix
    return out


def shifted(value, stage, steps, axis="samp"):
    stride, radix = stage
    count = lax.axis_size(axis)
    pairs = []
    for source in range(count):
        digit = (source // stride) % radix
        pairs.append((source, source + ((digit + steps) % radix - digit) * stride))
    return lax.ppermute(value, axis, pairs)


def small_call(kernel, args, outs, scratch=(), ties=(), name=None):
    def body(*refs):
        kernel(*refs[: len(args)], *refs[len(args) + len(ties) :])

    vmem = pl.BlockSpec(memory_space=pltpu.VMEM)
    size = lambda a: math.prod(a.shape) * jnp.dtype(a.dtype).itemsize
    total = sum(size(a) for a in (*args[1:], *outs)) + sum(
        math.prod(a.shape) * jnp.dtype(a.dtype).itemsize for a in scratch
    )
    return pl.pallas_call(
        body,
        in_specs=[
            pl.BlockSpec(memory_space=pltpu.SMEM),
            *[vmem] * (len(args) - 1),
            *[pl.BlockSpec(memory_space=pl.ANY)] * len(ties),
        ],
        out_specs=[vmem] * len(outs),
        out_shape=outs,
        scratch_shapes=list(scratch),
        compiler_params=pltpu.CompilerParams(vmem_limit_bytes=2 * total + 4 * 2**20),
        name=name,
    )(*args, *ties)


def spread_kernel(info_ref, *refs, count, radix, slot, extra):
    outputs = radix + (1 if extra and radix == 1 else 0)
    outs, total_ref = refs[count : count + outputs], refs[count + outputs]
    total = refs[0][...].astype(F32)
    for ref in refs[1:count]:
        total = total + ref[...].astype(F32)
    rows = total_ref.shape[0] - extra
    size = rows // radix
    total_ref[...] = total.astype(BF)
    if radix == 1:
        outs[0][...] = total_ref[:rows, :]
        if extra:
            outs[1][...] = total[rows:]
        return
    for k in range(radix):
        start = lax.rem(info_ref[slot] + k, radix) * size
        outs[k][:size, :] = total_ref[pl.ds(pl.multiple_of(start, 16), size), :]
        if extra:
            outs[k][size:, :] = total_ref[rows:, :]


def collect_kernel(info_ref, *refs, groups):
    at, out_at = 0, sum(groups)
    for count in groups:
        size = refs[at].shape[0]
        for k in range(count):
            refs[out_at][k * size : (k + 1) * size, :] = refs[at + k][...]
        at += count
        out_at += 1


class Layout:
    def __init__(self, count, rows):
        self.base = stages(count)
        self.count = count
        self.rows = rows
        table = np.zeros((2 * count, 1 + len(self.base)), np.int32)
        for device in range(2 * count):
            table[device, 0] = device % 2
            for i in range(len(self.base)):
                table[device, 1 + i] = self.digit(device, i)
        self.place = table.shape[1]
        places = np.stack([self.places(device, rows) for device in range(2 * count)])
        self.table = np.concatenate((table, places), 1).astype(np.int32)

    def digit(self, device, index):
        stride, radix = self.base[index]
        return (device // 2 // stride) % radix

    def places(self, device, rows):
        core = device % 2
        unit = rows // 2
        offsets = np.array([core * unit, (1 - core) * unit])
        for index, (_, radix) in enumerate(self.base):
            unit //= radix
            digit = (self.digit(device, index) - np.arange(radix)) % radix
            offsets = (offsets[:, None] + (digit * unit)[None, :]).reshape(-1)
        return offsets

    def own_places(self, rows):
        return np.array([self.places(device, rows)[0] for device in range(2 * self.count)], np.int32)


class Chain:
    def __init__(self, layout, info, extra=0):
        self.layout = layout
        self.info = info
        self.extra = extra
        self.rounds = len(layout.base)

    def start(self, kept, sent):
        self.pending = [kept, swap_cores(sent)]

    def scatter(self, level, ties=()):
        last = level == self.rounds
        radix = 1 if last else self.layout.base[level][1]
        rows, width = self.pending[0].shape
        size = (rows - self.extra) // radix
        if last:
            outs = [jax.ShapeDtypeStruct((size, width), BF)]
            if self.extra:
                outs.append(jax.ShapeDtypeStruct((self.extra, width), F32))
        else:
            outs = [jax.ShapeDtypeStruct((size + self.extra, width), BF)] * radix
        pieces = small_call(
            functools.partial(
                spread_kernel, count=len(self.pending), radix=radix, slot=1 + level, extra=self.extra
            ),
            (self.info, *self.pending), outs, [pltpu.VMEM((rows, width), BF)], ties, "spread",
        )
        if last:
            self.value = pieces[0]
            self.vectors = pieces[1] if self.extra else None
        else:
            stage = self.layout.base[level]
            self.pending = [pieces[0]] + [shifted(pieces[k], stage, k) for k in range(1, radix)]
        return pieces[0]

    def gather(self, level):
        stage = self.layout.base[level]
        self.pending = [self.value] + [shifted(self.value, stage, k) for k in range(1, stage[1])]

    def collect(self, ties=()):
        size, width = self.pending[0].shape
        outs = [jax.ShapeDtypeStruct((len(self.pending) * size, width), BF)]
        self.value = small_call(
            functools.partial(collect_kernel, groups=(len(self.pending),)),
            (self.info, *self.pending), outs, (), ties, "collect",
        )[0]
        return self.value


def restore(place_ref, flat_ref, ref, unit, at):
    def body(i, carry):
        start = pl.multiple_of(place_ref[at + i], 16)
        source = pl.multiple_of(i * unit, 16)
        chunk = ref[pl.ds(source, unit), :]
        flat_ref[pl.ds(start, unit), :] = chunk
        return carry

    lax.fori_loop(0, ref.shape[0] // unit, body, 0)


def finish_mlp_kernel(place_ref, all_ref, vectors_ref, pack_ref, w1_ref, fc2_ref, fc1_ref, rows_ref, flat_ref, *, unit):
    restore(place_ref, flat_ref, all_ref, unit, 0)
    hidden, width = fc2_ref.shape
    fc2_ref[...] = flat_ref[:hidden, :].astype(F32)
    columns = pack_ref[0:8, :].T
    gain = jnp.zeros((width, 1), F32)
    shift = jnp.zeros((width, 1), F32)
    for j in range(hidden // width):
        cols = slice(j * width, (j + 1) * width)
        hats = flat_ref[hidden + j * width : hidden + (j + 1) * width, :].astype(F32)
        sums = vectors_ref[j : j + 1, :]
        fc1_ref[:, cols] = hats * columns[:, GAIN2 : GAIN2 + 1] + columns[:, SHIFT2 : SHIFT2 + 1] * sums
        w = w1_ref[:, cols].astype(F32)
        gain = gain + jnp.sum(w * hats, -1, keepdims=True)
        shift = shift + jnp.sum(w * sums, -1, keepdims=True)
    lane = lax.broadcasted_iota(jnp.int32, (width, 128), 1)
    rows_ref[...] = jnp.where(lane == 0, gain, jnp.where(lane == 1, shift, 0.0)).T[0:8]


def finish_kernel(
    info_ref, own_ref, far_ref, vectors_ref, pack_ref, w_ref, qkv_ref, out_ref, rows_ref, flat_ref, *, unit, at
):
    restore(info_ref, flat_ref, own_ref, unit, at)
    restore(info_ref, flat_ref, far_ref, unit, at + own_ref.shape[0] // unit)
    width = out_ref.shape[0]
    columns = qkv_ref.shape[1]
    out_ref[...] = flat_ref[columns : columns + width, :].astype(F32)
    gain = jnp.zeros((1, width), F32)
    shift = jnp.zeros((1, width), F32)
    turned = vectors_ref[8:16, :].T
    for t in range(columns // width):
        part = slice(t * width, (t + 1) * width)
        hats = flat_ref[part, :].astype(F32)
        sums = turned[:, t : t + 1]
        result = hats * row_of(pack_ref, GAIN1) + sums * row_of(pack_ref, SHIFT1)
        qkv_ref[:, part] = result.T
        w = w_ref[part, :].astype(F32)
        gain = gain + jnp.sum(w * hats, 0, keepdims=True)
        shift = shift + jnp.sum(w * sums, 0, keepdims=True)
    rows_ref[...] = jnp.concatenate((gain, shift, jnp.zeros((6, width), F32)), 0)


def pad_rows(count, unit):
    return -(-count // unit) * unit


def per_device(
    tokens, view_count, norm1_gain, norm1_bias, w_qkv, qv_bias, w_out, out_bias,
    norm2_gain, norm2_bias, w_fc1, fc1_bias, w_fc2, fc2_bias, cot_tokens, cot_cls,
):
    core = lax.axis_index("blk")
    cores = lax.axis_size("blk")
    count = lax.axis_size("samp")
    samples, half, width = tokens.shape
    local = samples // cores
    rows = half * cores
    hidden = w_fc1.shape[1]
    blocks = hidden // width
    heads = width // HEAD_DIM
    pairs = heads // 2
    sds = jax.ShapeDtypeStruct

    unit = 32 * count
    parts1 = [pad_rows(2 * hidden, unit)]
    parts2 = [pad_rows(4 * width, unit)]
    layout = Layout(count, parts2[0])
    device = lax.axis_index("samp") * cores + core
    info = lax.dynamic_index_in_dim(jnp.asarray(layout.table), device, 0, keepdims=False)

    theirs = (1 - core) * local
    far_tokens = swap_cores(lax.dynamic_slice_in_dim(tokens, theirs, local, 0))
    far_cot = swap_cores(lax.dynamic_slice_in_dim(cot_tokens, theirs, local, 0))

    w_turned = w_qkv.T
    pack = jnp.concatenate(
        (
            norm1_gain, norm1_bias, norm2_gain, norm2_bias, out_bias, fc2_bias, qv_bias, fc1_bias,
            jnp.zeros(((8 - blocks) * width,), BF),
        )
    ).astype(F32).reshape(16, width)

    vmem = pl.BlockSpec(memory_space=pltpu.VMEM)
    half_spec = lambda f: pl.BlockSpec((1, half, width), f)
    own_map = lambda s, b, *_: (b[CORE] * local + s, 0, 0)
    by_sample = lambda s, *_: (s, 0, 0)
    rows_spec = pl.BlockSpec((1, rows, width), by_sample)
    turned_spec = pl.BlockSpec((1, width, rows), by_sample)
    rstd_spec = pl.BlockSpec((1, rows, 1), by_sample)
    hidden_spec = pl.BlockSpec((1, rows, hidden), by_sample)
    eight_spec = pl.BlockSpec((1, 8, rows), by_sample)

    def big_call(kernel, prefetch, args, in_specs, outs, out_specs, scratch=(), ties=(), grid=(local,), name=None):
        n = len(prefetch) + len(args)

        def body(*refs):
            kernel(*refs[:n], *refs[n + len(ties) :])

        return pl.pallas_call(
            body,
            grid_spec=pltpu.PrefetchScalarGridSpec(
                num_scalar_prefetch=len(prefetch),
                grid=grid,
                in_specs=[*in_specs, *[pl.BlockSpec(memory_space=pl.ANY)] * len(ties)],
                out_specs=out_specs,
                scratch_shapes=list(scratch),
            ),
            out_shape=outs,
            compiler_params=params(("arbitrary",) * len(grid)),
            name=name,
        )(*prefetch, *args, *ties)

    hat1, qkv, cls_rows, stats = big_call(
        project_kernel,
        (info, view_count),
        (tokens, far_tokens, w_turned, pack, w_out, w_fc1, w_fc2, cot_cls),
        [half_spec(own_map), half_spec(by_sample), *[vmem] * 6],
        [
            sds((local, rows, width), BF),
            sds((local, 3 * width, rows), BF),
            sds((8, width), F32),
            sds((8, width), F32),
        ],
        [rows_spec, pl.BlockSpec((1, 3 * width, rows), by_sample), vmem, vmem],
        [pltpu.VMEM((8, width), F32), pltpu.VMEM((8, width), F32), pltpu.VMEM((rows, width), BF)],
        name="project",
    )

    def add_kernel(info_ref, *refs):
        total = refs[0][...]
        for ref in refs[1:-1]:
            total = total + ref[...]
        refs[-1][...] = total

    first, *later = stages(count)
    stat_parts = [stats] + [shifted(stats, first, k) for k in range(1, first[1])]

    qkv_spec = lambda f: pl.BlockSpec((1, 3 * width, rows), f)
    totals, tops, plain, mixed = big_call(
        attention_kernel,
        (info, view_count),
        (qkv,),
        [qkv_spec(by_sample)],
        [
            sds((local, 8, rows), F32),
            sds((local, 8, rows), F32),
            sds((local,), jnp.int32),
            sds((local, width, rows), BF),
        ],
        [eight_spec, eight_spec, pl.BlockSpec(memory_space=pltpu.SMEM), turned_spec],
        [pltpu.VMEM((2, rows, rows), BF)],
        name="attention",
    )

    tie = totals
    for send in [functools.partial(lambda v, stage: [shifted(v, stage, k) for k in range(1, stage[1])], stage=stage) for stage in later] + [lambda v: [swap_cores(v)]]:
        stats = small_call(
            add_kernel, [info, *stat_parts], [sds((8, width), F32)], (), (tie,), "add"
        )[0]
        stat_parts = [stats] + send(stats)
        tie = stats

    tokens_out_own, out_far, g_mid, d_mix, inner, out_grad, cls_norm, biases, kept1, sent1 = big_call(
        functools.partial(
            layer_kernel, samples=local * cores * count, parts=parts1, peers=len(stat_parts)
        ),
        (info,),
        (
            tokens, far_tokens, cot_tokens, far_cot, mixed, totals, cls_rows, cot_cls, *stat_parts,
            w_out, w_fc1, w_fc2, pack,
        ),
        [
            half_spec(own_map), half_spec(by_sample), half_spec(own_map), half_spec(by_sample),
            turned_spec, eight_spec, vmem, vmem, *[vmem] * len(stat_parts), vmem, vmem, vmem, vmem,
        ],
        [
            sds((samples, half, width), BF),
            sds((local, half, width), BF),
            sds((local, rows, width), BF),
            sds((local, width, rows), BF),
            sds((local, 8, rows), F32),
            sds((width, width), F32),
            sds((local, width), BF),
            sds((8, width), F32),
            sds((sum(parts1) // 2, width), BF),
            sds((sum(parts1) // 2, width), BF),
        ],
        [
            half_spec(own_map), half_spec(by_sample), rows_spec, turned_spec, eight_spec,
            vmem, vmem, vmem, vmem, vmem,
        ],
        [
            pltpu.VMEM((rows, width), BF),
            pltpu.VMEM((rows, width), F32),
            pltpu.VMEM((rows, hidden), BF),
            pltpu.VMEM((rows, hidden), BF),
            pltpu.VMEM((8, width), F32),
            pltpu.VMEM((hidden, width), F32),
            pltpu.VMEM((width, hidden), F32),
            pltpu.VMEM((sum(parts1), width), BF),
        ],
        name="layer",
    )
    chain1 = Chain(layout, info)
    chain1.start(kept1, sent1)
    out_came = swap_cores(out_far)

    def attention_back(sample, ties):
        place = lambda *_: (sample, 0, 0)
        return big_call(
            functools.partial(attention_back_kernel, sample=sample, samples=local),
            (info, view_count, plain),
            (qkv, tops, d_mix, inner, hat1),
            [
                qkv_spec(place),
                pl.BlockSpec((1, 8, rows), place),
                pl.BlockSpec((1, width, rows), place),
                pl.BlockSpec((1, 8, rows), place),
                pl.BlockSpec((1, rows, width), place),
            ],
            [
                sds((1, 3 * width, rows), BF),
                sds((3 * width, width), BF),
                sds((8, 3 * width), F32),
            ],
            [qkv_spec(lambda *_: (0, 0, 0)), vmem, vmem],
            [pltpu.VMEM((2, rows, rows), BF)],
            ties,
            grid=(1,),
            name="attention_back",
        )

    ties = (inner,)
    d_parts, grads, sums = [], [], []
    for sample in range(local):
        d_part, grad, total = attention_back(sample, ties)
        d_parts.append(d_part)
        grads.append(grad)
        sums.append(total)
        if sample <= chain1.rounds:
            ties = (chain1.scatter(sample, (total,)),)
        if sample == 0:
            tokens_out = lax.dynamic_update_slice_in_dim(tokens_out_own, out_came, theirs, 0)
            ties = (*ties, tokens_out)
    for level in range(local, chain1.rounds + 1):
        ties = (chain1.scatter(level),)
    gathered = lax.all_gather(chain1.value, ("samp", "blk"), axis=0, tiled=True)

    chain2 = Chain(layout, info, EXTRA)
    kept2, sent2 = small_call(
        functools.partial(pack_kernel, sets=len(grads), parts=parts2),
        (info, *grads, *sums, out_grad, biases),
        [sds((sum(parts2) // 2 + EXTRA, width), BF)] * 2,
        [pltpu.VMEM((sum(parts2), width), BF)],
        ties,
        name="pack",
    )
    chain2.start(kept2, sent2)
    tie = chain2.scatter(0)

    grad_own, grad_far = big_call(
        functools.partial(tokens_back_kernel, sets=len(d_parts)),
        (info,),
        (*d_parts, w_turned, pack, tokens, far_tokens, g_mid),
        [
            *[pl.BlockSpec(memory_space=pl.ANY)] * len(d_parts),
            vmem, vmem, half_spec(own_map), half_spec(by_sample), rows_spec,
        ],
        [sds((samples, half, width), BF), sds((local, half, width), BF)],
        [half_spec(own_map), half_spec(by_sample)],
        [
            pltpu.VMEM((rows, width), BF),
            pltpu.VMEM((len(d_parts), 3 * width, rows), BF),
            pltpu.SemaphoreType.DMA((len(d_parts),)),
        ],
        (tie,),
        name="tokens_back",
    )
    grad_came = swap_cores(grad_far)
    ties = (grad_far,)
    for level in range(1, chain2.rounds + 1):
        chain2.scatter(level, ties)
        ties = ()
    for level in reversed(range(chain2.rounds)):
        chain2.gather(level)
        if level == chain2.rounds - 1:
            grad_tokens = lax.dynamic_update_slice_in_dim(grad_own, grad_came, theirs, 0)
            ties = (grad_tokens,)
        chain2.collect(ties)
        ties = ()
    other = swap_cores(chain2.value)

    grad_w_fc2, grad_w_fc1, rows2 = small_call(
        functools.partial(finish_mlp_kernel, unit=parts1[0] // (2 * count)),
        (jnp.asarray(layout.own_places(parts1[0])), gathered, chain2.vectors, pack, w_fc1),
        [sds((hidden, width), F32), sds((width, hidden), F32), sds((8, width), F32)],
        [pltpu.VMEM((parts1[0], width), BF)],
        (chain2.value,),
        name="finish_mlp",
    )
    grad_w_qkv, grad_w_out, rows1 = small_call(
        functools.partial(finish_kernel, unit=parts2[0] // (2 * count), at=layout.place),
        (info, chain2.value, other, chain2.vectors, pack, w_turned),
        [sds((width, 3 * width), F32), sds((width, width), F32), sds((8, width), F32)],
        [pltpu.VMEM((parts2[0], width), BF)],
        name="finish",
    )
    vectors = chain2.vectors
    grad_qv_bias = jnp.concatenate((vectors[8], vectors[10]))
    return (
        tokens_out, cls_norm, grad_tokens, rows1[0], rows1[1], grad_w_qkv, grad_qv_bias,
        grad_w_out, vectors[blocks + 1], rows2[0], rows2[1], grad_w_fc1,
        vectors[:blocks].reshape(hidden), grad_w_fc2, vectors[blocks],
    )


def solution(mesh):
    split = P("samp", "blk", None)
    classes = P(("samp", "blk"), None)
    return jax.shard_map(
        per_device,
        mesh=mesh,
        in_specs=(split, P("samp"), *([P()] * 12), split, classes),
        out_specs=(split, classes, split, *([P()] * 12)),
        check_vma=False,
    )
```

time: 259 us -> 300 us (1.16); the launches traced: 255 us -> 300 us
  Pallas kernels: 155 us -> 188 us
  between operations: 1.59 us -> 14.8 us
  starting transfers between devices: 52.7 us -> 42.6 us
  local copies, waits for them, and re-layouts: 19.5 us -> 28.4 us
    pallas_call x7, Pallas kernels: 137 us -> 172 us  [big_call(): pl.pallas_call(body, grid_spec=pltpu.PrefetchScalarGridSpec(num_scalar_pr...]
    ppermute x30 -> x24, starting transfers between devices: 51.1 us -> 41 us  [shifted(): return lax.ppermute(value, axis, pairs)]
    unnamed x99 -> x103, local copies, waits for them, and re-layouts: 12.2 us -> 18.2 us
    ppermute x30 -> x24, waiting for transfers between devices: 24.7 us -> 22 us  [shifted(): return lax.ppermute(value, axis, pairs)]
    pallas_call x15 -> x13, Pallas kernels: 17.7 us -> 16 us  [small_call(): pl.pallas_call(body, in_specs=[pl.BlockSpec(memory_space=pltpu.SMEM), *[v...]
  transfers between devices with their start and end apart: 39 -> 33, of which waited for: 12 -> 16; matrix products, arithmetic and copies ran while one was open for 3% -> 4% of each run, Pallas kernels for 40% -> 47%
where the time goes in v2:
time: 300 us
  Pallas kernels  188 us (63%)
  starting transfers between devices  42.6 us (14%)
  local copies, waits for them, and re-layouts  28.4 us (9%)
  waiting for transfers between devices  25.4 us (8%)
  between operations  14.8 us (5%)
    pallas_call x7, Pallas kernels, big_call(): pl.pallas_call(body, grid_spec=pltpu.PrefetchScalarGridSpec(num_scalar_pr...  172 us
    ppermute x24, starting transfers between devices, shifted(): return lax.ppermute(value, axis, pairs)  41 us
    ppermute x24, waiting for transfers between devices, shifted(): return lax.ppermute(value, axis, pairs)  22 us
    unnamed x103, local copies, waits for them, and re-layouts  18.2 us
    pallas_call x13, Pallas kernels, small_call(): pl.pallas_call(body, in_specs=[pl.BlockSpec(memory_space=pltpu.SMEM), *[v...  16 us
  transfers between devices with their start and end apart: 33, of which 16 were waited for; matrix products, arithmetic and copies ran while one was open for 4% of the time, Pallas kernels for 47%

profile of v2, /device:TPU:0, one launch (start us, length us, event | category | flops | bytes accessed | tf_op | source)
XLA Modules:
  0.0 299.8 jit_solution(4495213784735369877)
XLA Ops:
  7.3 2.3 constant_dynamic-slice_fusion.1
  13.8 2.2 copy.33
  18.1 13.3 %project.1 = (bf16[3,800,384]{2,1,0:T(8,128)(2,1)}, bf16[3,1152,800]{2,1,0:T(8,128)(2,1)}, f32[8,384]{1,0:T(8,128)}, f32[8,384]{1,0:T(8,128)}) custom-call(s32[35]{0:T(128)} %fusion.refs_0_, s32[6]{0:T(128)} %refs_1_.11, bf16[6,400,384]{2,1,0:T(8,128)(2,1)} %refs_6_.3, bf16[3,400,384]{2,1,0:T(8,128)(2,1)} %copy-done.33, bf16[1152,384]{1,0:T(8,128)(2,1)} %bitcast.3, ...), custom_call_target="tpu_custom_call" | custom-call | tf_op jit(solution)/shard_map/project/pallas_call | solution.py:677
  31.4 3.9 %collective-permute-start.4 = (f32[8,384]{1,0:T(8,128)}, f32[8,384]{1,0:T(8,128)S(1)}, u32[]{:S(2)}, u32[]{:S(2)}) collective-permute-start(f32[8,384]{1,0:T(8,128)} %get-tuple-element.74.refs_1_), channel_id=1, source_target_pairs={{0,6},{2,0},{4,2},{6,4},{8,14},{10,8},{12,10},{14,12},{16,22},{18,... | collective-permute-start | bytes 36872 | tf_op jit(solution)/shard_map/ppermute | solution.py:430
  36.4 23.0 %attention.1 = (f32[3,8,800]{2,1,0:T(8,128)}, f32[3,8,800]{2,1,0:T(8,128)}, s32[3]{0:T(128)}, bf16[3,384,800]{2,1,0:T(8,128)(2,1)}) custom-call(s32[35]{0:T(128)} %fusion.refs_0_, s32[6]{0:T(128)} %refs_1_.11, bf16[3,1152,800]{2,1,0:T(8,128)(2,1)} %get-tuple-element.70.refs_2_.refs_3_), custom_call_target="tpu_custom_call" | custom-call | tf_op jit(solution)/shard_map/attention/pallas_call | solution.py:677
  60.9 2.9 collective-permute-start.7
  72.2 40.2 %layer.1 = (bf16[6,400,384]{2,1,0:T(8,128)(2,1)}, bf16[3,400,384]{2,1,0:T(8,128)(2,1)}, bf16[3,800,384]{2,1,0:T(8,128)(2,1)}, bf16[3,384,800]{2,1,0:T(8,128)(2,1...) custom-call(s32[35]{0:T(128)} %fusion.refs_0_, ...), custom_call_target="tpu_custom_call" | custom-call | tf_op jit(solution)/shard_map/layer/pallas_call | solution.py:677
  112.9 24.5 %attention_back.3 = (bf16[1,1152,800]{2,1,0:T(8,128)(2,1)}, bf16[1152,384]{1,0:T(8,128)(2,1)}, f32[8,1152]{1,0:T(8,128)}) custom-call(s32[35]{0:T(128)} %fusion.refs_0_, s32[6]{0:T(128)} %refs_1_.11, s32[3]{0:T(128)} %get-tuple-element.78.refs_2_, bf16[3,1152,800]{2,1,0:T(8,128)(2,1)} %get-tuple-element.70.refs_2_.refs_3_, ...), custom_call_target="tpu_custom_call" | custom-call | tf_op jit(solution)/shard_map/attention_back/pallas_call | solution.py:677
  140.1 3.9 %collective-permute-start.11 = (bf16[384,384]{1,0:T(8,128)(2,1)S(1)}, bf16[384,384]{1,0:T(8,128)(2,1)S(1)}, u32[]{:S(2)}, u32[]{:S(2)}) collective-permute-start(bf16[384,384]{1,0:T(8,128)(2,1)S(1)} %get-tuple-element.89), channel_id=1, source_target_pairs={{0,2},{2,4},{4,6},{6,0},{8,10},{10,12},{12,14},{14,8},{16,18},{18,... | collective-permute-start | bytes 884744 | tf_op jit(solution)/shard_map/ppermute | solution.py:430
  148.1 29.2 %attention_back.4 = (bf16[1,1152,800]{2,1,0:T(8,128)(2,1)}, bf16[1152,384]{1,0:T(8,128)(2,1)}, f32[8,1152]{1,0:T(8,128)}) custom-call(s32[35]{0:T(128)} %fusion.refs_0_, s32[6]{0:T(128)} %refs_1_.11, s32[3]{0:T(128)} %get-tuple-element.78.refs_2_, bf16[3,1152,800]{2,1,0:T(8,128)(2,1)} %get-tuple-element.70.refs_2_.refs_3_, ...), custom_call_target="tpu_custom_call" | custom-call | tf_op jit(solution)/shard_map/attention_back/pallas_call | solution.py:677
  179.6 3.8 %collective-permute-start.16 = (bf16[96,384]{1,0:T(8,128)(2,1)S(1)}, bf16[96,384]{1,0:T(8,128)(2,1)S(1)}, u32[]{:S(2)}, u32[]{:S(2)}) collective-permute-start(bf16[96,384]{1,0:T(8,128)(2,1)S(1)} %get-tuple-element.104), channel_id=1, source_target_pairs={{0,24},{2,26},{4,28},{6,30},{8,0},{10,2},{12,4},{14,6},{16,8},{18,... | collective-permute-start | bytes 221192 | tf_op jit(solution)/shard_map/ppermute | solution.py:430
  183.4 31.7 %attention_back.5 = (bf16[1,1152,800]{2,1,0:T(8,128)(2,1)}, bf16[1152,384]{1,0:T(8,128)(2,1)}, f32[8,1152]{1,0:T(8,128)}) custom-call(s32[35]{0:T(128)} %fusion.refs_0_, s32[6]{0:T(128)} %refs_1_.11, s32[3]{0:T(128)} %get-tuple-element.78.refs_2_, bf16[3,1152,800]{2,1,0:T(8,128)(2,1)} %get-tuple-element.70.refs_2_.refs_3_, ...), custom_call_target="tpu_custom_call" | custom-call | tf_op jit(solution)/shard_map/attention_back/pallas_call | solution.py:677
  224.2 10.2 %tokens_back.1 = (bf16[6,400,384]{2,1,0:T(8,128)(2,1)}, bf16[3,400,384]{2,1,0:T(8,128)(2,1)}) custom-call(s32[35]{0:T(128)} %fusion.refs_0_, bf16[1,1152,800]{2,1,0:T(8,128)(2,1)} %get-tuple-element.83.refs_1_, bf16[1,1152,800]{2,1,0:T(8,128)(2,1)} %get-tuple-element.88.refs_2_, bf16[1,1152,800]{2,1,0:T(8,128)(2,1)} %get-tuple-element.94.refs_3_, ...), custom_call_target="tpu_custom_call" | custom-call | tf_op jit(solution)/shard_map/tokens_back/pallas_call | solution.py:677
  236.1 2.9 collective-permute-start.21
  239.0 3.5 %collective-permute-done.19.refs_2_ = bf16[208,384]{1,0:T(8,128)(2,1)S(1)} collective-permute-done((bf16[208,384]{1,0:T(8,128)(2,1)S(1)}, bf16[208,384]{1,0:T(8,128)(2,1)S(1)}, u32[]{:S(2)}, u32[]{:S(2)}) %collective-permute-start.19) | collective-permute-done | bytes 159776 | tf_op jit(solution)/shard_map/ppermute | solution.py:430
  247.2 3.1 %collective-permute-start.22 = (bf16[64,384]{1,0:T(8,128)(2,1)S(1)}, bf16[64,384]{1,0:T(8,128)(2,1)S(1)}, u32[]{:S(2)}, u32[]{:S(2)}) collective-permute-start(bf16[64,384]{1,0:T(8,128)(2,1)S(1)} %get-tuple-element.114), channel_id=1, source_target_pairs={{0,8},{2,10},{4,12},{6,14},{8,16},{10,18},{12,20},{14,22},{16,24},... | collective-permute-start | bytes 147464 | tf_op jit(solution)/shard_map/ppermute | solution.py:430
  250.3 3.1 %collective-permute-start.23 = (bf16[64,384]{1,0:T(8,128)(2,1)S(1)}, bf16[64,384]{1,0:T(8,128)(2,1)S(1)}, u32[]{:S(2)}, u32[]{:S(2)}) collective-permute-start(bf16[64,384]{1,0:T(8,128)(2,1)S(1)} %get-tuple-element.115), channel_id=1, source_target_pairs={{0,16},{2,18},{4,20},{6,22},{8,24},{10,26},{12,28},{14,30},{16,0},... | collective-permute-start | bytes 147464 | tf_op jit(solution)/shard_map/ppermute | solution.py:430
  253.4 2.8 collective-permute-start.24
  258.6 4.2 %collective-permute-start.27 = (bf16[48,384]{1,0:T(8,128)(2,1)S(1)}, bf16[48,384]{1,0:T(8,128)(2,1)S(1)}, u32[]{:S(2)}, u32[]{:S(2)}) collective-permute-start(bf16[48,384]{1,0:T(8,128)(2,1)S(1)} %get-tuple-element.117.refs_1_), channel_id=1, source_target_pairs={{0,24},{2,26},{4,28},{6,30},{8,0},{10,2},{12,4},{14,6},{16,8},{18,... | collective-permute-start | bytes 110600 | tf_op jit(solution)/shard_map/ppermute | solution.py:430
  264.5 3.6 %collective-permute-done.26.refs_3_ = bf16[48,384]{1,0:T(8,128)(2,1)S(1)} collective-permute-done((bf16[48,384]{1,0:T(8,128)(2,1)S(1)}, bf16[48,384]{1,0:T(8,128)(2,1)S(1)}, u32[]{:S(2)}, u32[]{:S(2)}) %collective-permute-start.26) | collective-permute-done | bytes 36896 | tf_op jit(solution)/shard_map/ppermute | solution.py:430
  270.8 2.5 collective-permute-start.30
  276.0 2.4 collective-permute-done.29.refs_3_
  282.7 3.1 %finish.1 = (f32[384,1152]{1,0:T(8,128)}, f32[384,384]{1,0:T(8,128)}, f32[8,384]{1,0:T(8,128)S(1)}) custom-call(s32[35]{0:T(128)S(1)} %copy-done.22, bf16[768,384]{1,0:T(8,128)(2,1)S(1)} %collect.3.refs_1_.refs_5_, bf16[768,384]{1,0:T(8,128)(2,1)S(1)} %collective-permute-done.31.refs_2_, f32[16,384]{1,0:T(8,128)S(1)} %get-tuple-element.118.refs_3_.refs_2_, ...), custom_call_target="tpu_custom_call" | custom-call | tf_op jit(solution)/shard_map/finish/pallas_call | solution.py:442
  288.1 4.0 %finish_mlp.1 = (f32[1536,384]{1,0:T(8,128)}, f32[384,1536]{1,0:T(8,128)}, f32[8,384]{1,0:T(8,128)S(1)}) custom-call(s32[32]{0:T(128)S(1)} %copy-done.32, bf16[3072,384]{1,0:T(8,128)(2,1)S(1)} %copy-done.2, f32[16,384]{1,0:T(8,128)S(1)} %get-tuple-element.118.refs_3_.refs_2_, f32[16,384]{1,0:T(8,128)S(1)} %copy-done.11, bf16[384,1536]{1,0:T(8,128)(2,1)S(1)} %copy-done.1, ...), custom_call_target="tpu_custom_call" | custom-call | tf_op jit(solution)/shard_map/finish_mlp/pallas_call | solution.py:442
  (181 shorter events, 58.5 us)
Async XLA Ops:
  7.2 279.3 %all-gather.2.cloned.1.call-start = ((), (), s32[]{:S(2)}) async-start(), calls=%async_computation | async-start | bytes 2433024 | tf_op jit(solution)/shard_map/all_gather | solution.py:825
  9.6 7.6 %collective-permute-start = (bf16[3,400,384]{2,1,0:T(8,128)(2,1)}, bf16[3,400,384]{2,1,0:T(8,128)(2,1)S(1)}, u32[]{:S(2)}, u32[]{:S(2)}) collective-permute-start(bf16[3,400,384]{2,1,0:T(8,128)(2,1)} %constant_dynamic-slice_fusion.1), channel_id=1, source_target_pairs={{0,1},{1,0},{2,3},{3,2},{4,5},{5,4},{6,7},{7,6},{8,9},{9,8},{10,11... | collective-permute-start | bytes 2764808 | tf_op jit(solution)/shard_map/ppermute | solution.py:409
  11.1 59.3 %collective-permute-start.1 = (bf16[3,400,384]{2,1,0:T(8,128)(2,1)}, bf16[3,400,384]{2,1,0:T(8,128)(2,1)S(1)}, u32[]{:S(2)}, u32[]{:S(2)}) collective-permute-start(bf16[3,400,384]{2,1,0:T(8,128)(2,1)} %constant_dynamic-slice_fusion), channel_id=1, source_target_pairs={{0,1},{1,0},{2,3},{3,2},{4,5},{5,4},{6,7},{7,6},{8,9},{9,8},{10,11... | collective-permute-start | bytes 2764808 | tf_op jit(solution)/shard_map/ppermute | solution.py:409
  31.4 28.0 %collective-permute-start.4 = (f32[8,384]{1,0:T(8,128)}, f32[8,384]{1,0:T(8,128)S(1)}, u32[]{:S(2)}, u32[]{:S(2)}) collective-permute-start(f32[8,384]{1,0:T(8,128)} %get-tuple-element.74.refs_1_), channel_id=1, source_target_pairs={{0,6},{2,0},{4,2},{6,4},{8,14},{10,8},{12,10},{14,12},{16,22},{18,... | collective-permute-start | bytes 36872 | tf_op jit(solution)/shard_map/ppermute | solution.py:430
  35.3 24.1 %collective-permute-start.3 = (f32[8,384]{1,0:T(8,128)}, f32[8,384]{1,0:T(8,128)S(1)}, u32[]{:S(2)}, u32[]{:S(2)}) collective-permute-start(f32[8,384]{1,0:T(8,128)} %get-tuple-element.74.refs_1_), channel_id=1, source_target_pairs={{0,4},{2,6},{4,0},{6,2},{8,12},{10,14},{12,8},{14,10},{16,20},{18,... | collective-permute-start | bytes 36872 | tf_op jit(solution)/shard_map/ppermute | solution.py:430
  35.8 23.6 %collective-permute-start.2 = (f32[8,384]{1,0:T(8,128)}, f32[8,384]{1,0:T(8,128)S(1)}, u32[]{:S(2)}, u32[]{:S(2)}) collective-permute-start(f32[8,384]{1,0:T(8,128)} %get-tuple-element.74.refs_1_), channel_id=1, source_target_pairs={{0,2},{2,4},{4,6},{6,0},{8,10},{10,12},{12,14},{14,8},{16,18},{18,... | collective-permute-start | bytes 36872 | tf_op jit(solution)/shard_map/ppermute | solution.py:430
  64.3 5.5 %collective-permute-start.5 = (f32[8,384]{1,0:T(8,128)S(1)}, f32[8,384]{1,0:T(8,128)S(1)}, u32[]{:S(2)}, u32[]{:S(2)}) collective-permute-start(f32[8,384]{1,0:T(8,128)S(1)} %add.26.refs_1_.refs_5_), channel_id=1, source_target_pairs={{0,8},{2,10},{4,12},{6,14},{8,16},{10,18},{12,20},{14,22},{16,24},... | collective-permute-start | bytes 36872 | tf_op jit(solution)/shard_map/ppermute | solution.py:430
  112.4 25.1 %collective-permute-start.10 = (bf16[1536,384]{1,0:T(8,128)(2,1)}, bf16[1536,384]{1,0:T(8,128)(2,1)S(1)}, u32[]{:S(2)}, u32[]{:S(2)}) collective-permute-start(bf16[1536,384]{1,0:T(8,128)(2,1)} %get-tuple-element.85), channel_id=1, source_target_pairs={{0,1},{1,0},{2,3},{3,2},{4,5},{5,4},{6,7},{7,6},{8,9},{9,8},{10,11... | collective-permute-start | bytes 3538952 | tf_op jit(solution)/shard_map/ppermute | solution.py:409
  112.6 32.9 %collective-permute-start.9 = (bf16[3,400,384]{2,1,0:T(8,128)(2,1)}, bf16[3,400,384]{2,1,0:T(8,128)(2,1)}, u32[]{:S(2)}, u32[]{:S(2)}) collective-permute-start(bf16[3,400,384]{2,1,0:T(8,128)(2,1)} %get-tuple-element.76), channel_id=1, source_target_pairs={{0,1},{1,0},{2,3},{3,2},{4,5},{5,4},{6,7},{7,6},{8,9},{9,8},{10,11... | collective-permute-start | bytes 2764808 | tf_op jit(solution)/shard_map/ppermute | solution.py:409
  140.1 37.2 %collective-permute-start.11 = (bf16[384,384]{1,0:T(8,128)(2,1)S(1)}, bf16[384,384]{1,0:T(8,128)(2,1)S(1)}, u32[]{:S(2)}, u32[]{:S(2)}) collective-permute-start(bf16[384,384]{1,0:T(8,128)(2,1)S(1)} %get-tuple-element.89), channel_id=1, source_target_pairs={{0,2},{2,4},{4,6},{6,0},{8,10},{10,12},{12,14},{14,8},{16,18},{18,... | collective-permute-start | bytes 884744 | tf_op jit(solution)/shard_map/ppermute | solution.py:430
  144.1 33.2 %collective-permute-start.12 = (bf16[384,384]{1,0:T(8,128)(2,1)S(1)}, bf16[384,384]{1,0:T(8,128)(2,1)S(1)}, u32[]{:S(2)}, u32[]{:S(2)}) collective-permute-start(bf16[384,384]{1,0:T(8,128)(2,1)S(1)} %get-tuple-element.90), channel_id=1, source_target_pairs={{0,4},{2,6},{4,0},{6,2},{8,12},{10,14},{12,8},{14,10},{16,20},{18,... | collective-permute-start | bytes 884744 | tf_op jit(solution)/shard_map/ppermute | solution.py:430
  144.1 33.2 %collective-permute-start.13 = (bf16[384,384]{1,0:T(8,128)(2,1)S(1)}, bf16[384,384]{1,0:T(8,128)(2,1)S(1)}, u32[]{:S(2)}, u32[]{:S(2)}) collective-permute-start(bf16[384,384]{1,0:T(8,128)(2,1)S(1)} %get-tuple-element.91), channel_id=1, source_target_pairs={{0,6},{2,0},{4,2},{6,4},{8,14},{10,8},{12,10},{14,12},{16,22},{18,... | collective-permute-start | bytes 884744 | tf_op jit(solution)/shard_map/ppermute | solution.py:430
  179.6 35.6 %collective-permute-start.14 = (bf16[96,384]{1,0:T(8,128)(2,1)S(1)}, bf16[96,384]{1,0:T(8,128)(2,1)S(1)}, u32[]{:S(2)}, u32[]{:S(2)}) collective-permute-start(bf16[96,384]{1,0:T(8,128)(2,1)S(1)} %get-tuple-element.102), channel_id=1, source_target_pairs={{0,8},{2,10},{4,12},{6,14},{8,16},{10,18},{12,20},{14,22},{16,24},... | collective-permute-start | bytes 221192 | tf_op jit(solution)/shard_map/ppermute | solution.py:430
  179.6 35.6 %collective-permute-start.15 = (bf16[96,384]{1,0:T(8,128)(2,1)S(1)}, bf16[96,384]{1,0:T(8,128)(2,1)S(1)}, u32[]{:S(2)}, u32[]{:S(2)}) collective-permute-start(bf16[96,384]{1,0:T(8,128)(2,1)S(1)} %get-tuple-element.103), channel_id=1, source_target_pairs={{0,16},{2,18},{4,20},{6,22},{8,24},{10,26},{12,28},{14,30},{16,0},... | collective-permute-start | bytes 221192 | tf_op jit(solution)/shard_map/ppermute | solution.py:430
  179.6 35.6 %collective-permute-start.16 = (bf16[96,384]{1,0:T(8,128)(2,1)S(1)}, bf16[96,384]{1,0:T(8,128)(2,1)S(1)}, u32[]{:S(2)}, u32[]{:S(2)}) collective-permute-start(bf16[96,384]{1,0:T(8,128)(2,1)S(1)} %get-tuple-element.104), channel_id=1, source_target_pairs={{0,24},{2,26},{4,28},{6,30},{8,0},{10,2},{12,4},{14,6},{16,8},{18,... | collective-permute-start | bytes 221192 | tf_op jit(solution)/shard_map/ppermute | solution.py:430
  234.4 29.1 %collective-permute-start.18 = (bf16[3,400,384]{2,1,0:T(8,128)(2,1)}, bf16[3,400,384]{2,1,0:T(8,128)(2,1)S(1)}, u32[]{:S(2)}, u32[]{:S(2)}) collective-permute-start(bf16[3,400,384]{2,1,0:T(8,128)(2,1)} %get-tuple-element.109.refs_5_), channel_id=1, source_target_pairs={{0,1},{1,0},{2,3},{3,2},{4,5},{5,4},{6,7},{7,6},{8,9},{9,8},{10,11... | collective-permute-start | bytes 2764808 | tf_op jit(solution)/shard_map/ppermute | solution.py:409
  234.6 7.9 %collective-permute-start.19 = (bf16[208,384]{1,0:T(8,128)(2,1)S(1)}, bf16[208,384]{1,0:T(8,128)(2,1)S(1)}, u32[]{:S(2)}, u32[]{:S(2)}) collective-permute-start(bf16[208,384]{1,0:T(8,128)(2,1)S(1)} %get-tuple-element.110), channel_id=1, source_target_pairs={{0,2},{2,4},{4,6},{6,0},{8,10},{10,12},{12,14},{14,8},{16,18},{18,... | collective-permute-start | bytes 479240 | tf_op jit(solution)/shard_map/ppermute | solution.py:430
  234.6 9.8 %collective-permute-start.20 = (bf16[208,384]{1,0:T(8,128)(2,1)S(1)}, bf16[208,384]{1,0:T(8,128)(2,1)S(1)}, u32[]{:S(2)}, u32[]{:S(2)}) collective-permute-start(bf16[208,384]{1,0:T(8,128)(2,1)S(1)} %get-tuple-element.111), channel_id=1, source_target_pairs={{0,4},{2,6},{4,0},{6,2},{8,12},{10,14},{12,8},{14,10},{16,20},{18,... | collective-permute-start | bytes 479240 | tf_op jit(solution)/shard_map/ppermute | solution.py:430
  236.1 9.3 %collective-permute-start.21 = (bf16[208,384]{1,0:T(8,128)(2,1)S(1)}, bf16[208,384]{1,0:T(8,128)(2,1)S(1)}, u32[]{:S(2)}, u32[]{:S(2)}) collective-permute-start(bf16[208,384]{1,0:T(8,128)(2,1)S(1)} %get-tuple-element.112), channel_id=1, source_target_pairs={{0,6},{2,0},{4,2},{6,4},{8,14},{10,8},{12,10},{14,12},{16,22},{18,... | collective-permute-start | bytes 479240 | tf_op jit(solution)/shard_map/ppermute | solution.py:430
  247.2 9.1 %collective-permute-start.22 = (bf16[64,384]{1,0:T(8,128)(2,1)S(1)}, bf16[64,384]{1,0:T(8,128)(2,1)S(1)}, u32[]{:S(2)}, u32[]{:S(2)}) collective-permute-start(bf16[64,384]{1,0:T(8,128)(2,1)S(1)} %get-tuple-element.114), channel_id=1, source_target_pairs={{0,8},{2,10},{4,12},{6,14},{8,16},{10,18},{12,20},{14,22},{16,24},... | collective-permute-start | bytes 147464 | tf_op jit(solution)/shard_map/ppermute | solution.py:430
  250.3 7.0 %collective-permute-start.23 = (bf16[64,384]{1,0:T(8,128)(2,1)S(1)}, bf16[64,384]{1,0:T(8,128)(2,1)S(1)}, u32[]{:S(2)}, u32[]{:S(2)}) collective-permute-start(bf16[64,384]{1,0:T(8,128)(2,1)S(1)} %get-tuple-element.115), channel_id=1, source_target_pairs={{0,16},{2,18},{4,20},{6,22},{8,24},{10,26},{12,28},{14,30},{16,0},... | collective-permute-start | bytes 147464 | tf_op jit(solution)/shard_map/ppermute | solution.py:430
  258.6 5.9 %collective-permute-start.27 = (bf16[48,384]{1,0:T(8,128)(2,1)S(1)}, bf16[48,384]{1,0:T(8,128)(2,1)S(1)}, u32[]{:S(2)}, u32[]{:S(2)}) collective-permute-start(bf16[48,384]{1,0:T(8,128)(2,1)S(1)} %get-tuple-element.117.refs_1_), channel_id=1, source_target_pairs={{0,24},{2,26},{4,28},{6,30},{8,0},{10,2},{12,4},{14,6},{16,8},{18,... | collective-permute-start | bytes 110600 | tf_op jit(solution)/shard_map/ppermute | solution.py:430
  262.8 5.9 %collective-permute-start.25 = (bf16[48,384]{1,0:T(8,128)(2,1)S(1)}, bf16[48,384]{1,0:T(8,128)(2,1)S(1)}, u32[]{:S(2)}, u32[]{:S(2)}) collective-permute-start(bf16[48,384]{1,0:T(8,128)(2,1)S(1)} %get-tuple-element.117.refs_1_), channel_id=1, source_target_pairs={{0,8},{2,10},{4,12},{6,14},{8,16},{10,18},{12,20},{14,22},{16,24},... | collective-permute-start | bytes 110600 | tf_op jit(solution)/shard_map/ppermute | solution.py:430
  274.0 6.1 %collective-permute-start.28 = (bf16[192,384]{1,0:T(8,128)(2,1)S(1)}, bf16[192,384]{1,0:T(8,128)(2,1)S(1)}, u32[]{:S(2)}, u32[]{:S(2)}) collective-permute-start(bf16[192,384]{1,0:T(8,128)(2,1)S(1)} %collect.2.refs_1_), channel_id=1, source_target_pairs={{0,2},{2,4},{4,6},{6,0},{8,10},{10,12},{12,14},{14,8},{16,18},{18,... | collective-permute-start | bytes 442376 | tf_op jit(solution)/shard_map/ppermute | solution.py:430
  (56 other events, 631.0 us)
Sparse Core Ops, SparseCore 0:
  217.3 60.5 all-gather.1

commit v3 on v2

--- a/solution.py
+++ b/solution.py
@@ -74,10 +74,15 @@
 
 
 def project_kernel(
-    blk_ref, views_ref, own_ref, far_ref, w_ref, pack_ref, w_out_ref, w1_ref, w2_ref, cot_ref,
-    hat_ref, qkv_ref, cls_ref, stat_ref, mix_ref, first_ref, full_ref,
+    blk_ref, views_ref, own_ref, far_ref, w_in_ref, pack_ref, w_out_ref, w1_ref, w2_ref, cot_ref,
+    hat_ref, qkv_ref, cls_ref, stat_ref, w_ref, mix_ref, first_ref, full_ref,
 ):
     step = pl.program_id(0)
+
+    @pl.when(step == 0)
+    def _():
+        w_ref[...] = w_in_ref[...].T
+
     rows = hat_ref.shape[1]
     width = own_ref.shape[2]
     place_halves(full_ref, blk_ref[0], own_ref[0], far_ref[0])
@@ -148,8 +153,8 @@
 
     def store(h, mixed):
         total = mixed[HEAD_DIM : HEAD_DIM + 1]
-        sum_ref[0, h : h + 1, :] = total
-        att_ref[0, h * HEAD_DIM : (h + 1) * HEAD_DIM, :] = (mixed[:HEAD_DIM] * (1.0 / total)).astype(BF)
+        sum_ref[0, pl.ds(h, 1), :] = total
+        att_ref[0, head_rows(h, 0), :] = (mixed[:HEAD_DIM] * (1.0 / total)).astype(BF)
 
     sum_ref[0, heads:8, :] = jnp.ones((8 - heads, rows), F32)
     for count, keys in key_counts(rows):
@@ -157,15 +162,22 @@
         @pl.when(views == count)
         def _(keys=keys):
             main = keys - 16
-            for h in range(heads):
-                query, key, value = head_parts(qkv_ref, h, width, keys)
-                slot = h % pow_ref.shape[0]
-                scores = dot(key, query, 0, 0)
-                pow_ref[slot, :main, :] = jnp.exp2(scores[:main]).astype(BF)
-                tail = masked_tail(scores[main:], main, limit)
-                pow_ref[slot, main:keys, :] = jnp.exp2(tail).astype(BF)
-                left = jnp.concatenate((value, ones[:, :keys]), 0)
-                store(h, dot(left, pow_ref[slot, :keys, :], 1, 0))
+
+            def pair(p, carry):
+                both = range(2)
+                parts = [head_parts(qkv_ref, 2 * p + k, width, keys) for k in both]
+                scores = [dot(key, query, 0, 0) for query, key, _ in parts]
+                for k in both:
+                    pow_ref[k, :main, :] = jnp.exp2(scores[k][:main]).astype(BF)
+                    tail = masked_tail(scores[k][main:], main, limit)
+                    pow_ref[k, main:keys, :] = jnp.exp2(tail).astype(BF)
+                lefts = [jnp.concatenate((value, ones[:, :keys]), 0) for _, _, value in parts]
+                mixed = [dot(lefts[k], pow_ref[k, :keys, :], 1, 0) for k in both]
+                for k in both:
+                    store(2 * p + k, mixed[k])
+                return carry
+
+            lax.fori_loop(0, heads // 2, pair, 0)
 
     totals = sum_ref[0]
     plain = (jnp.min(totals) > SUM_LOW) & (jnp.max(totals) < SUM_HIGH)
@@ -173,20 +185,39 @@
 
     @pl.when(jnp.logical_not(plain))
     def _():
-        for h in range(heads):
+        @each_head(heads)
+        def _(h, slot):
             query, key, value = head_parts(qkv_ref, h, width, rows)
-            slot = h % pow_ref.shape[0]
             scores = masked_tail(dot(key, query, 0, 0), 0, limit)
             top = jnp.max(scores, 0, keepdims=True)
-            top_ref[0, h : h + 1, :] = top
+            top_ref[0, pl.ds(h, 1), :] = top
             pow_ref[slot] = jnp.exp2(scores - top).astype(BF)
             left = jnp.concatenate((value, ones), 0)
             store(h, dot(left, pow_ref[slot], 1, 0))
 
 
+def each_head(heads):
+    def run(body):
+        def pair(p, carry):
+            for slot in range(2):
+                body(2 * p + slot, slot)
+            return carry
+
+        lax.fori_loop(0, heads // 2, pair, 0)
+
+    return run
+
+
+def head_rows(h, base):
+    return pl.ds(pl.multiple_of(base + h * HEAD_DIM, HEAD_DIM), HEAD_DIM)
+
+
 def head_parts(qkv_ref, h, width, keys):
-    part = lambda t: slice(t * width + h * HEAD_DIM, t * width + (h + 1) * HEAD_DIM)
-    return qkv_ref[0, part(0), :], qkv_ref[0, part(1), :keys], qkv_ref[0, part(2), :keys]
+    return (
+        qkv_ref[0, head_rows(h, 0), :],
+        qkv_ref[0, head_rows(h, width), :keys],
+        qkv_ref[0, head_rows(h, 2 * width), :keys],
+    )
 
 
 def layer_kernel(
@@ -282,58 +313,66 @@
     core_ref, views_ref, plain_ref, qkv_ref, top_ref, dmix_ref, inner_ref, hat_ref,
     dqkv_ref, grad_ref, sums_ref, pow_ref, *, sample, samples
 ):
+    pair = pl.program_id(0)
     rows, width = hat_ref.shape[1:]
-    heads = width // HEAD_DIM
     views = views_ref[core_ref[CORE] * samples + sample]
     limit = 1 + VIEW_ROWS * views
     plain = plain_ref[sample] == 1
-
-    def back(h, parts, slot, keys):
-        query, key, value = parts
-        place = lambda t: slice(t * width + h * HEAD_DIM, t * width + (h + 1) * HEAD_DIM)
-        d_mix = dmix_ref[0, place(0), :]
-        powers = pow_ref[slot, :keys, :]
-        d_weights = dot(value, d_mix, 0, 0)
-        inner = inner_ref[0, h : h + 1, :]
-        d_scores = (powers.astype(F32) * (d_weights - inner)).astype(BF)
-        d_query = dot(key, d_scores, 1, 0) * SCALE
-        d_key = dot(query, d_scores, 1, 1) * LN2
-        d_value = dot(d_mix, powers, 1, 1)
-        dqkv_ref[0, place(0), :] = d_query.astype(BF)
-        dqkv_ref[0, place(1), :keys] = d_key.astype(BF)
-        dqkv_ref[0, place(2), :keys] = d_value.astype(BF)
+    both = range(2)
+    lanes = [slice(k * HEAD_DIM, (k + 1) * HEAD_DIM) for k in both]
+
+    def back(keys, powers_of):
+        query = [qkv_ref[0, 0, part, :] for part in lanes]
+        key = [qkv_ref[0, 1, part, :keys] for part in lanes]
+        value = [qkv_ref[0, 2, part, :keys] for part in lanes]
+        d_mix = [dmix_ref[0, part, :] for part in lanes]
+        scores = [dot(key[k], query[k], 0, 0) for k in both]
+        for k in both:
+            powers_of(k, scores[k])
+        d_weights = [dot(value[k], d_mix[k], 0, 0) for k in both]
+        d_scores = []
+        for k in both:
+            inner = inner_ref[0, pl.ds(2 * pair + k, 1), :]
+            powers = pow_ref[k, :keys, :].astype(F32)
+            d_scores.append((powers * (d_weights[k] - inner)).astype(BF))
+        for k in both:
+            d_value = dot(d_mix[k], pow_ref[k, :keys, :], 1, 1)
+            dqkv_ref[0, 2, lanes[k], :keys] = d_value.astype(BF)
+        for k in both:
+            d_query = dot(key[k], d_scores[k], 1, 0) * SCALE
+            dqkv_ref[0, 0, lanes[k], :] = d_query.astype(BF)
+            d_key = dot(query[k], d_scores[k], 1, 1) * LN2
+            dqkv_ref[0, 1, lanes[k], :keys] = d_key.astype(BF)
         if keys < rows:
-            blank = jnp.zeros((HEAD_DIM, rows - keys), BF)
-            dqkv_ref[0, place(1), keys:] = blank
-            dqkv_ref[0, place(2), keys:] = blank
+            blank = jnp.zeros((2 * HEAD_DIM, rows - keys), BF)
+            dqkv_ref[0, 1, :, keys:] = blank
+            dqkv_ref[0, 2, :, keys:] = blank
 
     for count, keys in key_counts(rows):
 
         @pl.when((views == count) & plain)
         def _(keys=keys):
             main = keys - 16
-            for h in range(heads):
-                slot = h % pow_ref.shape[0]
-                parts = head_parts(qkv_ref, h, width, keys)
-                scores = dot(parts[1], parts[0], 0, 0)
-                pow_ref[slot, :main, :] = jnp.exp2(scores[:main]).astype(BF)
+
+            def powers_of(k, scores):
+                pow_ref[k, :main, :] = jnp.exp2(scores[:main]).astype(BF)
                 tail = masked_tail(scores[main:], main, limit)
-                pow_ref[slot, main:keys, :] = jnp.exp2(tail).astype(BF)
-                back(h, parts, slot, keys)
+                pow_ref[k, main:keys, :] = jnp.exp2(tail).astype(BF)
+
+            back(keys, powers_of)
 
     @pl.when(jnp.logical_not(plain))
     def _():
-        for h in range(heads):
-            slot = h % pow_ref.shape[0]
-            parts = head_parts(qkv_ref, h, width, rows)
-            scores = masked_tail(dot(parts[1], parts[0], 0, 0), 0, limit)
-            pow_ref[slot] = jnp.exp2(scores - top_ref[0, h : h + 1, :]).astype(BF)
-            back(h, parts, slot, rows)
+        def powers_of(k, scores):
+            top = top_ref[0, pl.ds(2 * pair + k, 1), :]
+            pow_ref[k] = jnp.exp2(masked_tail(scores, 0, limit) - top).astype(BF)
+
+        back(rows, powers_of)
 
     right = jnp.concatenate((hat_ref[0], jnp.ones((rows, 128), BF)), 1)
-    result = dot(dqkv_ref[0], right, 1, 0)
-    grad_ref[...] = result[:, :width].astype(BF)
-    sums_ref[...] = result[:, width:].T[:8]
+    result = dot(dqkv_ref[0].reshape(3 * 2 * HEAD_DIM, rows), right, 1, 0)
+    grad_ref[...] = result[:, :width].astype(BF).reshape(grad_ref.shape)
+    sums_ref[0] = result[:, width:].T[:8]
 
 
 def tokens_back_kernel(core_ref, *refs, sets):
@@ -398,11 +437,33 @@
     rows = lax.broadcasted_iota(jnp.int32, (8, width), 0)
     extra = jnp.zeros((8, width), F32)
     for t in range(used // width):
-        extra = jnp.where(rows == t, sums[0:1, t * width : (t + 1) * width], extra)
+        row = jnp.concatenate([sums[p, 0:1, t * 128 : (t + 1) * 128] for p in range(width // 128)], 1)
+        extra = jnp.where(rows == t, row, extra)
     vectors = jnp.concatenate((bias_ref[0:8, :], extra), 0).astype(BF)
     at = sum(parts) // 2
     kept_ref[at : at + EXTRA, :] = vectors
     sent_ref[at : at + EXTRA, :] = vectors
+
+
+def insert_rows(info, base, came):
+    count = came.shape[0]
+
+    def body(info_ref, came_ref, base_ref, out_ref, sem):
+        start = (1 - info_ref[CORE]) * count
+        copy = pltpu.make_async_copy(came_ref, out_ref.at[pl.ds(start, count)], sem)
+        copy.start()
+        copy.wait()
+
+    anywhere = pl.BlockSpec(memory_space=pl.ANY)
+    return pl.pallas_call(
+        body,
+        in_specs=[pl.BlockSpec(memory_space=pltpu.SMEM), anywhere, anywhere],
+        out_specs=anywhere,
+        out_shape=jax.ShapeDtypeStruct(base.shape, base.dtype),
+        scratch_shapes=[pltpu.SemaphoreType.DMA],
+        input_output_aliases={2: 0},
+        name="insert",
+    )(info, came, base)
 
 
 def swap_cores(value):
@@ -430,9 +491,11 @@
     return lax.ppermute(value, axis, pairs)
 
 
-def small_call(kernel, args, outs, scratch=(), ties=(), name=None):
+def small_call(kernel, args, outs, scratch=(), ties=(), name=None, through=()):
+    n, t, m, o = len(args), len(ties), len(through), len(outs)
+
     def body(*refs):
-        kernel(*refs[: len(args)], *refs[len(args) + len(ties) :])
+        kernel(*refs[:n], *refs[n + t + m : n + t + m + o], *refs[n + t + 2 * m + o :])
 
     vmem = pl.BlockSpec(memory_space=pltpu.VMEM)
     size = lambda a: math.prod(a.shape) * jnp.dtype(a.dtype).itemsize
@@ -444,14 +507,15 @@
         in_specs=[
             pl.BlockSpec(memory_space=pltpu.SMEM),
             *[vmem] * (len(args) - 1),
-            *[pl.BlockSpec(memory_space=pl.ANY)] * len(ties),
+            *[pl.BlockSpec(memory_space=pl.ANY)] * (t + m),
         ],
-        out_specs=[vmem] * len(outs),
-        out_shape=outs,
+        out_specs=[vmem] * o + [pl.BlockSpec(memory_space=pl.ANY)] * m,
+        out_shape=[*outs, *[jax.ShapeDtypeStruct(a.shape, a.dtype) for a in through]],
         scratch_shapes=list(scratch),
+        input_output_aliases={n + t + k: o + k for k in range(m)},
         compiler_params=pltpu.CompilerParams(vmem_limit_bytes=2 * total + 4 * 2**20),
         name=name,
-    )(*args, *ties)
+    )(*args, *ties, *through)
 
 
 def spread_kernel(info_ref, *refs, count, radix, slot, extra):
@@ -527,7 +591,7 @@
     def start(self, kept, sent):
         self.pending = [kept, swap_cores(sent)]
 
-    def scatter(self, level, ties=()):
+    def scatter(self, level, ties=(), through=()):
         last = level == self.rounds
         radix = 1 if last else self.layout.base[level][1]
         rows, width = self.pending[0].shape
@@ -542,8 +606,9 @@
             functools.partial(
                 spread_kernel, count=len(self.pending), radix=radix, slot=1 + level, extra=self.extra
             ),
-            (self.info, *self.pending), outs, [pltpu.VMEM((rows, width), BF)], ties, "spread",
+            (self.info, *self.pending), outs, [pltpu.VMEM((rows, width), BF)], ties, "spread", through,
         )
+        self.through = pieces[len(outs) :]
         if last:
             self.value = pieces[0]
             self.vectors = pieces[1] if self.extra else None
@@ -650,7 +715,6 @@
     far_tokens = swap_cores(lax.dynamic_slice_in_dim(tokens, theirs, local, 0))
     far_cot = swap_cores(lax.dynamic_slice_in_dim(cot_tokens, theirs, local, 0))
 
-    w_turned = w_qkv.T
     pack = jnp.concatenate(
         (
             norm1_gain, norm1_bias, norm2_gain, norm2_bias, out_bias, fc2_bias, qv_bias, fc1_bias,
@@ -688,18 +752,19 @@
             name=name,
         )(*prefetch, *args, *ties)
 
-    hat1, qkv, cls_rows, stats = big_call(
+    hat1, qkv, cls_rows, stats, w_turned = big_call(
         project_kernel,
         (info, view_count),
-        (tokens, far_tokens, w_turned, pack, w_out, w_fc1, w_fc2, cot_cls),
+        (tokens, far_tokens, w_qkv, pack, w_out, w_fc1, w_fc2, cot_cls),
         [half_spec(own_map), half_spec(by_sample), *[vmem] * 6],
         [
             sds((local, rows, width), BF),
             sds((local, 3 * width, rows), BF),
             sds((8, width), F32),
             sds((8, width), F32),
+            sds((3 * width, width), BF),
         ],
-        [rows_spec, pl.BlockSpec((1, 3 * width, rows), by_sample), vmem, vmem],
+        [rows_spec, pl.BlockSpec((1, 3 * width, rows), by_sample), vmem, vmem, vmem],
         [pltpu.VMEM((8, width), F32), pltpu.VMEM((8, width), F32), pltpu.VMEM((rows, width), BF)],
         name="project",
     )
@@ -710,7 +775,12 @@
             total = total + ref[...]
         refs[-1][...] = total
 
-    first, *later = stages(count)
+    *later, first = stages(count)
+
+    def add_all(values, ties=()):
+        return small_call(add_kernel, [info, *values], [sds((8, width), F32)], (), ties, "add")[0]
+
+    stats = add_all([stats, swap_cores(stats)])
     stat_parts = [stats] + [shifted(stats, first, k) for k in range(1, first[1])]
 
     qkv_spec = lambda f: pl.BlockSpec((1, 3 * width, rows), f)
@@ -727,15 +797,14 @@
         ],
         [eight_spec, eight_spec, pl.BlockSpec(memory_space=pltpu.SMEM), turned_spec],
         [pltpu.VMEM((2, rows, rows), BF)],
+        (stats,),
         name="attention",
     )
 
     tie = totals
-    for send in [functools.partial(lambda v, stage: [shifted(v, stage, k) for k in range(1, stage[1])], stage=stage) for stage in later] + [lambda v: [swap_cores(v)]]:
-        stats = small_call(
-            add_kernel, [info, *stat_parts], [sds((8, width), F32)], (), (tie,), "add"
-        )[0]
-        stat_parts = [stats] + send(stats)
+    for stage in later:
+        stats = add_all(stat_parts, (tie,))
+        stat_parts = [stats] + [shifted(stats, stage, k) for k in range(1, stage[1])]
         tie = stats
 
     tokens_out_own, out_far, g_mid, d_mix, inner, out_grad, cls_norm, biases, kept1, sent1 = big_call(
@@ -788,41 +857,49 @@
         return big_call(
             functools.partial(attention_back_kernel, sample=sample, samples=local),
             (info, view_count, plain),
-            (qkv, tops, d_mix, inner, hat1),
+            (qkv.reshape(local, 3, width, rows), tops, d_mix, inner, hat1),
             [
-                qkv_spec(place),
+                pl.BlockSpec((1, 3, 128, rows), lambda p, *_: (sample, 0, p, 0)),
                 pl.BlockSpec((1, 8, rows), place),
-                pl.BlockSpec((1, width, rows), place),
+                pl.BlockSpec((1, 128, rows), lambda p, *_: (sample, p, 0)),
                 pl.BlockSpec((1, 8, rows), place),
                 pl.BlockSpec((1, rows, width), place),
             ],
             [
-                sds((1, 3 * width, rows), BF),
-                sds((3 * width, width), BF),
-                sds((8, 3 * width), F32),
+                sds((1, 3, width, rows), BF),
+                sds((3, width, width), BF),
+                sds((pairs, 8, 384), F32),
             ],
-            [qkv_spec(lambda *_: (0, 0, 0)), vmem, vmem],
+            [
+                pl.BlockSpec((1, 3, 128, rows), lambda p, *_: (0, 0, p, 0)),
+                pl.BlockSpec((3, 128, width), lambda p, *_: (0, p, 0)),
+                pl.BlockSpec((1, 8, 384), lambda p, *_: (p, 0, 0)),
+            ],
             [pltpu.VMEM((2, rows, rows), BF)],
             ties,
-            grid=(1,),
+            grid=(pairs,),
             name="attention_back",
         )
 
-    ties = (inner,)
+    ties = (chain1.scatter(0),)
     d_parts, grads, sums = [], [], []
     for sample in range(local):
         d_part, grad, total = attention_back(sample, ties)
-        d_parts.append(d_part)
-        grads.append(grad)
+        d_parts.append(d_part.reshape(1, 3 * width, rows))
+        grads.append(grad.reshape(3 * width, width))
         sums.append(total)
-        if sample <= chain1.rounds:
-            ties = (chain1.scatter(sample, (total,)),)
+        ties = (total,)
+        if sample < chain1.rounds:
+            ties = (chain1.scatter(sample + 1, (total,)),)
         if sample == 0:
-            tokens_out = lax.dynamic_update_slice_in_dim(tokens_out_own, out_came, theirs, 0)
+            tokens_out = insert_rows(info, tokens_out_own, out_came)
             ties = (*ties, tokens_out)
-    for level in range(local, chain1.rounds + 1):
-        ties = (chain1.scatter(level),)
-    gathered = lax.all_gather(chain1.value, ("samp", "blk"), axis=0, tiled=True)
+        if sample + 1 == chain1.rounds:
+            gathered = lax.all_gather(chain1.value, ("samp", "blk"), axis=0, tiled=True)
+    if chain1.rounds > local:
+        for level in range(local + 1, chain1.rounds + 1):
+            ties = (chain1.scatter(level),)
+        gathered = lax.all_gather(chain1.value, ("samp", "blk"), axis=0, tiled=True)
 
     chain2 = Chain(layout, info, EXTRA)
     kept2, sent2 = small_call(
@@ -854,15 +931,15 @@
         (tie,),
         name="tokens_back",
     )
-    grad_came = swap_cores(grad_far)
-    ties = (grad_far,)
     for level in range(1, chain2.rounds + 1):
-        chain2.scatter(level, ties)
-        ties = ()
+        chain2.scatter(level, (), (grad_far,) if level == 1 else ())
+        if level == 1:
+            grad_came = swap_cores(chain2.through[0])
+    ties = ()
     for level in reversed(range(chain2.rounds)):
         chain2.gather(level)
         if level == chain2.rounds - 1:
-            grad_tokens = lax.dynamic_update_slice_in_dim(grad_own, grad_came, theirs, 0)
+            grad_tokens = insert_rows(info, grad_own, grad_came)
             ties = (grad_tokens,)
         chain2.collect(ties)
         ties = ()

time: 300 us -> 311 us (1.037)
  starting transfers between devices: 42.6 us -> 51.4 us
  Pallas kernels: 188 us -> 193 us
    pallas_call x0 -> x2, Pallas kernels: none -> 59.5 us  [insert_rows(): pl.pallas_call(body, in_specs=[pl.BlockSpec(memory_space=pltpu.SMEM), any...]
    pallas_call x7, Pallas kernels: 172 us -> 117 us  [big_call(): pl.pallas_call(body, grid_spec=pltpu.PrefetchScalarGridSpec(num_scalar_pr...]
    ppermute x8, starting transfers between devices: 1.49 us -> 6.4 us  [swap_cores(): return lax.ppermute(value, 'blk', [(0, 1), (1, 0)])]
    ppermute x24, waiting for transfers between devices: 22 us -> 17.7 us  [shifted(): return lax.ppermute(value, axis, pairs)]
    ppermute x24, starting transfers between devices: 41 us -> 45 us  [shifted(): return lax.ppermute(value, axis, pairs)]
    unnamed x103 -> x114, local copies, waits for them, and re-layouts: 18.2 us -> 18.6 us
  transfers between devices with their start and end apart: 33 -> 33, of which waited for: 16 -> 12; matrix products, arithmetic and copies ran while one was open for 4% -> 2% of each run, Pallas kernels for 47% -> 48%
where the time goes in v3:
time: 311 us; the launch traced here: 309 us
  Pallas kernels  193 us (62%)
  starting transfers between devices  51.4 us (17%)
  local copies, waits for them, and re-layouts  26.4 us (8%)
  waiting for transfers between devices  23.2 us (7%)
  between operations  15 us (5%)
    pallas_call x7, Pallas kernels, big_call(): pl.pallas_call(body, grid_spec=pltpu.PrefetchScalarGridSpec(num_scalar_pr...  117 us
    pallas_call x2, Pallas kernels, insert_rows(): pl.pallas_call(body, in_specs=[pl.BlockSpec(memory_space=pltpu.SMEM), any...  59.5 us
    ppermute x24, starting transfers between devices, shifted(): return lax.ppermute(value, axis, pairs)  45 us
    unnamed x114, local copies, waits for them, and re-layouts  18.6 us
    ppermute x24, waiting for transfers between devices, shifted(): return lax.ppermute(value, axis, pairs)  17.7 us
    pallas_call x13, Pallas kernels, small_call(): pl.pallas_call(body, in_specs=[pl.BlockSpec(memory_space=pltpu.SMEM), *[v...  16 us
    ppermute x8, starting transfers between devices, swap_cores(): return lax.ppermute(value, 'blk', [(0, 1), (1, 0)])  6.4 us
  transfers between devices with their start and end apart: 33, of which 12 were waited for; matrix products, arithmetic and copies ran while one was open for 2% of the time, Pallas kernels for 48%

profile of v3, /device:TPU:0, one launch (start us, length us, event | category | flops | bytes accessed | tf_op | source)
XLA Modules:
  0.0 309.1 jit_solution(16327744013020900965)
XLA Ops:
  16.0 13.8 %project.1 = (bf16[3,800,384]{2,1,0:T(8,128)(2,1)}, bf16[3,1152,800]{2,1,0:T(8,128)(2,1)}, f32[8,384]{1,0:T(8,128)}, f32[8,384]{1,0:T(8,128)}, bf16[1152,384]{1,0:T(8,128)(2,1)}) custom-call(s32[35]{0:T(128)} %fusion.refs_0_.info_ref, s32[6]{0:T(128)} %refs_1_.11, bf16[6,400,384]{2,1,0:T(8,128)(2,1)} %refs_6_.3, bf16[3,400,384]{2,1,0:T(8,128)(2,1)} %copy-done.37, ...), custom_call_target="tpu_custom_call" | custom-call | tf_op jit(solution)/shard_map/project/pallas_call | solution.py:741
  32.6 5.0 %collective-permute-start.5 = (f32[8,384]{1,0:T(8,128)S(1)}, f32[8,384]{1,0:T(8,128)S(1)}, u32[]{:S(2)}, u32[]{:S(2)}) collective-permute-start(f32[8,384]{1,0:T(8,128)S(1)} %add.24.refs_3_.refs_1_), channel_id=1, source_target_pairs={{0,24},{2,26},{4,28},{6,30},{8,0},{10,2},{12,4},{14,6},{16,8},{18,... | collective-permute-start | bytes 36872 | tf_op jit(solution)/shard_map/ppermute | solution.py:491
  38.6 10.9 %attention.1 = (f32[3,8,800]{2,1,0:T(8,128)}, f32[3,8,800]{2,1,0:T(8,128)}, s32[3]{0:T(128)}, bf16[3,384,800]{2,1,0:T(8,128)(2,1)}) custom-call(s32[35]{0:T(128)} %fusion.refs_0_.info_ref, s32[6]{0:T(128)} %refs_1_.11, bf16[3,1152,800]{2,1,0:T(8,128)(2,1)} %get-tuple-element.72.refs_2_, f32[8,384]{1,0:T(8,128)} %copy-done.31), custom_call_target="tpu_custom_call" | custom-call | tf_op jit(solution)/shard_map/attention/pallas_call | solution.py:741
  51.8 5.1 %collective-permute-start.8 = (f32[8,384]{1,0:T(8,128)S(1)}, f32[8,384]{1,0:T(8,128)S(1)}, u32[]{:S(2)}, u32[]{:S(2)}) collective-permute-start(f32[8,384]{1,0:T(8,128)S(1)} %add.25.refs_9_), channel_id=1, source_target_pairs={{0,6},{2,0},{4,2},{6,4},{8,14},{10,8},{12,10},{14,12},{16,22},{18,... | collective-permute-start | bytes 36872 | tf_op jit(solution)/shard_map/ppermute | solution.py:491
  62.3 40.4 %layer.1 = (bf16[6,400,384]{2,1,0:T(8,128)(2,1)}, bf16[3,400,384]{2,1,0:T(8,128)(2,1)}, bf16[3,800,384]{2,1,0:T(8,128)(2,1)}, bf16[3,384,800]{2,1,0:T(8,128)(2,1...) custom-call(s32[35]{0:T(128)} %fusion.refs_0_.info_ref, ...), custom_call_target="tpu_custom_call" | custom-call | tf_op jit(solution)/shard_map/layer/pallas_call | solution.py:741
  103.3 2.5 collective-permute-done.10.refs_2_
  111.0 2.9 collective-permute-start.13
  113.9 23.0 %attention_back.3 = (bf16[1,3,384,800]{3,2,1,0:T(8,128)(2,1)}, bf16[3,384,384]{2,1,0:T(8,128)(2,1)}, f32[3,8,384]{2,1,0:T(8,128)}) custom-call(s32[35]{0:T(128)} %fusion.refs_0_.info_ref, s32[6]{0:T(128)} %refs_1_.11, s32[3]{0:T(128)} %get-tuple-element.80.refs_2_, bf16[3,3,384,800]{3,2,1,0:T(8,128)(2,1)} %bitcast.12, ...), custom_call_target="tpu_custom_call" | custom-call | tf_op jit(solution)/shard_map/attention_back/pallas_call | solution.py:741
  139.2 5.4 %collective-permute-start.15 = (bf16[96,384]{1,0:T(8,128)(2,1)S(1)}, bf16[96,384]{1,0:T(8,128)(2,1)S(1)}, u32[]{:S(2)}, u32[]{:S(2)}) collective-permute-start(bf16[96,384]{1,0:T(8,128)(2,1)S(1)} %get-tuple-element.96), channel_id=1, source_target_pairs={{0,16},{2,18},{4,20},{6,22},{8,24},{10,26},{12,28},{14,30},{16,0},... | collective-permute-start | bytes 221192 | tf_op jit(solution)/shard_map/ppermute | solution.py:491
  144.6 2.9 collective-permute-start.16
  148.5 29.7 %insert.2.refs_9_ = bf16[6,400,384]{2,1,0:T(8,128)(2,1)} custom-call(s32[35]{0:T(128)} %fusion.refs_0_.info_ref, bf16[3,400,384]{2,1,0:T(8,128)(2,1)} %copy-done.39, bf16[6,400,384]{2,1,0:T(8,128)(2,1)} %get-tuple-element.78.base_ref), custom_call_target="tpu_custom_call", output_to_operand_aliasing={{}: (2, {})} | custom-call | tf_op jit(solution)/shard_map/insert/pallas_call | solution.py:458
  178.2 9.3 %attention_back.4 = (bf16[1,3,384,800]{3,2,1,0:T(8,128)(2,1)}, bf16[3,384,384]{2,1,0:T(8,128)(2,1)}, f32[3,8,384]{2,1,0:T(8,128)}) custom-call(s32[35]{0:T(128)} %fusion.refs_0_.info_ref, s32[6]{0:T(128)} %refs_1_.11, s32[3]{0:T(128)} %get-tuple-element.80.refs_2_, bf16[3,3,384,800]{3,2,1,0:T(8,128)(2,1)} %bitcast.13, ...), custom_call_target="tpu_custom_call" | custom-call | tf_op jit(solution)/shard_map/attention_back/pallas_call | solution.py:741
  189.6 9.3 %attention_back.5 = (bf16[1,3,384,800]{3,2,1,0:T(8,128)(2,1)}, bf16[3,384,384]{2,1,0:T(8,128)(2,1)}, f32[3,8,384]{2,1,0:T(8,128)}) custom-call(s32[35]{0:T(128)} %fusion.refs_0_.info_ref, s32[6]{0:T(128)} %refs_1_.11, s32[3]{0:T(128)} %get-tuple-element.80.refs_2_, bf16[3,3,384,800]{3,2,1,0:T(8,128)(2,1)} %bitcast.14, ...), custom_call_target="tpu_custom_call" | custom-call | tf_op jit(solution)/shard_map/attention_back/pallas_call | solution.py:741
  202.2 4.7 %collective-permute-start.17 = (bf16[784,384]{1,0:T(8,128)(2,1)S(1)}, bf16[784,384]{1,0:T(8,128)(2,1)S(1)}, u32[]{:S(2)}, u32[]{:S(2)}) collective-permute-start(bf16[784,384]{1,0:T(8,128)(2,1)S(1)} %get-tuple-element.104), channel_id=1, source_target_pairs={{0,1},{1,0},{2,3},{3,2},{4,5},{5,4},{6,7},{7,6},{8,9},{9,8},{10,11... | collective-permute-start | bytes 1806344 | tf_op jit(solution)/shard_map/ppermute | solution.py:470
  212.4 4.5 %collective-permute-start.19 = (bf16[208,384]{1,0:T(8,128)(2,1)S(1)}, bf16[208,384]{1,0:T(8,128)(2,1)S(1)}, u32[]{:S(2)}, u32[]{:S(2)}) collective-permute-start(bf16[208,384]{1,0:T(8,128)(2,1)S(1)} %get-tuple-element.107), channel_id=1, source_target_pairs={{0,4},{2,6},{4,0},{6,2},{8,12},{10,14},{12,8},{14,10},{16,20},{18,... | collective-permute-start | bytes 479240 | tf_op jit(solution)/shard_map/ppermute | solution.py:491
  216.8 10.3 %tokens_back.1 = (bf16[6,400,384]{2,1,0:T(8,128)(2,1)}, bf16[3,400,384]{2,1,0:T(8,128)(2,1)}) custom-call(s32[35]{0:T(128)} %fusion.refs_0_.info_ref, bf16[1,1152,800]{2,1,0:T(8,128)(2,1)} %bitcast.15, bf16[1,1152,800]{2,1,0:T(8,128)(2,1)} %bitcast.16, bf16[1,1152,800]{2,1,0:T(8,128)(2,1)} %bitcast.17, bf16[1152,384]{1,0:T(8,128)(2,1)} %get-tuple-element.112.refs_4_.refs_5_, ...), custom_call_target="tpu_custom_call" | custom-call | tf_op jit(solution)/shard_map/tokens_back/pallas_call | solution.py:741
  229.2 7.2 %collective-permute-start.23 = (bf16[64,384]{1,0:T(8,128)(2,1)S(1)}, bf16[64,384]{1,0:T(8,128)(2,1)S(1)}, u32[]{:S(2)}, u32[]{:S(2)}) collective-permute-start(bf16[64,384]{1,0:T(8,128)(2,1)S(1)} %get-tuple-element.119), channel_id=1, source_target_pairs={{0,16},{2,18},{4,20},{6,22},{8,24},{10,26},{12,28},{14,30},{16,0},... | collective-permute-start | bytes 147464 | tf_op jit(solution)/shard_map/ppermute | solution.py:491
  238.5 2.4 collective-permute-done.23.refs_3_
  243.4 2.5 collective-permute-start.27
  247.5 29.8 %insert.3.refs_5_ = bf16[6,400,384]{2,1,0:T(8,128)(2,1)} custom-call(s32[35]{0:T(128)} %fusion.refs_0_.info_ref, bf16[3,400,384]{2,1,0:T(8,128)(2,1)} %copy-done.40, bf16[6,400,384]{2,1,0:T(8,128)(2,1)} %get-tuple-element.116.base_ref), custom_call_target="tpu_custom_call", output_to_operand_aliasing={{}: (2, {})} | custom-call | tf_op jit(solution)/shard_map/insert/pallas_call | solution.py:458
  282.1 3.6 %collective-permute-done.30.refs_4_ = bf16[192,384]{1,0:T(8,128)(2,1)S(1)} collective-permute-done((bf16[192,384]{1,0:T(8,128)(2,1)S(1)}, bf16[192,384]{1,0:T(8,128)(2,1)S(1)}, u32[]{:S(2)}, u32[]{:S(2)}) %collective-permute-start.30) | collective-permute-done | bytes 147488 | tf_op jit(solution)/shard_map/ppermute | solution.py:491
  285.6 3.7 %collective-permute-done.29.refs_3_ = bf16[192,384]{1,0:T(8,128)(2,1)S(1)} collective-permute-done((bf16[192,384]{1,0:T(8,128)(2,1)S(1)}, bf16[192,384]{1,0:T(8,128)(2,1)S(1)}, u32[]{:S(2)}, u32[]{:S(2)}) %collective-permute-start.29) | collective-permute-done | bytes 147488 | tf_op jit(solution)/shard_map/ppermute | solution.py:491
  292.1 3.1 %finish.1 = (f32[384,1152]{1,0:T(8,128)}, f32[384,384]{1,0:T(8,128)}, f32[8,384]{1,0:T(8,128)S(1)}) custom-call(s32[35]{0:T(128)S(1)} %copy-done.25, bf16[768,384]{1,0:T(8,128)(2,1)S(1)} %collect.3.refs_1_.refs_5_, bf16[768,384]{1,0:T(8,128)(2,1)S(1)} %collective-permute-done.31.refs_2_, f32[16,384]{1,0:T(8,128)S(1)} %get-tuple-element.122.refs_3_.refs_2_, ...), custom_call_target="tpu_custom_call" | custom-call | tf_op jit(solution)/shard_map/finish/pallas_call | solution.py:505
  297.4 4.0 %finish_mlp.1 = (f32[1536,384]{1,0:T(8,128)}, f32[384,1536]{1,0:T(8,128)}, f32[8,384]{1,0:T(8,128)S(1)}) custom-call(s32[32]{0:T(128)S(1)} %copy-done.36, bf16[3072,384]{1,0:T(8,128)(2,1)S(1)} %copy-done.3, f32[16,384]{1,0:T(8,128)S(1)} %get-tuple-element.122.refs_3_.refs_2_, f32[16,384]{1,0:T(8,128)S(1)} %copy-done.11, bf16[384,1536]{1,0:T(8,128)(2,1)S(1)} %copy-done, ...), custom_call_target="tpu_custom_call" | custom-call | tf_op jit(solution)/shard_map/finish_mlp/pallas_call | solution.py:505
  (192 shorter events, 58.2 us)
Async XLA Ops:
  7.2 288.6 %all-gather.2.cloned.1.call-start = ((), (), s32[]{:S(2)}) async-start(), calls=%async_computation | async-start | bytes 2433024 | tf_op jit(solution)/shard_map/all_gather | solution.py:898
  11.1 46.6 %collective-permute-start.1 = (bf16[3,400,384]{2,1,0:T(8,128)(2,1)}, bf16[3,400,384]{2,1,0:T(8,128)(2,1)S(1)}, u32[]{:S(2)}, u32[]{:S(2)}) collective-permute-start(bf16[3,400,384]{2,1,0:T(8,128)(2,1)} %constant_dynamic-slice_fusion), channel_id=1, source_target_pairs={{0,1},{1,0},{2,3},{3,2},{4,5},{5,4},{6,7},{7,6},{8,9},{9,8},{10,11... | collective-permute-start | bytes 2764808 | tf_op jit(solution)/shard_map/ppermute | solution.py:470
  32.6 17.0 %collective-permute-start.5 = (f32[8,384]{1,0:T(8,128)S(1)}, f32[8,384]{1,0:T(8,128)S(1)}, u32[]{:S(2)}, u32[]{:S(2)}) collective-permute-start(f32[8,384]{1,0:T(8,128)S(1)} %add.24.refs_3_.refs_1_), channel_id=1, source_target_pairs={{0,24},{2,26},{4,28},{6,30},{8,0},{10,2},{12,4},{14,6},{16,8},{18,... | collective-permute-start | bytes 36872 | tf_op jit(solution)/shard_map/ppermute | solution.py:491
  37.6 12.0 %collective-permute-start.4 = (f32[8,384]{1,0:T(8,128)S(1)}, f32[8,384]{1,0:T(8,128)S(1)}, u32[]{:S(2)}, u32[]{:S(2)}) collective-permute-start(f32[8,384]{1,0:T(8,128)S(1)} %add.24.refs_3_.refs_1_), channel_id=1, source_target_pairs={{0,16},{2,18},{4,20},{6,22},{8,24},{10,26},{12,28},{14,30},{16,0},... | collective-permute-start | bytes 36872 | tf_op jit(solution)/shard_map/ppermute | solution.py:491
  37.6 12.0 %collective-permute-start.3 = (f32[8,384]{1,0:T(8,128)S(1)}, f32[8,384]{1,0:T(8,128)S(1)}, u32[]{:S(2)}, u32[]{:S(2)}) collective-permute-start(f32[8,384]{1,0:T(8,128)S(1)} %add.24.refs_3_.refs_1_), channel_id=1, source_target_pairs={{0,8},{2,10},{4,12},{6,14},{8,16},{10,18},{12,20},{14,22},{16,24},... | collective-permute-start | bytes 36872 | tf_op jit(solution)/shard_map/ppermute | solution.py:491
  51.8 6.5 %collective-permute-start.8 = (f32[8,384]{1,0:T(8,128)S(1)}, f32[8,384]{1,0:T(8,128)S(1)}, u32[]{:S(2)}, u32[]{:S(2)}) collective-permute-start(f32[8,384]{1,0:T(8,128)S(1)} %add.25.refs_9_), channel_id=1, source_target_pairs={{0,6},{2,0},{4,2},{6,4},{8,14},{10,8},{12,10},{14,12},{16,22},{18,... | collective-permute-start | bytes 36872 | tf_op jit(solution)/shard_map/ppermute | solution.py:491
  102.8 44.8 %collective-permute-start.9 = (bf16[3,400,384]{2,1,0:T(8,128)(2,1)}, bf16[3,400,384]{2,1,0:T(8,128)(2,1)S(1)}, u32[]{:S(2)}, u32[]{:S(2)}) collective-permute-start(bf16[3,400,384]{2,1,0:T(8,128)(2,1)} %get-tuple-element.77), channel_id=1, source_target_pairs={{0,1},{1,0},{2,3},{3,2},{4,5},{5,4},{6,7},{7,6},{8,9},{9,8},{10,11... | collective-permute-start | bytes 2764808 | tf_op jit(solution)/shard_map/ppermute | solution.py:470
  109.0 28.0 %collective-permute-start.11 = (bf16[384,384]{1,0:T(8,128)(2,1)S(1)}, bf16[384,384]{1,0:T(8,128)(2,1)S(1)}, u32[]{:S(2)}, u32[]{:S(2)}) collective-permute-start(bf16[384,384]{1,0:T(8,128)(2,1)S(1)} %get-tuple-element.89), channel_id=1, source_target_pairs={{0,2},{2,4},{4,6},{6,0},{8,10},{10,12},{12,14},{14,8},{16,18},{18,... | collective-permute-start | bytes 884744 | tf_op jit(solution)/shard_map/ppermute | solution.py:491
  109.3 27.7 %collective-permute-start.12 = (bf16[384,384]{1,0:T(8,128)(2,1)S(1)}, bf16[384,384]{1,0:T(8,128)(2,1)S(1)}, u32[]{:S(2)}, u32[]{:S(2)}) collective-permute-start(bf16[384,384]{1,0:T(8,128)(2,1)S(1)} %get-tuple-element.90), channel_id=1, source_target_pairs={{0,4},{2,6},{4,0},{6,2},{8,12},{10,14},{12,8},{14,10},{16,20},{18,... | collective-permute-start | bytes 884744 | tf_op jit(solution)/shard_map/ppermute | solution.py:491
  111.0 26.0 %collective-permute-start.13 = (bf16[384,384]{1,0:T(8,128)(2,1)S(1)}, bf16[384,384]{1,0:T(8,128)(2,1)S(1)}, u32[]{:S(2)}, u32[]{:S(2)}) collective-permute-start(bf16[384,384]{1,0:T(8,128)(2,1)S(1)} %get-tuple-element.91), channel_id=1, source_target_pairs={{0,6},{2,0},{4,2},{6,4},{8,14},{10,8},{12,10},{14,12},{16,22},{18,... | collective-permute-start | bytes 884744 | tf_op jit(solution)/shard_map/ppermute | solution.py:491
  139.2 48.2 %collective-permute-start.14 = (bf16[96,384]{1,0:T(8,128)(2,1)S(1)}, bf16[96,384]{1,0:T(8,128)(2,1)S(1)}, u32[]{:S(2)}, u32[]{:S(2)}) collective-permute-start(bf16[96,384]{1,0:T(8,128)(2,1)S(1)} %get-tuple-element.95), channel_id=1, source_target_pairs={{0,8},{2,10},{4,12},{6,14},{8,16},{10,18},{12,20},{14,22},{16,24},... | collective-permute-start | bytes 221192 | tf_op jit(solution)/shard_map/ppermute | solution.py:491
  139.2 48.2 %collective-permute-start.15 = (bf16[96,384]{1,0:T(8,128)(2,1)S(1)}, bf16[96,384]{1,0:T(8,128)(2,1)S(1)}, u32[]{:S(2)}, u32[]{:S(2)}) collective-permute-start(bf16[96,384]{1,0:T(8,128)(2,1)S(1)} %get-tuple-element.96), channel_id=1, source_target_pairs={{0,16},{2,18},{4,20},{6,22},{8,24},{10,26},{12,28},{14,30},{16,0},... | collective-permute-start | bytes 221192 | tf_op jit(solution)/shard_map/ppermute | solution.py:491
  144.6 42.9 %collective-permute-start.16 = (bf16[96,384]{1,0:T(8,128)(2,1)S(1)}, bf16[96,384]{1,0:T(8,128)(2,1)S(1)}, u32[]{:S(2)}, u32[]{:S(2)}) collective-permute-start(bf16[96,384]{1,0:T(8,128)(2,1)S(1)} %get-tuple-element.97), channel_id=1, source_target_pairs={{0,24},{2,26},{4,28},{6,30},{8,0},{10,2},{12,4},{14,6},{16,8},{18,... | collective-permute-start | bytes 221192 | tf_op jit(solution)/shard_map/ppermute | solution.py:491
  210.1 17.0 %collective-permute-start.18 = (bf16[208,384]{1,0:T(8,128)(2,1)S(1)}, bf16[208,384]{1,0:T(8,128)(2,1)S(1)}, u32[]{:S(2)}, u32[]{:S(2)}) collective-permute-start(bf16[208,384]{1,0:T(8,128)(2,1)S(1)} %get-tuple-element.106), channel_id=1, source_target_pairs={{0,2},{2,4},{4,6},{6,0},{8,10},{10,12},{12,14},{14,8},{16,18},{18,... | collective-permute-start | bytes 479240 | tf_op jit(solution)/shard_map/ppermute | solution.py:491
  212.4 14.7 %collective-permute-start.19 = (bf16[208,384]{1,0:T(8,128)(2,1)S(1)}, bf16[208,384]{1,0:T(8,128)(2,1)S(1)}, u32[]{:S(2)}, u32[]{:S(2)}) collective-permute-start(bf16[208,384]{1,0:T(8,128)(2,1)S(1)} %get-tuple-element.107), channel_id=1, source_target_pairs={{0,4},{2,6},{4,0},{6,2},{8,12},{10,14},{12,8},{14,10},{16,20},{18,... | collective-permute-start | bytes 479240 | tf_op jit(solution)/shard_map/ppermute | solution.py:491
  216.8 10.3 %collective-permute-start.20 = (bf16[208,384]{1,0:T(8,128)(2,1)S(1)}, bf16[208,384]{1,0:T(8,128)(2,1)S(1)}, u32[]{:S(2)}, u32[]{:S(2)}) collective-permute-start(bf16[208,384]{1,0:T(8,128)(2,1)S(1)} %get-tuple-element.108), channel_id=1, source_target_pairs={{0,6},{2,0},{4,2},{6,4},{8,14},{10,8},{12,10},{14,12},{16,22},{18,... | collective-permute-start | bytes 479240 | tf_op jit(solution)/shard_map/ppermute | solution.py:491
  229.0 17.5 %collective-permute-start.21 = (bf16[3,400,384]{2,1,0:T(8,128)(2,1)S(1)}, bf16[3,400,384]{2,1,0:T(8,128)(2,1)S(1)}, u32[]{:S(2)}, u32[]{:S(2)}) collective-permute-start(bf16[3,400,384]{2,1,0:T(8,128)(2,1)S(1)} %get-tuple-element.115), channel_id=1, source_target_pairs={{0,1},{1,0},{2,3},{3,2},{4,5},{5,4},{6,7},{7,6},{8,9},{9,8},{10,11... | collective-permute-start | bytes 2764808 | tf_op jit(solution)/shard_map/ppermute | solution.py:470
  229.1 9.4 %collective-permute-start.22 = (bf16[64,384]{1,0:T(8,128)(2,1)S(1)}, bf16[64,384]{1,0:T(8,128)(2,1)S(1)}, u32[]{:S(2)}, u32[]{:S(2)}) collective-permute-start(bf16[64,384]{1,0:T(8,128)(2,1)S(1)} %get-tuple-element.118), channel_id=1, source_target_pairs={{0,8},{2,10},{4,12},{6,14},{8,16},{10,18},{12,20},{14,22},{16,24},... | collective-permute-start | bytes 147464 | tf_op jit(solution)/shard_map/ppermute | solution.py:491
  229.2 11.7 %collective-permute-start.23 = (bf16[64,384]{1,0:T(8,128)(2,1)S(1)}, bf16[64,384]{1,0:T(8,128)(2,1)S(1)}, u32[]{:S(2)}, u32[]{:S(2)}) collective-permute-start(bf16[64,384]{1,0:T(8,128)(2,1)S(1)} %get-tuple-element.119), channel_id=1, source_target_pairs={{0,16},{2,18},{4,20},{6,22},{8,24},{10,26},{12,28},{14,30},{16,0},... | collective-permute-start | bytes 147464 | tf_op jit(solution)/shard_map/ppermute | solution.py:491
  243.4 33.9 %collective-permute-start.27 = (bf16[48,384]{1,0:T(8,128)(2,1)S(1)}, bf16[48,384]{1,0:T(8,128)(2,1)S(1)}, u32[]{:S(2)}, u32[]{:S(2)}) collective-permute-start(bf16[48,384]{1,0:T(8,128)(2,1)S(1)} %get-tuple-element.121.refs_1_), channel_id=1, source_target_pairs={{0,24},{2,26},{4,28},{6,30},{8,0},{10,2},{12,4},{14,6},{16,8},{18,... | collective-permute-start | bytes 110600 | tf_op jit(solution)/shard_map/ppermute | solution.py:491
  245.9 31.4 %collective-permute-start.26 = (bf16[48,384]{1,0:T(8,128)(2,1)S(1)}, bf16[48,384]{1,0:T(8,128)(2,1)S(1)}, u32[]{:S(2)}, u32[]{:S(2)}) collective-permute-start(bf16[48,384]{1,0:T(8,128)(2,1)S(1)} %get-tuple-element.121.refs_1_), channel_id=1, source_target_pairs={{0,16},{2,18},{4,20},{6,22},{8,24},{10,26},{12,28},{14,30},{16,0},... | collective-permute-start | bytes 110600 | tf_op jit(solution)/shard_map/ppermute | solution.py:491
  246.4 30.9 %collective-permute-start.25 = (bf16[48,384]{1,0:T(8,128)(2,1)S(1)}, bf16[48,384]{1,0:T(8,128)(2,1)S(1)}, u32[]{:S(2)}, u32[]{:S(2)}) collective-permute-start(bf16[48,384]{1,0:T(8,128)(2,1)S(1)} %get-tuple-element.121.refs_1_), channel_id=1, source_target_pairs={{0,8},{2,10},{4,12},{6,14},{8,16},{10,18},{12,20},{14,22},{16,24},... | collective-permute-start | bytes 110600 | tf_op jit(solution)/shard_map/ppermute | solution.py:491
  281.4 7.9 %collective-permute-start.29 = (bf16[192,384]{1,0:T(8,128)(2,1)S(1)}, bf16[192,384]{1,0:T(8,128)(2,1)S(1)}, u32[]{:S(2)}, u32[]{:S(2)}) collective-permute-start(bf16[192,384]{1,0:T(8,128)(2,1)S(1)} %collect.2.refs_1_), channel_id=1, source_target_pairs={{0,4},{2,6},{4,0},{6,2},{8,12},{10,14},{12,8},{14,10},{16,20},{18,... | collective-permute-start | bytes 442376 | tf_op jit(solution)/shard_map/ppermute | solution.py:491
  281.4 7.9 %collective-permute-start.28 = (bf16[192,384]{1,0:T(8,128)(2,1)S(1)}, bf16[192,384]{1,0:T(8,128)(2,1)S(1)}, u32[]{:S(2)}, u32[]{:S(2)}) collective-permute-start(bf16[192,384]{1,0:T(8,128)(2,1)S(1)} %collect.2.refs_1_), channel_id=1, source_target_pairs={{0,2},{2,4},{4,6},{6,0},{8,10},{10,12},{12,14},{14,8},{16,18},{18,... | collective-permute-start | bytes 442376 | tf_op jit(solution)/shard_map/ppermute | solution.py:491
  (62 other events, 494.5 us)
Sparse Core Ops, SparseCore 0:
  189.6 63.8 all-gather.1
